TPU v7x, 32 devices: a whole 2x2x4 slice. The times are simulated.
32 devices in a mesh: gx: 2 (over y), gy: 4 (over x, core), gz: 4 (over z).
Axes of the slice: x: 2, y: 2, z: 4, core: 2. Of those that a mesh axis runs over, the one named last changes fastest.
Arguments:
- tensor_blocks: bfloat16 [2, 4, 4, 3, 128, 128, 128], P('gx', 'gy', 'gz'), may hold values from 0 to 3
- fiber_mask: int32 [2, 4, 4, 3, 128, 128], P('gx', 'gy', 'gz'), may hold values 0 or 1
- block_coords: int32 [2, 4, 4, 3, 3], P('gx', 'gy', 'gz'), may hold values from 0 to 7, as said below
- block_counts: int32 [2, 4, 4], P('gx', 'gy', 'gz'), may hold values from 0 to 3, as said below
- factor_a: bfloat16 [2, 512, 256], P('gx', ('gy', 'gz')), may hold values from -0.59765625 to 0.59765625
- factor_b: bfloat16 [4, 1024, 256], P('gy', ('gx', 'gz')), may hold values from -0.59765625 to 0.59765625
- factor_c: bfloat16 [4, 512, 256], P('gz', ('gx', 'gy')), may hold values from -0.59765625 to 0.59765625
Outputs:
- grad_a: float32 [2, 512, 256], P('gx', ('gy', 'gz'))
- grad_b: float32 [4, 1024, 256], P('gy', ('gx', 'gz'))
- grad_c: float32 [4, 512, 256], P('gz', ('gx', 'gy'))
Inputs may be any that keep to these rules, and one draw needn't show every extreme that they name: `block_counts`: some sub-box holds exactly 3 blocks and some holds none, in every draw; slots at and past a sub-box's count hold no block. `block_coords`: the 3 columns of one sub-box name distinct blocks; row 0 is below 4, row 1 below 8, row 2 below 4.
All inputs are finite; a program needn't handle non-finite values. No bound on the sum of `fiber_mask` on one device may be relied on, other than what follows from the above.
Results may differ from a plain program's by a relative error of at most 0.0014.
Values may be sent and summed in bfloat16 or wider, within the bound.
No kernel may reach another device: no remote copies, remote signals or barrier semaphores. Data moves between devices by JAX's collectives and lax.ppermute only.
A program may use at most 128 MiB of HBM per device.

v0:
```python
from functools import partial

import jax
import jax.numpy as jnp
from jax import lax
from jax.sharding import PartitionSpec as P

R = 256
BLK = 128
SLOTS = 3


def block_terms(rows_a, rows_b, rows_c, entries, fibers):
    khatri = (
        rows_b[:, None, :].astype(jnp.float32) * rows_c[None, :, :].astype(jnp.float32)
    ).astype(jnp.bfloat16)
    khatri = khatri.reshape(BLK * BLK, R)
    log_rate = jnp.einsum("ur,kr->uk", rows_a, khatri, preferred_element_type=jnp.float32)
    weight = fibers.astype(jnp.float32).reshape(BLK, BLK, 1)
    misfit = weight * (jnp.exp(log_rate.reshape(BLK, BLK, BLK)) - entries.astype(jnp.float32)) / BLK
    misfit = misfit.astype(jnp.bfloat16).reshape(BLK, BLK * BLK)
    part_a = jnp.dot(misfit, khatri, preferred_element_type=jnp.float32)
    folded = jnp.einsum("uk,ur->kr", misfit, rows_a, preferred_element_type=jnp.float32)
    folded = folded.astype(jnp.bfloat16).reshape(BLK, BLK, R)
    part_b = jnp.einsum("vwr,wr->vr", folded, rows_c, preferred_element_type=jnp.float32)
    part_c = jnp.einsum("vwr,vr->wr", folded, rows_b, preferred_element_type=jnp.float32)
    return (part_a, part_b, part_c)


def add_rows(total, start, part):
    current = lax.dynamic_slice_in_dim(total, start, BLK, 0)
    return lax.dynamic_update_slice_in_dim(total, current + part, start, 0)


def add_block(slot_index, coords, tensor_blocks, fiber_mask, slabs, totals):
    slab_rows_a, slab_rows_b, slab_rows_c = slabs
    grad_a, grad_b, grad_c = totals
    start_a = coords[0, slot_index] * BLK
    start_b = coords[1, slot_index] * BLK
    start_c = coords[2, slot_index] * BLK
    rows_a = lax.dynamic_slice_in_dim(slab_rows_a, start_a, BLK, 0)
    rows_b = lax.dynamic_slice_in_dim(slab_rows_b, start_b, BLK, 0)
    rows_c = lax.dynamic_slice_in_dim(slab_rows_c, start_c, BLK, 0)
    entries = tensor_blocks[0, 0, 0, slot_index]
    fibers = fiber_mask[0, 0, 0, slot_index]
    part_a, part_b, part_c = block_terms(rows_a, rows_b, rows_c, entries, fibers)
    return (
        add_rows(grad_a, start_a, part_a),
        add_rows(grad_b, start_b, part_b),
        add_rows(grad_c, start_c, part_c),
    )


def keep_totals(totals):
    return totals


def per_device(tensor_blocks, fiber_mask, block_coords, block_counts, factor_a, factor_b, factor_c):
    slab_rows_a = lax.all_gather(factor_a, ("gy", "gz"), axis=1, tiled=True)[0]
    inner_b = lax.all_gather(factor_b, "gz", axis=1, tiled=True)
    inner_c = lax.all_gather(factor_c, "gy", axis=1, tiled=True)
    whole_b, whole_c = (
        lax.all_gather(inner_b, "gx", axis=1, tiled=True),
        lax.all_gather(inner_c, "gx", axis=1, tiled=True),
    )
    slab_rows_b = whole_b[0]
    slab_rows_c = whole_c[0]
    slabs = (slab_rows_a, slab_rows_b, slab_rows_c)
    filled = block_counts[0, 0, 0]
    coords = block_coords[0, 0, 0]
    totals = (
        jnp.zeros(slab_rows_a.shape, jnp.float32),
        jnp.zeros(slab_rows_b.shape, jnp.float32),
        jnp.zeros(slab_rows_c.shape, jnp.float32),
    )
    for slot_index in range(SLOTS):
        adder = partial(add_block, slot_index, coords, tensor_blocks, fiber_mask, slabs)
        totals = lax.cond(slot_index < filled, adder, keep_totals, totals)
    terms_a, terms_b, terms_c = totals
    grad_a = lax.psum_scatter(terms_a[None], ("gy", "gz"), scatter_dimension=1, tiled=True)
    first_b, first_c = (
        lax.psum_scatter(terms_b[None], "gx", scatter_dimension=1, tiled=True),
        lax.psum_scatter(terms_c[None], "gx", scatter_dimension=1, tiled=True),
    )
    grad_b = lax.psum_scatter(first_b, "gz", scatter_dimension=1, tiled=True)
    grad_c = lax.psum_scatter(first_c, "gy", scatter_dimension=1, tiled=True)
    return (grad_a, grad_b, grad_c)


def solution(mesh):
    placed = (
        P("gx", "gy", "gz", None, None, None, None),
        P("gx", "gy", "gz", None, None, None),
        P("gx", "gy", "gz", None, None),
        P("gx", "gy", "gz"),
        P("gx", ("gy", "gz"), None),
        P("gy", ("gx", "gz"), None),
        P("gz", ("gx", "gy"), None),
    )
    return jax.shard_map(
        per_device,
        mesh=mesh,
        in_specs=placed,
        out_specs=(
            P("gx", ("gy", "gz"), None),
            P("gy", ("gx", "gz"), None),
            P("gz", ("gx", "gy"), None),
        ),
        check_vma=False,
    )
```

profile of v0, /device:TPU:0, one launch (start us, length us, event | category | flops | bytes accessed | tf_op | source)
XLA Modules:
  0.0 331.1 jit_solution(9786309254293367656)
XLA Ops:
  7.2 15.8 %all_gather.16 = bf16[1,512,256]{2,1,0:T(8,128)(2,1)S(1)} all-gather(bf16[1,128,256]{2,1,0:T(8,128)(2,1)} %param.18), channel_id=1, replica_groups=mesh['gx'=2,'gy'=4,'gz'=4] {'gz'}, dimensions={1}, use_global_device_ids=true | all-gather | bytes 327680 | tf_op jit(solution)/shard_map/all_gather | solution.py:60
  23.0 7.0 %all_gather.17 = bf16[1,1024,256]{2,1,0:T(8,128)(2,1)S(1)} all-gather(bf16[1,512,256]{2,1,0:T(8,128)(2,1)S(1)} %all_gather.16), channel_id=1, replica_groups=mesh['gx'=2,'gy'=4,'gz'=4] {'gx'}, dimensions={1}, use_global_device_ids=true | all-gather | bytes 786432 | tf_op jit(solution)/shard_map/all_gather | solution.py:63
  30.1 5.6 %all_gather.18 = bf16[1,256,256]{2,1,0:T(8,128)(2,1)S(1)} all-gather(bf16[1,64,256]{2,1,0:T(8,128)(2,1)} %param.19), channel_id=1, replica_groups=mesh['gx'=2,'gy'=4,'gz'=4] {'gy'}, dimensions={1}, use_global_device_ids=true | all-gather | bytes 163840 | tf_op jit(solution)/shard_map/all_gather | solution.py:61
  35.7 6.4 %all_gather.19 = bf16[1,512,256]{2,1,0:T(8,128)(2,1)S(1)} all-gather(bf16[1,256,256]{2,1,0:T(8,128)(2,1)S(1)} %all_gather.18), channel_id=1, replica_groups=mesh['gx'=2,'gy'=4,'gz'=4] {'gx'}, dimensions={1}, use_global_device_ids=true | all-gather | bytes 393216 | tf_op jit(solution)/shard_map/all_gather | solution.py:64
  42.1 34.7 %all_gather.15 = bf16[1,512,256]{2,1,0:T(8,128)(2,1)S(1)} all-gather(bf16[1,32,256]{2,1,0:T(8,128)(2,1)} %param.17), channel_id=1, replica_groups=mesh['gx'=2,'gy'=4,'gz'=4] {'gy','gz'}, dimensions={1}, use_global_device_ids=true | all-gather | bytes 278528 | tf_op jit(solution)/shard_map/all_gather | solution.py:59
  76.9 0.7 copy.72
  78.2 36.4 %conditional.3 = (f32[512,256]{1,0:T(8,128)}, f32[1024,256]{1,0:T(8,128)}, f32[512,256]{1,0:T(8,128)}) conditional(s32[]{:T(128)} %bitcast.53, () %tuple.28, (s32[1,1,1,3,128,128]{5,4,3,2,1,0:T(8,128)}, s32[3,3]{1,0:T(4,128)S(1)}, bf16[512,256]{1,0:T(8,128)(2,1)S(1)}, bf16[1024,256]{1,0:T(8,128)(2,1)S(1)}, bf16[512,256]{1,0:T(8,128)(2,1)S(1)}, ...), branch_computations={%region_0.0_spmd, %region_1.0_spmd} | conditional | flops 3277930496 | bytes 64684284 | solution.py:78
  80.8 17.6 %copy.14 = bf16[1,1,1,3,128,128,128]{4,6,5,3,2,1,0:T(8,128)(2,1)} copy(bf16[1,1,1,3,128,128,128]{6,5,4,3,2,1,0:T(8,128)(2,1)} %get-tuple-element.110) | data formatting | bytes 25165824 | tf_op jit(solution)/shard_map
  98.5 4.7 %fusion.4 = bf16[128,128,128]{0,2,1:T(8,128)(2,1)S(1)} fusion(bf16[1,1,1,3,128,128,128]{4,6,5,3,2,1,0:T(8,128)(2,1)} %copy.14, f32[128,128]{0,1:T(8,128)S(1)} %fusion.11, f32[128,256]{1,0:T(8,128)S(1)} %get-tuple-element.138, f32[128,256]{1,0:T(8,128)S(1)} %get-tuple-element.130, bf16[512,256]{1,0:T(8,128)(2,1)S(1)} %get-tuple-element.61, s32[]{:T(128)S(6)} %select_n.12), kind=kOutput, calls=%fused_computation.9 | convolution fusion | flops 1092616192 | bytes 8781828 | tf_op jit(solution)/shard_map/cond/branch_1_fun/ur,kr->uk/dot_general | solution.py:18
  103.1 2.6 multiply_reduce_fusion.1
  105.7 1.1 broadcast_in_dim.12
  106.8 0.7 bitcast_dynamic-update-slice_fusion.1
  107.5 2.8 multiply_reduce_fusion
  110.3 0.8 broadcast.26.clone.1
  111.1 0.6 bitcast_dynamic-update-slice_fusion
  111.7 0.8 broadcast.26.clone
  112.5 2.0 fusion.10
  114.7 0.7 reduce-scatter.8.cloned.1.call-update
  115.4 0.7 reduce-scatter.6.cloned.1.call-update
  116.1 79.4 %reduce-scatter.12.cloned.1.call-done = f32[1,256,256]{2,1,0:T(8,128)} async-done(((f32[1,512,256]{2,1,0:T(8,128)}), f32[1,256,256]{2,1,0:T(8,128)}) %reduce-scatter.12.cloned.1.call-update) | async-done | bytes 262160 | tf_op jit(solution)/shard_map/reduce_scatter | solution.py:83
  195.6 22.6 %reduce-scatter.8.cloned.1.call-done = f32[1,512,256]{2,1,0:T(8,128)} async-done(((f32[1,1024,256]{2,1,0:T(8,128)}), f32[1,512,256]{2,1,0:T(8,128)}) %reduce-scatter.8.cloned.1.call-update) | async-done | bytes 524304 | tf_op jit(solution)/shard_map/reduce_scatter | solution.py:82
  218.2 59.9 %reduce-scatter.6.cloned.1.call-done = f32[1,32,256]{2,1,0:T(8,128)} async-done(((f32[1,512,256]{2,1,0:T(8,128)}), f32[1,32,256]{2,1,0:T(8,128)}) %reduce-scatter.6.cloned.1.call-update) | async-done | bytes 32784 | tf_op jit(solution)/shard_map/reduce_scatter | solution.py:80
  278.1 22.1 %reduce-scatter.14.cloned.1.call-done = f32[1,64,256]{2,1,0:T(8,128)} async-done(((f32[1,256,256]{2,1,0:T(8,128)}), f32[1,64,256]{2,1,0:T(8,128)}) %reduce-scatter.14.cloned.1.call-update) | async-done | bytes 65552 | tf_op jit(solution)/shard_map/reduce_scatter | solution.py:86
  300.2 24.4 %reduce-scatter.10.cloned.1.call-done = f32[1,128,256]{2,1,0:T(8,128)} async-done(((f32[1,512,256]{2,1,0:T(8,128)}), f32[1,128,256]{2,1,0:T(8,128)}) %reduce-scatter.10.cloned.1.call-update) | async-done | bytes 131088 | tf_op jit(solution)/shard_map/reduce_scatter | solution.py:85
  (16 shorter events, 1.0 us)
Async XLA Ops:
  7.2 188.3 %reduce-scatter.12.cloned.1.call-start = ((), (), s32[]{:S(2)}) async-start(), calls=%async_computation.8 | async-start | bytes 786432 | tf_op jit(solution)/shard_map/reduce_scatter | solution.py:83
  80.8 17.6 %copy-start = (s32[1,1,1,3,128,128]{5,4,3,2,1,0:T(8,128)S(1)}, s32[1,1,1,3,128,128]{5,4,3,2,1,0:T(8,128)}, u32[]{:S(2)}) copy-start(s32[1,1,1,3,128,128]{5,4,3,2,1,0:T(8,128)} %get-tuple-element.105) | copy-start | bytes 589828 | tf_op jit(solution)/shard_map/cond
  114.6 103.6 %reduce-scatter.8.cloned.1.call-start = ((), (), s32[]{:S(2)}) async-start(), calls=%async_computation.6 | async-start | bytes 1572864 | tf_op jit(solution)/shard_map/reduce_scatter | solution.py:82
  115.4 162.7 %reduce-scatter.6.cloned.1.call-start = ((), (), s32[]{:S(2)}) async-start(), calls=%async_computation.5 | async-start | bytes 557056 | tf_op jit(solution)/shard_map/reduce_scatter | solution.py:80
  116.1 184.1 %reduce-scatter.14.cloned.1.call-start = ((), (), s32[]{:S(2)}) async-start(), calls=%async_computation.9 | async-start | bytes 327680 | tf_op jit(solution)/shard_map/reduce_scatter | solution.py:86
  195.5 129.1 %reduce-scatter.10.cloned.1.call-start = ((), (), s32[]{:S(2)}) async-start(), calls=%async_computation.7 | async-start | bytes 655360 | tf_op jit(solution)/shard_map/reduce_scatter | solution.py:85
Sparse Core Ops, SparseCore 0:
  114.7 80.7 reduce-scatter.11
  197.8 20.2 reduce-scatter.7
  222.3 55.7 reduce-scatter.5
  281.1 19.0 reduce-scatter.13
  302.9 21.6 reduce-scatter.9
where the time goes:
time: 333 us; the launch traced here: 331 us
  waiting for transfers between devices  210 us (63%)
  blocking collectives  69.6 us (21%)
  local copies, waits for them, and re-layouts  23 us (7%)
  between operations  14.4 us (4%)
  matrix products  9.27 us (3%)
    reduce_scatter x1, waiting for transfers between devices, per_device(): lax.psum_scatter(terms_c[None], 'gx', scatter_dimension=1, tiled=True)  79.4 us
    reduce_scatter x1, waiting for transfers between devices, per_device(): lax.psum_scatter(terms_a[None], ('gy', 'gz'), scatter_dimension=1, tiled=...  59.9 us
    all_gather x1, blocking collectives, per_device(): slab_rows_a = lax.all_gather(factor_a, ('gy', 'gz'), axis=1, tiled=True)[0]  34.7 us
    reduce_scatter x1, waiting for transfers between devices, per_device(): grad_b = lax.psum_scatter(first_b, 'gz', scatter_dimension=1, tiled=True)  24.4 us
    reduce_scatter x1, waiting for transfers between devices, per_device(): lax.psum_scatter(terms_b[None], 'gx', scatter_dimension=1, tiled=True)  22.6 us
    reduce_scatter x1, waiting for transfers between devices, per_device(): grad_c = lax.psum_scatter(first_c, 'gy', scatter_dimension=1, tiled=True)  22.1 us
    another operation x4, local copies, waits for them, and re-layouts  19.3 us
    all_gather x1, blocking collectives, per_device(): inner_b = lax.all_gather(factor_b, 'gz', axis=1, tiled=True)  15.8 us
  transfers between devices with their start and end apart: 5, of which 5 were waited for; matrix products, arithmetic and copies ran while one was open for 0% of the time, Pallas kernels for 0%

commit v1 on v0

v1 whole, which is shorter than its diff:
```python
import functools

import jax
import jax.numpy as jnp
from jax import lax
from jax.experimental import pallas as pl
from jax.experimental.pallas import tpu as pltpu
from jax.sharding import PartitionSpec as P

BLK = 128
STEP = 64
GROUP = 8
PAD = 16
TOP = 32000.0


def pack(parts, target):
    at, powers = 0, []
    for part in parts:
        largest = jnp.maximum(jnp.max(jnp.abs(part), 0, keepdims=True), 1e-33)
        power = jnp.clip(jnp.ceil(jnp.log2(largest * (1.0 / TOP))), -120.0, 120.0)
        values = jnp.round(part * jnp.exp2(-power)).astype(jnp.int32)
        target[at : at + part.shape[0], :] = values.astype(jnp.int16)
        powers.append(power.astype(jnp.int32))
        at += part.shape[0]
    fill = jnp.zeros((PAD - len(powers), powers[0].shape[1]), jnp.int32)
    target[at : at + PAD, :] = jnp.concatenate([*powers, fill], 0).astype(jnp.int16)


def unpack(source, sizes):
    at, parts = 0, []
    powers = source[sum(sizes) : sum(sizes) + PAD, :].astype(jnp.int32).astype(jnp.float32)
    for i, size in enumerate(sizes):
        values = source[at : at + size, :].astype(jnp.int32).astype(jnp.float32)
        parts.append(values * jnp.exp2(powers[i : i + 1, :]))
        at += size
    return parts


def block_kernel(nx, ny, nz, filled, coords, entries, *refs):
    n_bc, n_a = nx, ny
    got_bc, got_a = refs[:n_bc], refs[n_bc : n_bc + n_a]
    refs = refs[n_bc + n_a :]
    own_bc, own_a = refs[:2]
    send_bc, send_a = refs[2 : 2 + nx - 1], refs[1 + nx : nx + ny]
    slab_a, slab_b, slab_c, grad_a, grad_b, grad_c = refs[nx + ny :]
    x, y, z = (lax.axis_index(name) for name in ("gx", "gy", "gz"))
    rank = slab_a.shape[1]
    all_a, all_b, all_c = (s.shape[0] for s in (slab_a, slab_b, slab_c))
    per_a, per_b, per_c = all_a // (ny * nz), all_b // (nx * nz), all_c // (nx * ny)
    slot, step = pl.program_id(0), pl.program_id(1)

    @pl.when((slot == 0) & (step == 0))
    def _():
        grad_a[...] = jnp.zeros_like(grad_a)
        grad_b[...] = jnp.zeros_like(grad_b)
        grad_c[...] = jnp.zeros_like(grad_c)
        for i in range(nx):
            of_x = lax.rem(x + nx - i, nx)
            for j in range(nz):
                at = (of_x * nz + lax.rem(z + nz - j, nz)) * per_b
                slab_b[pl.ds(pl.multiple_of(at, per_b), per_b), :] = got_bc[i][j * per_b : (j + 1) * per_b, :]
            for j in range(ny):
                at = (of_x * ny + lax.rem(y + ny - j, ny)) * per_c
                first = nz * per_b + j * per_c
                slab_c[pl.ds(pl.multiple_of(at, per_c), per_c), :] = got_bc[i][first : first + per_c, :]
        for i in range(ny):
            of_y = lax.rem(y + ny - i, ny)
            for j in range(nz):
                at = (of_y * nz + lax.rem(z + nz - j, nz)) * per_a
                slab_a[pl.ds(pl.multiple_of(at, per_a), per_a), :] = got_a[i][j * per_a : (j + 1) * per_a, :]

    @pl.when(slot < filled[0, 0, 0])
    def _():
        at_a = pl.multiple_of(coords[0, 0, 0, 0, slot] * BLK + step * STEP, STEP)
        at_b = pl.multiple_of(coords[0, 0, 0, 1, slot] * BLK, BLK)
        at_c = pl.multiple_of(coords[0, 0, 0, 2, slot] * BLK, BLK)
        rows_a = slab_a[pl.ds(at_a, STEP), :].astype(jnp.float32)
        rows_b = slab_b[pl.ds(at_b, BLK), :]
        rows_c = slab_c[pl.ds(at_c, BLK), :]
        wide_b = rows_b.astype(jnp.float32)
        sum_b = jnp.zeros((BLK, rank), jnp.float32)
        sum_c = jnp.zeros((BLK, rank), jnp.float32)
        parts = []
        for first in range(0, STEP, GROUP):
            mixed = []
            for u in range(first, first + GROUP):
                row = jnp.broadcast_to(rows_a[u : u + 1, :], (16, rank)).astype(jnp.bfloat16)
                mixed.append((rows_b.reshape(BLK // 16, 16, rank) * row[None]).reshape(BLK, rank))
            mixed = jnp.concatenate(mixed, 0)
            rate = lax.dot_general(mixed, rows_c, (((1,), (1,)), ((), ())), preferred_element_type=jnp.float32)
            seen = entries[0, first : first + GROUP].reshape(GROUP * BLK, BLK).astype(jnp.float32)
            error = jnp.where(seen < 0, 0.0, jnp.exp(rate) - seen).astype(jnp.bfloat16)
            spread = jnp.dot(error, rows_c, preferred_element_type=jnp.float32)
            for i in range(GROUP):
                mine = spread[i * BLK : (i + 1) * BLK]
                sum_b = sum_b + mine * rows_a[first + i : first + i + 1, :]
                parts.append(jnp.sum(mine * wide_b, 0, keepdims=True))
            sum_c = sum_c + lax.dot_general(
                error, mixed, (((0,), (0,)), ((), ())), preferred_element_type=jnp.float32
            )
        grad_a[pl.ds(at_a, STEP), :] += jnp.concatenate(parts, 0)
        grad_b[pl.ds(at_b, BLK), :] += sum_b
        grad_c[pl.ds(at_c, BLK), :] += sum_c

    @pl.when((slot == pl.num_programs(0) - 1) & (step == pl.num_programs(1) - 1))
    def _():
        some_b, some_c, some_a = all_b // nx, all_c // nx, all_a // ny
        for i in range(nx):
            to_x = lax.rem(x + i, nx)
            part_b = grad_b[pl.ds(pl.multiple_of(to_x * some_b, some_b), some_b), :]
            part_c = grad_c[pl.ds(pl.multiple_of(to_x * some_c, some_c), some_c), :]
            if i == 0:
                own_bc[:some_b, :] = part_b
                own_bc[some_b:, :] = part_c
            else:
                pack((part_b, part_c), send_bc[i - 1])
        for i in range(ny):
            to_y = lax.rem(y + i, ny)
            part_a = grad_a[pl.ds(pl.multiple_of(to_y * some_a, some_a), some_a), :]
            if i == 0:
                own_a[...] = part_a
            else:
                pack((part_a,), send_a[i - 1])


def whole(array):
    zeros = (0,) * len(array.shape)
    return pl.BlockSpec(array.shape, lambda *_: zeros)


def middle_kernel(nx, ny, nz, sizes, *refs):
    some_b, some_c, some_a = sizes
    own_bc, own_a = refs[:2]
    got_bc, got_a = refs[2 : 1 + nx], refs[1 + nx : nx + ny]
    own_ba, own_c = refs[nx + ny : nx + ny + 2]
    send_ba = refs[nx + ny + 2 : nx + ny + 1 + nz]
    send_c = refs[nx + ny + 1 + nz : nx + 2 * ny + nz]
    sum_b, sum_c, sum_a = refs[nx + 2 * ny + nz :]
    y, z = lax.axis_index("gy"), lax.axis_index("gz")
    total_b, total_c, total_a = own_bc[:some_b, :], own_bc[some_b:, :], own_a[...]
    for ref in got_bc:
        part_b, part_c = unpack(ref, (some_b, some_c))
        total_b, total_c = total_b + part_b, total_c + part_c
    for ref in got_a:
        total_a = total_a + unpack(ref, (some_a,))[0]
    sum_b[...], sum_c[...], sum_a[...] = total_b, total_c, total_a
    per_b, per_c, per_a = some_b // nz, some_c // ny, some_a // nz
    for i in range(nz):
        to_z = lax.rem(z + i, nz)
        part_b = sum_b[pl.ds(pl.multiple_of(to_z * per_b, per_b), per_b), :]
        part_a = sum_a[pl.ds(pl.multiple_of(to_z * per_a, per_a), per_a), :]
        if i == 0:
            own_ba[:per_b, :] = part_b
            own_ba[per_b:, :] = part_a
        else:
            pack((part_b, part_a), send_ba[i - 1])
    for i in range(ny):
        to_y = lax.rem(y + i, ny)
        part_c = sum_c[pl.ds(pl.multiple_of(to_y * per_c, per_c), per_c), :]
        if i == 0:
            own_c[...] = part_c
        else:
            pack((part_c,), send_c[i - 1])


def last_kernel(ny, nz, sizes, *refs):
    per_b, per_c, per_a = sizes
    own_ba, own_c = refs[:2]
    got_ba, got_c = refs[2 : 1 + nz], refs[1 + nz : nz + ny]
    grad_a, grad_b, grad_c = refs[nz + ny :]
    total_b, total_a, total_c = own_ba[:per_b, :], own_ba[per_b:, :], own_c[...]
    for ref in got_ba:
        part_b, part_a = unpack(ref, (per_b, per_a))
        total_b, total_a = total_b + part_b, total_a + part_a
    for ref in got_c:
        total_c = total_c + unpack(ref, (per_c,))[0]
    grad_a[0] = total_a * (1.0 / BLK)
    grad_b[0] = total_b * (1.0 / BLK)
    grad_c[0] = total_c * (1.0 / BLK)


def shift(array, axis, size, by):
    return lax.ppermute(array, axis, [(i, (i + by) % size) for i in range(size)])


def around(array, axis, size):
    return [array] + [shift(array, axis, size, by) for by in range(1, size)]


def per_device(nx, ny, nz, tensor_blocks, fiber_mask, block_coords, block_counts, factor_a, factor_b, factor_c):
    per_a, per_b, per_c = (f.shape[1] for f in (factor_a, factor_b, factor_c))
    rank = factor_a.shape[2]
    all_a, all_b, all_c = per_a * ny * nz, per_b * nx * nz, per_c * nx * ny
    some_a, some_b, some_c = per_a * nz, per_b * nz, per_c * ny
    slots = tensor_blocks.shape[3]

    entries = jnp.where(fiber_mask[0, 0, 0][..., None] != 0, tensor_blocks[0, 0, 0], -1)

    along_z = around(jnp.concatenate([factor_b[0], factor_a[0]], 0), "gz", nz)
    along_y = around(factor_c[0], "gy", ny)
    half_bc = jnp.concatenate([p[:per_b] for p in along_z] + along_y, 0)
    some_rows_a = jnp.concatenate([p[per_b:] for p in along_z], 0)
    got_bc = around(half_bc, "gx", nx)
    got_a = around(some_rows_a, "gy", ny)

    def where(slot, step, filled, coords):
        held = filled[0, 0, 0]
        last = jnp.maximum(held - 1, 0)
        return (jnp.minimum(slot, last), jnp.where(slot < held, step, BLK // STEP - 1), 0, 0)

    f32, i16 = jnp.float32, jnp.int16
    outs = [jax.ShapeDtypeStruct((some_b + some_c, rank), f32), jax.ShapeDtypeStruct((some_a, rank), f32)]
    outs += [jax.ShapeDtypeStruct((some_b + some_c + PAD, rank), i16)] * (nx - 1)
    outs += [jax.ShapeDtypeStruct((some_a + PAD, rank), i16)] * (ny - 1)
    results = pl.pallas_call(
        functools.partial(block_kernel, nx, ny, nz),
        grid_spec=pltpu.PrefetchScalarGridSpec(
            num_scalar_prefetch=2,
            grid=(slots, BLK // STEP),
            in_specs=[pl.BlockSpec((1, STEP, BLK, BLK), where), *map(whole, got_bc), *map(whole, got_a)],
            out_specs=[*map(whole, outs)],
            scratch_shapes=[pltpu.VMEM((n, rank), jnp.bfloat16) for n in (all_a, all_b, all_c)]
            + [pltpu.VMEM((n, rank), f32) for n in (all_a, all_b, all_c)],
        ),
        out_shape=outs,
        compiler_params=pltpu.CompilerParams(
            vmem_limit_bytes=40 * 2**20, dimension_semantics=("arbitrary", "arbitrary")
        ),
        name="blocks",
    )(block_counts, block_coords, entries, *got_bc, *got_a)

    own_bc, own_a = results[:2]
    got_bc = [shift(r, "gx", nx, i + 1) for i, r in enumerate(results[2 : 1 + nx])]
    got_a = [shift(r, "gy", ny, i + 1) for i, r in enumerate(results[1 + nx :])]
    outs = [jax.ShapeDtypeStruct((per_b + per_a, rank), f32), jax.ShapeDtypeStruct((per_c, rank), f32)]
    outs += [jax.ShapeDtypeStruct((per_b + per_a + PAD, rank), i16)] * (nz - 1)
    outs += [jax.ShapeDtypeStruct((per_c + PAD, rank), i16)] * (ny - 1)
    results = pl.pallas_call(
        functools.partial(middle_kernel, nx, ny, nz, (some_b, some_c, some_a)),
        out_shape=outs,
        scratch_shapes=[pltpu.VMEM((n, rank), f32) for n in (some_b, some_c, some_a)],
        compiler_params=pltpu.CompilerParams(vmem_limit_bytes=32 * 2**20),
        name="middle",
    )(own_bc, own_a, *got_bc, *got_a)

    own_ba, own_c = results[:2]
    got_ba = [shift(r, "gz", nz, i + 1) for i, r in enumerate(results[2 : 1 + nz])]
    got_c = [shift(r, "gy", ny, i + 1) for i, r in enumerate(results[1 + nz :])]
    return pl.pallas_call(
        functools.partial(last_kernel, ny, nz, (per_b, per_c, per_a)),
        out_shape=[jax.ShapeDtypeStruct((1, n, rank), f32) for n in (per_a, per_b, per_c)],
        compiler_params=pltpu.CompilerParams(vmem_limit_bytes=32 * 2**20),
        name="last",
    )(own_ba, own_c, *got_ba, *got_c)


def solution(mesh):
    nx, ny, nz = (mesh.shape[name] for name in ("gx", "gy", "gz"))
    placed = (
        P("gx", "gy", "gz", None, None, None, None),
        P("gx", "gy", "gz", None, None, None),
        P("gx", "gy", "gz", None, None),
        P("gx", "gy", "gz"),
        P("gx", ("gy", "gz"), None),
        P("gy", ("gx", "gz"), None),
        P("gz", ("gx", "gy"), None),
    )
    return jax.shard_map(
        functools.partial(per_device, nx, ny, nz),
        mesh=mesh,
        in_specs=placed,
        out_specs=(
            P("gx", ("gy", "gz"), None),
            P("gy", ("gx", "gz"), None),
            P("gz", ("gx", "gy"), None),
        ),
        check_vma=False,
    )
```

time: 333 us -> 78.4 us (0.24)
  waiting for transfers between devices: 210 us -> 16.7 us
  blocking collectives: 69.6 us -> 0 us
  Pallas kernels: 0 us -> 24.5 us
  local copies, waits for them, and re-layouts: 23 us -> 1.66 us
  starting transfers between devices: 0.19 us -> 19.6 us
  between operations: 14.4 us -> 1.46 us
  other arithmetic: 2.82 us -> 14 us
  matrix products: 9.27 us -> 0 us
    reduce_scatter x5 -> x0, waiting for transfers between devices: 208 us -> none  [the longest x1 79.4 us: per_device(): lax.psum_scatter(terms_c[None], 'gx', scatter_dimension=1, tiled=True)]
    all_gather x5 -> x0, blocking collectives: 69.6 us -> none  [the longest x1 34.7 us: per_device(): slab_rows_a = lax.all_gather(factor_a, ('gy', 'gz'), axis=1, tiled=True)[0]]
    pallas_call x0 -> x3, Pallas kernels: none -> 24.5 us  [the longest x1 23.4 us: per_device(): pl.pallas_call(functools.partial(block_kernel, nx, ny, nz), grid_spec=plt...]
    ppermute x0 -> x20, starting transfers between devices: none -> 19.6 us  [shift(): lax.ppermute(array, axis, [(i, (i + by) % size) for i in range(size)])]
    another operation x4 -> x0, local copies, waits for them, and re-layouts: 19.3 us -> none
    ppermute x0 -> x20, waiting for transfers between devices: none -> 16.7 us  [shift(): lax.ppermute(array, axis, [(i, (i + by) % size) for i in range(size)])]
    select_n x0 -> x1, other arithmetic: none -> 11.5 us  [per_device(): jnp.where(fiber_mask[0, 0, 0][..., None] != 0, tensor_blocks[0, 0, 0], -1)]
    dot_general x3 -> x0, matrix products: 9.27 us -> none  [the longest x1 4.66 us: block_terms(): jnp.einsum('ur,kr->uk', rows_a, khatri, preferred_element_type=jnp.float32)]
  transfers between devices with their start and end apart: 5 -> 20, of which waited for: 5 -> 8; matrix products, arithmetic and copies ran while one was open for 0% -> 20% of each run, Pallas kernels for 0% -> 0%
where the time goes in v1:
time: 78.4 us; the launch traced here: 77.9 us
  Pallas kernels  24.5 us (31%)
  starting transfers between devices  19.6 us (25%)
  waiting for transfers between devices  16.7 us (21%)
  other arithmetic  14 us (18%)
  local copies, waits for them, and re-layouts  1.66 us (2%)
  between operations  1.46 us (2%)
    pallas_call x1, Pallas kernels, per_device(): pl.pallas_call(functools.partial(block_kernel, nx, ny, nz), grid_spec=plt...  23.4 us
    ppermute x20, starting transfers between devices, shift(): lax.ppermute(array, axis, [(i, (i + by) % size) for i in range(size)])  19.6 us
    ppermute x20, waiting for transfers between devices, shift(): lax.ppermute(array, axis, [(i, (i + by) % size) for i in range(size)])  16.7 us
    select_n x1, other arithmetic, per_device(): jnp.where(fiber_mask[0, 0, 0][..., None] != 0, tensor_blocks[0, 0, 0], -1)  11.5 us
    unnamed x10, local copies, waits for them, and re-layouts  1.65 us
  transfers between devices with their start and end apart: 20, of which 8 were waited for; matrix products, arithmetic and copies ran while one was open for 20% of the time, Pallas kernels for 0%

profile of v1, /device:TPU:0, one launch (start us, length us, event | category | flops | bytes accessed | tf_op | source)
XLA Modules:
  0.0 77.9 jit_solution(3279319830597209829)
XLA Ops:
  0.6 2.4 %collective-permute-start.5 = (bf16[64,256]{1,0:T(8,128)(2,1)}, bf16[64,256]{1,0:T(8,128)(2,1)S(1)}, u32[]{:S(2)}, u32[]{:S(2)}) collective-permute-start(bf16[64,256]{1,0:T(8,128)(2,1)} %bitcast.12), channel_id=1, source_target_pairs={{0,12},{4,0},{8,4},{12,8},{1,13},{5,1},{9,5},{13,9},{2,14},{6,2},{... | collective-permute-start | bytes 98312 | tf_op jit(solution)/shard_map/ppermute | solution.py:184
  3.7 0.9 %pad_maximum_fusion = bf16[160,256]{1,0:T(8,128)(2,1)S(1)} fusion(bf16[32,256]{1,0:T(8,128)(2,1)} %bitcast.10, bf16[128,256]{1,0:T(8,128)(2,1)} %bitcast.9), kind=kLoop, calls=%fused_computation.2 | loop fusion | flops 163840 | bytes 163840 | tf_op jit(solution)/shard_map/concatenate | solution.py:200
  4.6 3.6 %collective-permute-start.2 = (bf16[160,256]{1,0:T(8,128)(2,1)S(1)}, bf16[160,256]{1,0:T(8,128)(2,1)S(1)}, u32[]{:S(2)}, u32[]{:S(2)}) collective-permute-start(bf16[160,256]{1,0:T(8,128)(2,1)S(1)} %pad_maximum_fusion), channel_id=1, source_target_pairs={{0,3},{1,0},{2,1},{3,2},{4,7},{5,4},{6,5},{7,6},{8,11},{9,8},{10,9... | collective-permute-start | bytes 245768 | tf_op jit(solution)/shard_map/ppermute | solution.py:184
  8.2 1.0 %collective-permute-start = (bf16[160,256]{1,0:T(8,128)(2,1)S(1)}, bf16[160,256]{1,0:T(8,128)(2,1)S(1)}, u32[]{:S(2)}, u32[]{:S(2)}) collective-permute-start(bf16[160,256]{1,0:T(8,128)(2,1)S(1)} %pad_maximum_fusion), channel_id=1, source_target_pairs={{0,1},{1,2},{2,3},{3,0},{4,5},{5,6},{6,7},{7,4},{8,9},{9,10},{10,1... | collective-permute-start | bytes 245768 | tf_op jit(solution)/shard_map/ppermute | solution.py:184
  9.2 1.0 %compare_bitcast_fusion = pred[3,128,128]{2,1,0:T(8,128)(4,1)S(1)} fusion(s32[1,1,1,3,128,128]{5,4,3,2,1,0:T(8,128)} %param.8), kind=kLoop, calls=%fused_computation.1 | loop fusion | flops 49152 | bytes 245760 | tf_op jit(solution)/shard_map/ne | solution.py:198
  10.1 0.8 %constant_dynamic-update-slice_fusion.4 = bf16[768,256]{1,0:T(8,128)(2,1)S(1)} fusion(bf16[1,128,256]{2,1,0:T(8,128)(2,1)} %param.12), kind=kLoop, calls=%fused_computation.11 | loop fusion | bytes 131072
  11.0 5.2 %collective-permute-done.1 = bf16[160,256]{1,0:T(8,128)(2,1)S(1)} collective-permute-done((bf16[160,256]{1,0:T(8,128)(2,1)S(1)}, bf16[160,256]{1,0:T(8,128)(2,1)S(1)}, u32[]{:S(2)}, u32[]{:S(2)}) %collective-permute-start.1) | collective-permute-done | bytes 81952 | tf_op jit(solution)/shard_map/ppermute | solution.py:184
  16.2 0.7 pad_maximum_fusion.1.refs_2_
  16.9 1.5 %collective-permute-start.8 = (bf16[128,256]{1,0:T(8,128)(2,1)S(1)}, bf16[128,256]{1,0:T(8,128)(2,1)S(1)}, u32[]{:S(2)}, u32[]{:S(2)}) collective-permute-start(bf16[128,256]{1,0:T(8,128)(2,1)S(1)} %pad_maximum_fusion.1.refs_2_), channel_id=1, source_target_pairs={{0,8},{4,12},{8,0},{12,4},{1,9},{5,13},{9,1},{13,5},{2,10},{6,14},... | collective-permute-start | bytes 196616 | tf_op jit(solution)/shard_map/ppermute | solution.py:184
  18.4 0.8 constant_dynamic-update-slice_fusion.3
  19.3 1.6 %collective-permute-start.6 = (bf16[768,256]{1,0:T(8,128)(2,1)S(1)}, bf16[768,256]{1,0:T(8,128)(2,1)S(1)}, u32[]{:S(2)}, u32[]{:S(2)}) collective-permute-start(bf16[768,256]{1,0:T(8,128)(2,1)S(1)} %constant_dynamic-update-slice_fusion.refs_0_), channel_id=1, source_target_pairs={{0,16},{16,0},{1,17},{17,1},{2,18},{18,2},{3,19},{19,3},{4,20},{20... | collective-permute-start | bytes 1179656 | tf_op jit(solution)/shard_map/ppermute | solution.py:184
  20.9 11.5 %bitcast_select_fusion.entries = bf16[3,128,128,128]{3,2,1,0:T(8,128)(2,1)} fusion(bf16[1,1,1,3,128,128,128]{6,5,4,3,2,1,0:T(8,128)(2,1)} %param.7, pred[3,128,128]{2,1,0:T(8,128)(4,1)S(1)} %compare_bitcast_fusion), kind=kLoop, calls=%fused_computation | loop fusion | flops 6291456 | bytes 25214976 | tf_op jit(solution)/shard_map/jit(_where)/select_n | solution.py:198
  33.1 23.4 %blocks.1 = (f32[768,256]{1,0:T(8,128)S(1)}, f32[128,256]{1,0:T(8,128)S(1)}, s16[784,256]{1,0:T(8,128)(2,1)S(1)}, s16[144,256]{1,0:T(8,128)(2,1)S(1)}, s16[144,2...) custom-call(s32[1,1,1]{2,1,0:T(1,128)S(6)} %copy.18.filled, s32[1,1,1,3,3]{4,3,2,1,0:T(4,128)S(1)} %copy.10.coords, ...), custom_call_target="tpu_custom_call" | custom-call | tf_op jit(solution)/shard_map/blocks/pallas_call | solution.py:216
  56.6 1.2 %collective-permute-start.12 = (s16[144,256]{1,0:T(8,128)(2,1)S(1)}, s16[144,256]{1,0:T(8,128)(2,1)S(1)}, u32[]{:S(2)}, u32[]{:S(2)}) collective-permute-start(s16[144,256]{1,0:T(8,128)(2,1)S(1)} %get-tuple-element.21), channel_id=1, source_target_pairs={{0,8},{4,12},{8,0},{12,4},{1,9},{5,13},{9,1},{13,5},{2,10},{6,14},... | collective-permute-start | bytes 221192 | tf_op jit(solution)/shard_map/ppermute | solution.py:184
  57.9 1.4 %collective-permute-start.13 = (s16[144,256]{1,0:T(8,128)(2,1)S(1)}, s16[144,256]{1,0:T(8,128)(2,1)S(1)}, u32[]{:S(2)}, u32[]{:S(2)}) collective-permute-start(s16[144,256]{1,0:T(8,128)(2,1)S(1)} %get-tuple-element.22), channel_id=1, source_target_pairs={{0,12},{4,0},{8,4},{12,8},{1,13},{5,1},{9,5},{13,9},{2,14},{6,2},{... | collective-permute-start | bytes 221192 | tf_op jit(solution)/shard_map/ppermute | solution.py:184
  59.3 1.3 %collective-permute-done.11.refs_3_ = s16[144,256]{1,0:T(8,128)(2,1)S(1)} collective-permute-done((s16[144,256]{1,0:T(8,128)(2,1)S(1)}, s16[144,256]{1,0:T(8,128)(2,1)S(1)}, u32[]{:S(2)}, u32[]{:S(2)}) %collective-permute-start.11) | collective-permute-done | bytes 73760 | tf_op jit(solution)/shard_map/ppermute | solution.py:184
  60.6 1.2 %collective-permute-done.12.refs_4_ = s16[144,256]{1,0:T(8,128)(2,1)S(1)} collective-permute-done((s16[144,256]{1,0:T(8,128)(2,1)S(1)}, s16[144,256]{1,0:T(8,128)(2,1)S(1)}, u32[]{:S(2)}, u32[]{:S(2)}) %collective-permute-start.12) | collective-permute-done | bytes 73760 | tf_op jit(solution)/shard_map/ppermute | solution.py:184
  61.8 2.6 %collective-permute-done.10.refs_2_ = s16[784,256]{1,0:T(8,128)(2,1)S(1)} collective-permute-done((s16[784,256]{1,0:T(8,128)(2,1)S(1)}, s16[784,256]{1,0:T(8,128)(2,1)S(1)}, u32[]{:S(2)}, u32[]{:S(2)}) %collective-permute-start.10) | collective-permute-done | bytes 401440 | tf_op jit(solution)/shard_map/ppermute | solution.py:184
  64.9 6.0 %collective-permute-start.15 = (s16[176,256]{1,0:T(8,128)(2,1)S(1)}, s16[176,256]{1,0:T(8,128)(2,1)S(1)}, u32[]{:S(2)}, u32[]{:S(2)}) collective-permute-start(s16[176,256]{1,0:T(8,128)(2,1)S(1)} %get-tuple-element.26), channel_id=1, source_target_pairs={{0,2},{1,3},{2,0},{3,1},{4,6},{5,7},{6,4},{7,5},{8,10},{9,11},{10,... | collective-permute-start | bytes 270344 | tf_op jit(solution)/shard_map/ppermute | solution.py:184
  70.8 3.4 %collective-permute-done.17.refs_5_ = s16[80,256]{1,0:T(8,128)(2,1)S(1)} collective-permute-done((s16[80,256]{1,0:T(8,128)(2,1)S(1)}, s16[80,256]{1,0:T(8,128)(2,1)S(1)}, u32[]{:S(2)}, u32[]{:S(2)}) %collective-permute-start.17) | collective-permute-done | bytes 40992 | tf_op jit(solution)/shard_map/ppermute | solution.py:184
  74.3 0.9 %collective-permute-done.18.refs_6_ = s16[80,256]{1,0:T(8,128)(2,1)S(1)} collective-permute-done((s16[80,256]{1,0:T(8,128)(2,1)S(1)}, s16[80,256]{1,0:T(8,128)(2,1)S(1)}, u32[]{:S(2)}, u32[]{:S(2)}) %collective-permute-start.18) | collective-permute-done | bytes 40992 | tf_op jit(solution)/shard_map/ppermute | solution.py:184
  75.1 0.8 %collective-permute-done.19.refs_7_ = s16[80,256]{1,0:T(8,128)(2,1)S(1)} collective-permute-done((s16[80,256]{1,0:T(8,128)(2,1)S(1)}, s16[80,256]{1,0:T(8,128)(2,1)S(1)}, u32[]{:S(2)}, u32[]{:S(2)}) %collective-permute-start.19) | collective-permute-done | bytes 40992 | tf_op jit(solution)/shard_map/ppermute | solution.py:184
  75.9 1.2 %collective-permute-done.15.refs_3_ = s16[176,256]{1,0:T(8,128)(2,1)S(1)} collective-permute-done((s16[176,256]{1,0:T(8,128)(2,1)S(1)}, s16[176,256]{1,0:T(8,128)(2,1)S(1)}, u32[]{:S(2)}, u32[]{:S(2)}) %collective-permute-start.15) | collective-permute-done | bytes 90144 | tf_op jit(solution)/shard_map/ppermute | solution.py:184
  77.2 0.7 last.1
  (37 shorter events, 1.4 us)
Async XLA Ops:
  0.6 18.6 %collective-permute-start.5 = (bf16[64,256]{1,0:T(8,128)(2,1)}, bf16[64,256]{1,0:T(8,128)(2,1)S(1)}, u32[]{:S(2)}, u32[]{:S(2)}) collective-permute-start(bf16[64,256]{1,0:T(8,128)(2,1)} %bitcast.12), channel_id=1, source_target_pairs={{0,12},{4,0},{8,4},{12,8},{1,13},{5,1},{9,5},{13,9},{2,14},{6,2},{... | collective-permute-start | bytes 98312 | tf_op jit(solution)/shard_map/ppermute | solution.py:184
  3.1 16.2 %collective-permute-start.4 = (bf16[64,256]{1,0:T(8,128)(2,1)}, bf16[64,256]{1,0:T(8,128)(2,1)S(1)}, u32[]{:S(2)}, u32[]{:S(2)}) collective-permute-start(bf16[64,256]{1,0:T(8,128)(2,1)} %bitcast.13), channel_id=1, source_target_pairs={{0,8},{4,12},{8,0},{12,4},{1,9},{5,13},{9,1},{13,5},{2,10},{6,14},... | collective-permute-start | bytes 98312 | tf_op jit(solution)/shard_map/ppermute | solution.py:184
  4.6 6.5 %collective-permute-start.2 = (bf16[160,256]{1,0:T(8,128)(2,1)S(1)}, bf16[160,256]{1,0:T(8,128)(2,1)S(1)}, u32[]{:S(2)}, u32[]{:S(2)}) collective-permute-start(bf16[160,256]{1,0:T(8,128)(2,1)S(1)} %pad_maximum_fusion), channel_id=1, source_target_pairs={{0,3},{1,0},{2,1},{3,2},{4,7},{5,4},{6,5},{7,6},{8,11},{9,8},{10,9... | collective-permute-start | bytes 245768 | tf_op jit(solution)/shard_map/ppermute | solution.py:184
  8.2 8.0 %collective-permute-start.1 = (bf16[160,256]{1,0:T(8,128)(2,1)S(1)}, bf16[160,256]{1,0:T(8,128)(2,1)S(1)}, u32[]{:S(2)}, u32[]{:S(2)}) collective-permute-start(bf16[160,256]{1,0:T(8,128)(2,1)S(1)} %pad_maximum_fusion), channel_id=1, source_target_pairs={{0,2},{1,3},{2,0},{3,1},{4,6},{5,7},{6,4},{7,5},{8,10},{9,11},{10,... | collective-permute-start | bytes 245768 | tf_op jit(solution)/shard_map/ppermute | solution.py:184
  8.2 8.0 %collective-permute-start = (bf16[160,256]{1,0:T(8,128)(2,1)S(1)}, bf16[160,256]{1,0:T(8,128)(2,1)S(1)}, u32[]{:S(2)}, u32[]{:S(2)}) collective-permute-start(bf16[160,256]{1,0:T(8,128)(2,1)S(1)} %pad_maximum_fusion), channel_id=1, source_target_pairs={{0,1},{1,2},{2,3},{3,0},{4,5},{5,6},{6,7},{7,4},{8,9},{9,10},{10,1... | collective-permute-start | bytes 245768 | tf_op jit(solution)/shard_map/ppermute | solution.py:184
  11.0 8.2 %collective-permute-start.3 = (bf16[64,256]{1,0:T(8,128)(2,1)}, bf16[64,256]{1,0:T(8,128)(2,1)S(1)}, u32[]{:S(2)}, u32[]{:S(2)}) collective-permute-start(bf16[64,256]{1,0:T(8,128)(2,1)} %bitcast.14), channel_id=1, source_target_pairs={{0,4},{4,8},{8,12},{12,0},{1,5},{5,9},{9,13},{13,1},{2,6},{6,10},{... | collective-permute-start | bytes 98312 | tf_op jit(solution)/shard_map/ppermute | solution.py:184
  16.9 16.1 %collective-permute-start.9 = (bf16[128,256]{1,0:T(8,128)(2,1)S(1)}, bf16[128,256]{1,0:T(8,128)(2,1)S(1)}, u32[]{:S(2)}, u32[]{:S(2)}) collective-permute-start(bf16[128,256]{1,0:T(8,128)(2,1)S(1)} %pad_maximum_fusion.1.refs_2_), channel_id=1, source_target_pairs={{0,12},{4,0},{8,4},{12,8},{1,13},{5,1},{9,5},{13,9},{2,14},{6,2},{... | collective-permute-start | bytes 196616 | tf_op jit(solution)/shard_map/ppermute | solution.py:184
  16.9 16.1 %collective-permute-start.8 = (bf16[128,256]{1,0:T(8,128)(2,1)S(1)}, bf16[128,256]{1,0:T(8,128)(2,1)S(1)}, u32[]{:S(2)}, u32[]{:S(2)}) collective-permute-start(bf16[128,256]{1,0:T(8,128)(2,1)S(1)} %pad_maximum_fusion.1.refs_2_), channel_id=1, source_target_pairs={{0,8},{4,12},{8,0},{12,4},{1,9},{5,13},{9,1},{13,5},{2,10},{6,14},... | collective-permute-start | bytes 196616 | tf_op jit(solution)/shard_map/ppermute | solution.py:184
  19.2 13.8 %collective-permute-start.7 = (bf16[128,256]{1,0:T(8,128)(2,1)S(1)}, bf16[128,256]{1,0:T(8,128)(2,1)S(1)}, u32[]{:S(2)}, u32[]{:S(2)}) collective-permute-start(bf16[128,256]{1,0:T(8,128)(2,1)S(1)} %pad_maximum_fusion.1.refs_2_), channel_id=1, source_target_pairs={{0,4},{4,8},{8,12},{12,0},{1,5},{5,9},{9,13},{13,1},{2,6},{6,10},{... | collective-permute-start | bytes 196616 | tf_op jit(solution)/shard_map/ppermute | solution.py:184
  19.3 13.7 %copy-start = (s32[1,1,1,3,3]{4,2,3,1,0:T(1,128)S(1)}, s32[1,1,1,3,3]{4,2,3,1,0:T(1,128)}, u32[]{:S(2)}) copy-start(s32[1,1,1,3,3]{4,2,3,1,0:T(1,128)} %param.9) | copy-start | bytes 112
  19.3 13.8 %collective-permute-start.6 = (bf16[768,256]{1,0:T(8,128)(2,1)S(1)}, bf16[768,256]{1,0:T(8,128)(2,1)S(1)}, u32[]{:S(2)}, u32[]{:S(2)}) collective-permute-start(bf16[768,256]{1,0:T(8,128)(2,1)S(1)} %constant_dynamic-update-slice_fusion.refs_0_), channel_id=1, source_target_pairs={{0,16},{16,0},{1,17},{17,1},{2,18},{18,2},{3,19},{19,3},{4,20},{20... | collective-permute-start | bytes 1179656 | tf_op jit(solution)/shard_map/ppermute | solution.py:184
  56.5 7.9 %collective-permute-start.10 = (s16[784,256]{1,0:T(8,128)(2,1)S(1)}, s16[784,256]{1,0:T(8,128)(2,1)S(1)}, u32[]{:S(2)}, u32[]{:S(2)}) collective-permute-start(s16[784,256]{1,0:T(8,128)(2,1)S(1)} %get-tuple-element.19), channel_id=1, source_target_pairs={{0,16},{16,0},{1,17},{17,1},{2,18},{18,2},{3,19},{19,3},{4,20},{20... | collective-permute-start | bytes 1204232 | tf_op jit(solution)/shard_map/ppermute | solution.py:184
  56.6 4.0 %collective-permute-start.11 = (s16[144,256]{1,0:T(8,128)(2,1)S(1)}, s16[144,256]{1,0:T(8,128)(2,1)S(1)}, u32[]{:S(2)}, u32[]{:S(2)}) collective-permute-start(s16[144,256]{1,0:T(8,128)(2,1)S(1)} %get-tuple-element.20), channel_id=1, source_target_pairs={{0,4},{4,8},{8,12},{12,0},{1,5},{5,9},{9,13},{13,1},{2,6},{6,10},{... | collective-permute-start | bytes 221192 | tf_op jit(solution)/shard_map/ppermute | solution.py:184
  56.6 5.2 %collective-permute-start.12 = (s16[144,256]{1,0:T(8,128)(2,1)S(1)}, s16[144,256]{1,0:T(8,128)(2,1)S(1)}, u32[]{:S(2)}, u32[]{:S(2)}) collective-permute-start(s16[144,256]{1,0:T(8,128)(2,1)S(1)} %get-tuple-element.21), channel_id=1, source_target_pairs={{0,8},{4,12},{8,0},{12,4},{1,9},{5,13},{9,1},{13,5},{2,10},{6,14},... | collective-permute-start | bytes 221192 | tf_op jit(solution)/shard_map/ppermute | solution.py:184
  57.9 3.9 %collective-permute-start.13 = (s16[144,256]{1,0:T(8,128)(2,1)S(1)}, s16[144,256]{1,0:T(8,128)(2,1)S(1)}, u32[]{:S(2)}, u32[]{:S(2)}) collective-permute-start(s16[144,256]{1,0:T(8,128)(2,1)S(1)} %get-tuple-element.22), channel_id=1, source_target_pairs={{0,12},{4,0},{8,4},{12,8},{1,13},{5,1},{9,5},{13,9},{2,14},{6,2},{... | collective-permute-start | bytes 221192 | tf_op jit(solution)/shard_map/ppermute | solution.py:184
  64.8 11.1 %collective-permute-start.14 = (s16[176,256]{1,0:T(8,128)(2,1)S(1)}, s16[176,256]{1,0:T(8,128)(2,1)S(1)}, u32[]{:S(2)}, u32[]{:S(2)}) collective-permute-start(s16[176,256]{1,0:T(8,128)(2,1)S(1)} %get-tuple-element.25), channel_id=1, source_target_pairs={{0,1},{1,2},{2,3},{3,0},{4,5},{5,6},{6,7},{7,4},{8,9},{9,10},{10,1... | collective-permute-start | bytes 270344 | tf_op jit(solution)/shard_map/ppermute | solution.py:184
  64.9 12.3 %collective-permute-start.15 = (s16[176,256]{1,0:T(8,128)(2,1)S(1)}, s16[176,256]{1,0:T(8,128)(2,1)S(1)}, u32[]{:S(2)}, u32[]{:S(2)}) collective-permute-start(s16[176,256]{1,0:T(8,128)(2,1)S(1)} %get-tuple-element.26), channel_id=1, source_target_pairs={{0,2},{1,3},{2,0},{3,1},{4,6},{5,7},{6,4},{7,5},{8,10},{9,11},{10,... | collective-permute-start | bytes 270344 | tf_op jit(solution)/shard_map/ppermute | solution.py:184
  70.8 6.4 %collective-permute-start.16 = (s16[176,256]{1,0:T(8,128)(2,1)S(1)}, s16[176,256]{1,0:T(8,128)(2,1)S(1)}, u32[]{:S(2)}, u32[]{:S(2)}) collective-permute-start(s16[176,256]{1,0:T(8,128)(2,1)S(1)} %get-tuple-element.27), channel_id=1, source_target_pairs={{0,3},{1,0},{2,1},{3,2},{4,7},{5,4},{6,5},{7,6},{8,11},{9,8},{10,9... | collective-permute-start | bytes 270344 | tf_op jit(solution)/shard_map/ppermute | solution.py:184
  70.8 3.4 %collective-permute-start.17 = (s16[80,256]{1,0:T(8,128)(2,1)S(1)}, s16[80,256]{1,0:T(8,128)(2,1)S(1)}, u32[]{:S(2)}, u32[]{:S(2)}) collective-permute-start(s16[80,256]{1,0:T(8,128)(2,1)S(1)} %get-tuple-element.28), channel_id=1, source_target_pairs={{0,4},{4,8},{8,12},{12,0},{1,5},{5,9},{9,13},{13,1},{2,6},{6,10},{... | collective-permute-start | bytes 122888 | tf_op jit(solution)/shard_map/ppermute | solution.py:184
  70.8 4.3 %collective-permute-start.18 = (s16[80,256]{1,0:T(8,128)(2,1)S(1)}, s16[80,256]{1,0:T(8,128)(2,1)S(1)}, u32[]{:S(2)}, u32[]{:S(2)}) collective-permute-start(s16[80,256]{1,0:T(8,128)(2,1)S(1)} %get-tuple-element.29), channel_id=1, source_target_pairs={{0,8},{4,12},{8,0},{12,4},{1,9},{5,13},{9,1},{13,5},{2,10},{6,14},... | collective-permute-start | bytes 122888 | tf_op jit(solution)/shard_map/ppermute | solution.py:184
  74.3 1.7 %collective-permute-start.19 = (s16[80,256]{1,0:T(8,128)(2,1)S(1)}, s16[80,256]{1,0:T(8,128)(2,1)S(1)}, u32[]{:S(2)}, u32[]{:S(2)}) collective-permute-start(s16[80,256]{1,0:T(8,128)(2,1)S(1)} %get-tuple-element.30), channel_id=1, source_target_pairs={{0,12},{4,0},{8,4},{12,8},{1,13},{5,1},{9,5},{13,9},{2,14},{6,2},{... | collective-permute-start | bytes 122888 | tf_op jit(solution)/shard_map/ppermute | solution.py:184

commit v2 on v1

v2 whole, which is shorter than its diff:
```python
import functools

import jax
import jax.numpy as jnp
from jax import lax
from jax.experimental import pallas as pl
from jax.experimental.pallas import tpu as pltpu
from jax.sharding import PartitionSpec as P

BLK = 128
STEP = 64
GROUP = 8
PAD = 16
TOP = 32000.0


def pack(parts, target):
    at, powers = 0, []
    for part in parts:
        largest = jnp.maximum(jnp.max(jnp.abs(part), 0, keepdims=True), 1e-33)
        power = jnp.clip(jnp.ceil(jnp.log2(largest * (1.0 / TOP))), -120.0, 120.0)
        values = jnp.round(part * jnp.exp2(-power)).astype(jnp.int32)
        target[at : at + part.shape[0], :] = values.astype(jnp.int16)
        powers.append(power.astype(jnp.int32))
        at += part.shape[0]
    fill = jnp.zeros((PAD - len(powers), powers[0].shape[1]), jnp.int32)
    target[at : at + PAD, :] = jnp.concatenate([*powers, fill], 0).astype(jnp.int16)


def unpack(source, sizes):
    at, parts = 0, []
    powers = source[sum(sizes) : sum(sizes) + PAD, :].astype(jnp.int32).astype(jnp.float32)
    for i, size in enumerate(sizes):
        values = source[at : at + size, :].astype(jnp.int32).astype(jnp.float32)
        parts.append(values * jnp.exp2(powers[i : i + 1, :]))
        at += size
    return parts


def block_kernel(nx, ny, nz, filled, coords, entries, fibers, *refs):
    got_b, got_ac = refs[:nx], refs[nx : nx + ny]
    refs = refs[nx + ny :]
    own_b, own_ac = refs[:2]
    send_b, send_ac = refs[2 : 1 + nx], refs[1 + nx : nx + ny]
    slab_a, slab_b, slab_c, grad_a, grad_b, grad_c = refs[nx + ny :]
    x, y, z = (lax.axis_index(name) for name in ("gx", "gy", "gz"))
    rank = slab_a.shape[1]
    all_a, all_b, all_c = (s.shape[0] for s in (slab_a, slab_b, slab_c))
    per_a, per_b, per_c = all_a // (ny * nz), all_b // (nx * nz), all_c // (nx * ny)
    slot, step = pl.program_id(0), pl.program_id(1)

    @pl.when((slot == 0) & (step == 0))
    def _():
        grad_a[...] = jnp.zeros_like(grad_a)
        grad_b[...] = jnp.zeros_like(grad_b)
        grad_c[...] = jnp.zeros_like(grad_c)
        for j in range(nz):
            of_z = lax.rem(z + nz - j, nz)
            for i in range(nx):
                at = (lax.rem(x + nx - i, nx) * nz + of_z) * per_b
                slab_b[pl.ds(pl.multiple_of(at, per_b), per_b), :] = got_b[i][j * per_b : (j + 1) * per_b, :]
            for i in range(ny):
                at = (lax.rem(y + ny - i, ny) * nz + of_z) * per_a
                slab_a[pl.ds(pl.multiple_of(at, per_a), per_a), :] = got_ac[i][j * per_a : (j + 1) * per_a, :]
        for j in range(nx):
            of_x = lax.rem(x + nx - j, nx)
            for i in range(ny):
                at = (of_x * ny + lax.rem(y + ny - i, ny)) * per_c
                first = nz * per_a + j * per_c
                slab_c[pl.ds(pl.multiple_of(at, per_c), per_c), :] = got_ac[i][first : first + per_c, :]

    @pl.when(slot < filled[0, 0, 0])
    def _():
        at_a = pl.multiple_of(coords[0, 0, 0, 0, slot] * BLK + step * STEP, STEP)
        at_b = pl.multiple_of(coords[0, 0, 0, 1, slot] * BLK, BLK)
        at_c = pl.multiple_of(coords[0, 0, 0, 2, slot] * BLK, BLK)
        rows_a = slab_a[pl.ds(at_a, STEP), :].astype(jnp.float32)
        rows_b = slab_b[pl.ds(at_b, BLK), :]
        rows_c = slab_c[pl.ds(at_c, BLK), :]
        wide_b = rows_b.astype(jnp.float32)
        sum_b = jnp.zeros((BLK, rank), jnp.float32)
        sum_c = jnp.zeros((BLK, rank), jnp.float32)
        parts = []
        weight = jnp.transpose(fibers[0, 0, 0, 0].astype(jnp.float32)).astype(jnp.bfloat16)
        for first in range(0, STEP, GROUP):
            mixed = []
            for u in range(first, first + GROUP):
                row = jnp.broadcast_to(rows_a[u : u + 1, :], (16, rank)).astype(jnp.bfloat16)
                mixed.append((rows_b.reshape(BLK // 16, 16, rank) * row[None]).reshape(BLK, rank))
            mixed = jnp.concatenate(mixed, 0)
            rate = lax.dot_general(mixed, rows_c, (((1,), (1,)), ((), ())), preferred_element_type=jnp.float32)
            seen = entries[0, 0, 0, 0, first : first + GROUP].reshape(GROUP * BLK, BLK).astype(jnp.float32)
            error = (jnp.exp(rate) - seen).astype(jnp.bfloat16)
            error = [
                error[i * BLK : (i + 1) * BLK] * weight[:, first + i : first + i + 1] for i in range(GROUP)
            ]
            error = jnp.concatenate(error, 0)
            spread = jnp.dot(error, rows_c, preferred_element_type=jnp.float32)
            for i in range(GROUP):
                mine = spread[i * BLK : (i + 1) * BLK]
                sum_b = sum_b + mine * rows_a[first + i : first + i + 1, :]
                parts.append(jnp.sum(mine * wide_b, 0, keepdims=True))
            sum_c = sum_c + lax.dot_general(
                error, mixed, (((0,), (0,)), ((), ())), preferred_element_type=jnp.float32
            )
        grad_a[pl.ds(at_a, STEP), :] += jnp.concatenate(parts, 0)
        grad_b[pl.ds(at_b, BLK), :] += sum_b
        grad_c[pl.ds(at_c, BLK), :] += sum_c

    @pl.when((slot == pl.num_programs(0) - 1) & (step == pl.num_programs(1) - 1))
    def _():
        some_b, some_a = all_b // nx, all_a // ny
        for i in range(nx):
            to_x = lax.rem(x + i, nx)
            part_b = grad_b[pl.ds(pl.multiple_of(to_x * some_b, some_b), some_b), :]
            if i == 0:
                own_b[...] = part_b
            else:
                pack((part_b,), send_b[i - 1])
        for i in range(ny):
            to_y = lax.rem(y + i, ny)
            part_a = grad_a[pl.ds(pl.multiple_of(to_y * some_a, some_a), some_a), :]
            part_c = jnp.concatenate(
                [grad_c[pl.ds(pl.multiple_of((j * ny + to_y) * per_c, per_c), per_c), :] for j in range(nx)], 0
            )
            if i == 0:
                own_ac[:some_a, :] = part_a
                own_ac[some_a:, :] = part_c
            else:
                pack((part_a, part_c), send_ac[i - 1])


def whole(array):
    zeros = (0,) * len(array.shape)
    return pl.BlockSpec(array.shape, lambda *_: zeros)


def middle_kernel(nx, ny, nz, sizes, *refs):
    some_b, some_c, some_a = sizes
    own_b, own_ac = refs[:2]
    got_b, got_ac = refs[2 : 1 + nx], refs[1 + nx : nx + ny]
    own_ba, own_c = refs[nx + ny : nx + ny + 2]
    send_ba = refs[nx + ny + 2 : nx + ny + 1 + nz]
    send_c = refs[nx + ny + 1 + nz : 2 * nx + ny + nz]
    sum_b, sum_c, sum_a = refs[2 * nx + ny + nz :]
    x, z = lax.axis_index("gx"), lax.axis_index("gz")
    total_b, total_a, total_c = own_b[...], own_ac[:some_a, :], own_ac[some_a:, :]
    for ref in got_b:
        total_b = total_b + unpack(ref, (some_b,))[0]
    for ref in got_ac:
        part_a, part_c = unpack(ref, (some_a, some_c))
        total_a, total_c = total_a + part_a, total_c + part_c
    sum_b[...], sum_c[...], sum_a[...] = total_b, total_c, total_a
    per_b, per_c, per_a = some_b // nz, some_c // nx, some_a // nz
    for i in range(nz):
        to_z = lax.rem(z + i, nz)
        part_b = sum_b[pl.ds(pl.multiple_of(to_z * per_b, per_b), per_b), :]
        part_a = sum_a[pl.ds(pl.multiple_of(to_z * per_a, per_a), per_a), :]
        if i == 0:
            own_ba[:per_b, :] = part_b
            own_ba[per_b:, :] = part_a
        else:
            pack((part_b, part_a), send_ba[i - 1])
    for i in range(nx):
        to_x = lax.rem(x + i, nx)
        part_c = sum_c[pl.ds(pl.multiple_of(to_x * per_c, per_c), per_c), :]
        if i == 0:
            own_c[...] = part_c
        else:
            pack((part_c,), send_c[i - 1])


def last_kernel(nx, nz, sizes, *refs):
    per_b, per_c, per_a = sizes
    own_ba, own_c = refs[:2]
    got_ba, got_c = refs[2 : 1 + nz], refs[1 + nz : nz + nx]
    grad_a, grad_b, grad_c = refs[nz + nx :]
    total_b, total_a, total_c = own_ba[:per_b, :], own_ba[per_b:, :], own_c[...]
    for ref in got_ba:
        part_b, part_a = unpack(ref, (per_b, per_a))
        total_b, total_a = total_b + part_b, total_a + part_a
    for ref in got_c:
        total_c = total_c + unpack(ref, (per_c,))[0]
    grad_a[0] = total_a * (1.0 / BLK)
    grad_b[0] = total_b * (1.0 / BLK)
    grad_c[0] = total_c * (1.0 / BLK)


def shift(array, axis, size, by):
    return lax.ppermute(array, axis, [(i, (i + by) % size) for i in range(size)])


def around(array, axis, size):
    return [array] + [shift(array, axis, size, by) for by in range(1, size)]


def per_device(nx, ny, nz, tensor_blocks, fiber_mask, block_coords, block_counts, factor_a, factor_b, factor_c):
    per_a, per_b, per_c = (f.shape[1] for f in (factor_a, factor_b, factor_c))
    rank = factor_a.shape[2]
    all_a, all_b, all_c = per_a * ny * nz, per_b * nx * nz, per_c * nx * ny
    some_a, some_b, some_c = per_a * nz, per_b * nz, per_c * nx
    slots = tensor_blocks.shape[3]

    along_z = around(jnp.concatenate([factor_b[0], factor_a[0]], 0), "gz", nz)
    along_x = around(factor_c[0], "gx", nx)
    got_b = around(jnp.concatenate([p[:per_b] for p in along_z], 0), "gx", nx)
    got_ac = around(jnp.concatenate([p[per_b:] for p in along_z] + along_x, 0), "gy", ny)

    def where(slot, step, filled, coords):
        held = filled[0, 0, 0]
        last = jnp.maximum(held - 1, 0)
        return (0, 0, 0, jnp.minimum(slot, last), jnp.where(slot < held, step, BLK // STEP - 1), 0, 0)

    f32, i16 = jnp.float32, jnp.int16
    outs = [jax.ShapeDtypeStruct((some_b, rank), f32), jax.ShapeDtypeStruct((some_a + some_c, rank), f32)]
    outs += [jax.ShapeDtypeStruct((some_b + PAD, rank), i16)] * (nx - 1)
    outs += [jax.ShapeDtypeStruct((some_a + some_c + PAD, rank), i16)] * (ny - 1)
    results = pl.pallas_call(
        functools.partial(block_kernel, nx, ny, nz),
        grid_spec=pltpu.PrefetchScalarGridSpec(
            num_scalar_prefetch=2,
            grid=(slots, BLK // STEP),
            in_specs=[
                pl.BlockSpec((1, 1, 1, 1, STEP, BLK, BLK), where),
                pl.BlockSpec((1, 1, 1, 1, STEP, BLK), lambda *at: where(*at)[:-1]),
                *map(whole, got_b),
                *map(whole, got_ac),
            ],
            out_specs=[*map(whole, outs)],
            scratch_shapes=[pltpu.VMEM((n, rank), jnp.bfloat16) for n in (all_a, all_b, all_c)]
            + [pltpu.VMEM((n, rank), f32) for n in (all_a, all_b, all_c)],
        ),
        out_shape=outs,
        compiler_params=pltpu.CompilerParams(
            vmem_limit_bytes=40 * 2**20, dimension_semantics=("arbitrary", "arbitrary")
        ),
        name="blocks",
    )(block_counts, block_coords, tensor_blocks, fiber_mask, *got_b, *got_ac)

    own_b, own_ac = results[:2]
    got_b = [shift(r, "gx", nx, i + 1) for i, r in enumerate(results[2 : 1 + nx])]
    got_ac = [shift(r, "gy", ny, i + 1) for i, r in enumerate(results[1 + nx :])]
    outs = [jax.ShapeDtypeStruct((per_b + per_a, rank), f32), jax.ShapeDtypeStruct((per_c, rank), f32)]
    outs += [jax.ShapeDtypeStruct((per_b + per_a + PAD, rank), i16)] * (nz - 1)
    outs += [jax.ShapeDtypeStruct((per_c + PAD, rank), i16)] * (nx - 1)
    results = pl.pallas_call(
        functools.partial(middle_kernel, nx, ny, nz, (some_b, some_c, some_a)),
        out_shape=outs,
        scratch_shapes=[pltpu.VMEM((n, rank), f32) for n in (some_b, some_c, some_a)],
        compiler_params=pltpu.CompilerParams(vmem_limit_bytes=32 * 2**20),
        name="middle",
    )(own_b, own_ac, *got_b, *got_ac)

    own_ba, own_c = results[:2]
    got_ba = [shift(r, "gz", nz, i + 1) for i, r in enumerate(results[2 : 1 + nz])]
    got_c = [shift(r, "gx", nx, i + 1) for i, r in enumerate(results[1 + nz :])]
    return pl.pallas_call(
        functools.partial(last_kernel, nx, nz, (per_b, per_c, per_a)),
        out_shape=[jax.ShapeDtypeStruct((1, n, rank), f32) for n in (per_a, per_b, per_c)],
        compiler_params=pltpu.CompilerParams(vmem_limit_bytes=32 * 2**20),
        name="last",
    )(own_ba, own_c, *got_ba, *got_c)


def solution(mesh):
    nx, ny, nz = (mesh.shape[name] for name in ("gx", "gy", "gz"))
    placed = (
        P("gx", "gy", "gz", None, None, None, None),
        P("gx", "gy", "gz", None, None, None),
        P("gx", "gy", "gz", None, None),
        P("gx", "gy", "gz"),
        P("gx", ("gy", "gz"), None),
        P("gy", ("gx", "gz"), None),
        P("gz", ("gx", "gy"), None),
    )
    return jax.shard_map(
        functools.partial(per_device, nx, ny, nz),
        mesh=mesh,
        in_specs=placed,
        out_specs=(
            P("gx", ("gy", "gz"), None),
            P("gy", ("gx", "gz"), None),
            P("gz", ("gx", "gy"), None),
        ),
        check_vma=False,
    )
```

time: 78.4 us -> 69.1 us (0.88)
  Pallas kernels: 24.5 us -> 10.7 us
  other arithmetic: 14 us -> 1.73 us
  starting transfers between devices: 19.6 us -> 31.3 us
  waiting for transfers between devices: 16.7 us -> 20.7 us
  local copies, waits for them, and re-layouts: 1.66 us -> 3.12 us
    pallas_call x1, Pallas kernels: 23.4 us -> 9.57 us  [per_device(): pl.pallas_call(functools.partial(block_kernel, nx, ny, nz), grid_spec=plt...]
    ppermute x20 -> x16, starting transfers between devices: 19.6 us -> 31.3 us  [shift(): lax.ppermute(array, axis, [(i, (i + by) % size) for i in range(size)])]
    select_n x1 -> x0, other arithmetic: 11.5 us -> none  [per_device(): jnp.where(fiber_mask[0, 0, 0][..., None] != 0, tensor_blocks[0, 0, 0], -1)]
    ppermute x20 -> x16, waiting for transfers between devices: 16.7 us -> 20.7 us  [shift(): lax.ppermute(array, axis, [(i, (i + by) % size) for i in range(size)])]
    unnamed x10 -> x8, local copies, waits for them, and re-layouts: 1.65 us -> 3.1 us
    ne x1 -> x0, other arithmetic: 0.95 us -> none  [per_device(): fiber_mask[0, 0, 0][..., None] != 0]
  transfers between devices with their start and end apart: 20 -> 16, of which waited for: 8 -> 9; matrix products, arithmetic and copies ran while one was open for 20% -> 4% of each run, Pallas kernels for 0% -> 0%
where the time goes in v2:
time: 69.1 us; the launch traced here: 68.9 us
  starting transfers between devices  31.3 us (45%)
  waiting for transfers between devices  20.7 us (30%)
  Pallas kernels  10.7 us (15%)
  local copies, waits for them, and re-layouts  3.12 us (5%)
  other arithmetic  1.73 us (3%)
  between operations  1.35 us (2%)
    ppermute x16, starting transfers between devices, shift(): lax.ppermute(array, axis, [(i, (i + by) % size) for i in range(size)])  31.3 us
    ppermute x16, waiting for transfers between devices, shift(): lax.ppermute(array, axis, [(i, (i + by) % size) for i in range(size)])  20.7 us
    pallas_call x1, Pallas kernels, per_device(): pl.pallas_call(functools.partial(block_kernel, nx, ny, nz), grid_spec=plt...  9.57 us
    unnamed x8, local copies, waits for them, and re-layouts  3.1 us
  transfers between devices with their start and end apart: 16, of which 9 were waited for; matrix products, arithmetic and copies ran while one was open for 4% of the time, Pallas kernels for 0%

profile of v2, /device:TPU:0, one launch (start us, length us, event | category | flops | bytes accessed | tf_op | source)
XLA Modules:
  0.0 68.9 jit_solution(5336919196469751304)
XLA Ops:
  0.6 0.9 %pad_maximum_fusion.1 = bf16[160,256]{1,0:T(8,128)(2,1)S(1)} fusion(bf16[32,256]{1,0:T(8,128)(2,1)} %bitcast.7, bf16[128,256]{1,0:T(8,128)(2,1)} %bitcast.5), kind=kLoop, calls=%fused_computation.1 | loop fusion | flops 163840 | bytes 163840 | tf_op jit(solution)/shard_map/concatenate | solution.py:204
  1.5 5.0 %collective-permute-start.2 = (bf16[160,256]{1,0:T(8,128)(2,1)S(1)}, bf16[160,256]{1,0:T(8,128)(2,1)S(1)}, u32[]{:S(2)}, u32[]{:S(2)}) collective-permute-start(bf16[160,256]{1,0:T(8,128)(2,1)S(1)} %pad_maximum_fusion.1), channel_id=1, source_target_pairs={{0,3},{1,0},{2,1},{3,2},{4,7},{5,4},{6,5},{7,6},{8,11},{9,8},{10,9... | collective-permute-start | bytes 245768 | tf_op jit(solution)/shard_map/ppermute | solution.py:190
  6.5 1.0 %collective-permute-start = (bf16[160,256]{1,0:T(8,128)(2,1)S(1)}, bf16[160,256]{1,0:T(8,128)(2,1)S(1)}, u32[]{:S(2)}, u32[]{:S(2)}) collective-permute-start(bf16[160,256]{1,0:T(8,128)(2,1)S(1)} %pad_maximum_fusion.1), channel_id=1, source_target_pairs={{0,1},{1,2},{2,3},{3,0},{4,5},{5,6},{6,7},{7,4},{8,9},{9,10},{10,1... | collective-permute-start | bytes 245768 | tf_op jit(solution)/shard_map/ppermute | solution.py:190
  7.6 1.5 %collective-permute-start.4 = (bf16[64,256]{1,0:T(8,128)(2,1)}, bf16[64,256]{1,0:T(8,128)(2,1)S(1)}, u32[]{:S(2)}, u32[]{:S(2)}) collective-permute-start(bf16[64,256]{1,0:T(8,128)(2,1)} %bitcast.8), channel_id=1, source_target_pairs={{0,16},{16,0},{1,17},{17,1},{2,18},{18,2},{3,19},{19,3},{4,20},{20... | collective-permute-start | bytes 98312 | tf_op jit(solution)/shard_map/ppermute | solution.py:190
  9.8 4.3 %collective-permute-done.1 = bf16[160,256]{1,0:T(8,128)(2,1)S(1)} collective-permute-done((bf16[160,256]{1,0:T(8,128)(2,1)S(1)}, bf16[160,256]{1,0:T(8,128)(2,1)S(1)}, u32[]{:S(2)}, u32[]{:S(2)}) %collective-permute-start.1) | collective-permute-done | bytes 81952 | tf_op jit(solution)/shard_map/ppermute | solution.py:190
  14.1 0.9 %pad_maximum_fusion.refs_0_ = bf16[512,256]{1,0:T(8,128)(2,1)S(1)} fusion(bf16[128,256]{1,0:T(8,128)(2,1)S(1)} %slice.26, bf16[128,256]{1,0:T(8,128)(2,1)S(1)} %slice.25, bf16[128,256]{1,0:T(8,128)(2,1)S(1)} %slice.24, bf16[128,256]{1,0:T(8,128)(2,1)} %bitcast.6), kind=kLoop, calls=%fused_computation | loop fusion | flops 1048576 | bytes 524288 | tf_op jit(solution)/shard_map/concatenate | solution.py:206
  15.0 1.6 %collective-permute-start.3 = (bf16[512,256]{1,0:T(8,128)(2,1)S(1)}, bf16[512,256]{1,0:T(8,128)(2,1)S(1)}, u32[]{:S(2)}, u32[]{:S(2)}) collective-permute-start(bf16[512,256]{1,0:T(8,128)(2,1)S(1)} %pad_maximum_fusion.refs_0_), channel_id=1, source_target_pairs={{0,16},{16,0},{1,17},{17,1},{2,18},{18,2},{3,19},{19,3},{4,20},{20... | collective-permute-start | bytes 786440 | tf_op jit(solution)/shard_map/ppermute | solution.py:190
  16.5 0.8 %constant_dynamic-update-slice_fusion.1 = bf16[256,256]{1,0:T(8,128)(2,1)S(1)} fusion(bf16[256,256]{1,0:T(8,128)(2,1)S(1)} %slice_dynamic-update-slice_fusion, bf16[1,64,256]{2,1,0:T(8,128)(2,1)} %param.13), kind=kLoop, calls=%fused_computation.6 | loop fusion | bytes 65536
  17.9 1.1 %collective-permute-start.6 = (bf16[256,256]{1,0:T(8,128)(2,1)S(1)}, bf16[256,256]{1,0:T(8,128)(2,1)S(1)}, u32[]{:S(2)}, u32[]{:S(2)}) collective-permute-start(bf16[256,256]{1,0:T(8,128)(2,1)S(1)} %constant_dynamic-update-slice_fusion.refs_2_), channel_id=1, source_target_pairs={{0,8},{4,12},{8,0},{12,4},{1,9},{5,13},{9,1},{13,5},{2,10},{6,14},... | collective-permute-start | bytes 393224 | tf_op jit(solution)/shard_map/ppermute | solution.py:190
  20.4 0.9 %collective-permute-done.7.refs_5_ = bf16[256,256]{1,0:T(8,128)(2,1)S(1)} collective-permute-done((bf16[256,256]{1,0:T(8,128)(2,1)S(1)}, bf16[256,256]{1,0:T(8,128)(2,1)S(1)}, u32[]{:S(2)}, u32[]{:S(2)}) %collective-permute-start.7) | collective-permute-done | bytes 131104 | tf_op jit(solution)/shard_map/ppermute | solution.py:190
  21.3 4.6 %collective-permute-done.6.refs_4_ = bf16[256,256]{1,0:T(8,128)(2,1)S(1)} collective-permute-done((bf16[256,256]{1,0:T(8,128)(2,1)S(1)}, bf16[256,256]{1,0:T(8,128)(2,1)S(1)}, u32[]{:S(2)}, u32[]{:S(2)}) %collective-permute-start.6) | collective-permute-done | bytes 131104 | tf_op jit(solution)/shard_map/ppermute | solution.py:190
  26.0 0.9 %copy-done = s32[1,1,1,3,128,128]{5,4,3,2,1,0:T(8,128)S(1)} copy-done((s32[1,1,1,3,128,128]{5,4,3,2,1,0:T(8,128)S(1)}, s32[1,1,1,3,128,128]{5,4,3,2,1,0:T(8,128)}, u32[]{:S(2)}) %copy-start) | copy-done | bytes 196632
  27.0 9.6 %blocks.1 = (f32[512,256]{1,0:T(8,128)S(1)}, f32[256,256]{1,0:T(8,128)S(1)}, s16[528,256]{1,0:T(8,128)(2,1)S(1)}, s16[272,256]{1,0:T(8,128)(2,1)S(1)}, s16[272,2...) custom-call(s32[1,1,1]{2,1,0:T(1,128)S(6)} %copy.16.filled, s32[1,1,1,3,3]{4,3,2,1,0:T(4,128)S(1)} %copy.10.coords, ...), custom_call_target="tpu_custom_call" | custom-call | tf_op jit(solution)/shard_map/blocks/pallas_call | solution.py:218
  36.5 13.6 %collective-permute-start.8 = (s16[528,256]{1,0:T(8,128)(2,1)S(1)}, s16[528,256]{1,0:T(8,128)(2,1)S(1)}, u32[]{:S(2)}, u32[]{:S(2)}) collective-permute-start(s16[528,256]{1,0:T(8,128)(2,1)S(1)} %get-tuple-element.17), channel_id=1, source_target_pairs={{0,16},{16,0},{1,17},{17,1},{2,18},{18,2},{3,19},{19,3},{4,20},{20... | collective-permute-start | bytes 811016 | tf_op jit(solution)/shard_map/ppermute | solution.py:190
  50.2 1.1 %collective-permute-start.10 = (s16[272,256]{1,0:T(8,128)(2,1)S(1)}, s16[272,256]{1,0:T(8,128)(2,1)S(1)}, u32[]{:S(2)}, u32[]{:S(2)}) collective-permute-start(s16[272,256]{1,0:T(8,128)(2,1)S(1)} %get-tuple-element.19), channel_id=1, source_target_pairs={{0,8},{4,12},{8,0},{12,4},{1,9},{5,13},{9,1},{13,5},{2,10},{6,14},... | collective-permute-start | bytes 417800 | tf_op jit(solution)/shard_map/ppermute | solution.py:190
  51.2 1.4 %collective-permute-start.11 = (s16[272,256]{1,0:T(8,128)(2,1)S(1)}, s16[272,256]{1,0:T(8,128)(2,1)S(1)}, u32[]{:S(2)}, u32[]{:S(2)}) collective-permute-start(s16[272,256]{1,0:T(8,128)(2,1)S(1)} %get-tuple-element.20), channel_id=1, source_target_pairs={{0,12},{4,0},{8,4},{12,8},{1,13},{5,1},{9,5},{13,9},{2,14},{6,2},{... | collective-permute-start | bytes 417800 | tf_op jit(solution)/shard_map/ppermute | solution.py:190
  52.7 2.9 %collective-permute-done.9.refs_3_ = s16[272,256]{1,0:T(8,128)(2,1)S(1)} collective-permute-done((s16[272,256]{1,0:T(8,128)(2,1)S(1)}, s16[272,256]{1,0:T(8,128)(2,1)S(1)}, u32[]{:S(2)}, u32[]{:S(2)}) %collective-permute-start.9) | collective-permute-done | bytes 139296 | tf_op jit(solution)/shard_map/ppermute | solution.py:190
  55.6 1.1 %collective-permute-done.10.refs_4_ = s16[272,256]{1,0:T(8,128)(2,1)S(1)} collective-permute-done((s16[272,256]{1,0:T(8,128)(2,1)S(1)}, s16[272,256]{1,0:T(8,128)(2,1)S(1)}, u32[]{:S(2)}, u32[]{:S(2)}) %collective-permute-start.10) | collective-permute-done | bytes 139296 | tf_op jit(solution)/shard_map/ppermute | solution.py:190
  56.7 1.0 %collective-permute-done.11.refs_5_ = s16[272,256]{1,0:T(8,128)(2,1)S(1)} collective-permute-done((s16[272,256]{1,0:T(8,128)(2,1)S(1)}, s16[272,256]{1,0:T(8,128)(2,1)S(1)}, u32[]{:S(2)}, u32[]{:S(2)}) %collective-permute-start.11) | collective-permute-done | bytes 139296 | tf_op jit(solution)/shard_map/ppermute | solution.py:190
  58.1 1.3 %collective-permute-start.13 = (s16[176,256]{1,0:T(8,128)(2,1)S(1)}, s16[176,256]{1,0:T(8,128)(2,1)S(1)}, u32[]{:S(2)}, u32[]{:S(2)}) collective-permute-start(s16[176,256]{1,0:T(8,128)(2,1)S(1)} %get-tuple-element.24), channel_id=1, source_target_pairs={{0,2},{1,3},{2,0},{3,1},{4,6},{5,7},{6,4},{7,5},{8,10},{9,11},{10,... | collective-permute-start | bytes 270344 | tf_op jit(solution)/shard_map/ppermute | solution.py:190
  59.4 2.7 %collective-permute-start.14 = (s16[176,256]{1,0:T(8,128)(2,1)S(1)}, s16[176,256]{1,0:T(8,128)(2,1)S(1)}, u32[]{:S(2)}, u32[]{:S(2)}) collective-permute-start(s16[176,256]{1,0:T(8,128)(2,1)S(1)} %get-tuple-element.25), channel_id=1, source_target_pairs={{0,3},{1,0},{2,1},{3,2},{4,7},{5,4},{6,5},{7,6},{8,11},{9,8},{10,9... | collective-permute-start | bytes 270344 | tf_op jit(solution)/shard_map/ppermute | solution.py:190
  62.3 3.9 %collective-permute-done.15.refs_5_ = s16[80,256]{1,0:T(8,128)(2,1)S(1)} collective-permute-done((s16[80,256]{1,0:T(8,128)(2,1)S(1)}, s16[80,256]{1,0:T(8,128)(2,1)S(1)}, u32[]{:S(2)}, u32[]{:S(2)}) %collective-permute-start.15) | collective-permute-done | bytes 40992 | tf_op jit(solution)/shard_map/ppermute | solution.py:190
  66.1 2.0 %collective-permute-done.13.refs_3_ = s16[176,256]{1,0:T(8,128)(2,1)S(1)} collective-permute-done((s16[176,256]{1,0:T(8,128)(2,1)S(1)}, s16[176,256]{1,0:T(8,128)(2,1)S(1)}, u32[]{:S(2)}, u32[]{:S(2)}) %collective-permute-start.13) | collective-permute-done | bytes 90144 | tf_op jit(solution)/shard_map/ppermute | solution.py:190
  68.2 0.7 %last.1 = (f32[1,32,256]{2,1,0:T(8,128)}, f32[1,128,256]{2,1,0:T(8,128)}, f32[1,64,256]{2,1,0:T(8,128)}) custom-call(f32[160,256]{1,0:T(8,128)S(1)} %get-tuple-element.21.refs_0_, f32[64,256]{1,0:T(8,128)S(1)} %get-tuple-element.22.refs_1_, s16[176,256]{1,0:T(8,128)(2,1)S(1)} %collective-permute-done.12.refs_2_, ...), custom_call_target="tpu_custom_call" | custom-call | tf_op jit(solution)/shard_map/last/pallas_call | solution.py:257
  (25 shorter events, 2.8 us)
Async XLA Ops:
  1.5 8.3 %collective-permute-start.2 = (bf16[160,256]{1,0:T(8,128)(2,1)S(1)}, bf16[160,256]{1,0:T(8,128)(2,1)S(1)}, u32[]{:S(2)}, u32[]{:S(2)}) collective-permute-start(bf16[160,256]{1,0:T(8,128)(2,1)S(1)} %pad_maximum_fusion.1), channel_id=1, source_target_pairs={{0,3},{1,0},{2,1},{3,2},{4,7},{5,4},{6,5},{7,6},{8,11},{9,8},{10,9... | collective-permute-start | bytes 245768 | tf_op jit(solution)/shard_map/ppermute | solution.py:190
  6.5 7.5 %collective-permute-start.1 = (bf16[160,256]{1,0:T(8,128)(2,1)S(1)}, bf16[160,256]{1,0:T(8,128)(2,1)S(1)}, u32[]{:S(2)}, u32[]{:S(2)}) collective-permute-start(bf16[160,256]{1,0:T(8,128)(2,1)S(1)} %pad_maximum_fusion.1), channel_id=1, source_target_pairs={{0,2},{1,3},{2,0},{3,1},{4,6},{5,7},{6,4},{7,5},{8,10},{9,11},{10,... | collective-permute-start | bytes 245768 | tf_op jit(solution)/shard_map/ppermute | solution.py:190
  6.5 7.5 %collective-permute-start = (bf16[160,256]{1,0:T(8,128)(2,1)S(1)}, bf16[160,256]{1,0:T(8,128)(2,1)S(1)}, u32[]{:S(2)}, u32[]{:S(2)}) collective-permute-start(bf16[160,256]{1,0:T(8,128)(2,1)S(1)} %pad_maximum_fusion.1), channel_id=1, source_target_pairs={{0,1},{1,2},{2,3},{3,0},{4,5},{5,6},{6,7},{7,4},{8,9},{9,10},{10,1... | collective-permute-start | bytes 245768 | tf_op jit(solution)/shard_map/ppermute | solution.py:190
  7.6 9.8 %collective-permute-start.4 = (bf16[64,256]{1,0:T(8,128)(2,1)}, bf16[64,256]{1,0:T(8,128)(2,1)S(1)}, u32[]{:S(2)}, u32[]{:S(2)}) collective-permute-start(bf16[64,256]{1,0:T(8,128)(2,1)} %bitcast.8), channel_id=1, source_target_pairs={{0,16},{16,0},{1,17},{17,1},{2,18},{18,2},{3,19},{19,3},{4,20},{20... | collective-permute-start | bytes 98312 | tf_op jit(solution)/shard_map/ppermute | solution.py:190
  15.0 11.1 %collective-permute-start.3 = (bf16[512,256]{1,0:T(8,128)(2,1)S(1)}, bf16[512,256]{1,0:T(8,128)(2,1)S(1)}, u32[]{:S(2)}, u32[]{:S(2)}) collective-permute-start(bf16[512,256]{1,0:T(8,128)(2,1)S(1)} %pad_maximum_fusion.refs_0_), channel_id=1, source_target_pairs={{0,16},{16,0},{1,17},{17,1},{2,18},{18,2},{3,19},{19,3},{4,20},{20... | collective-permute-start | bytes 786440 | tf_op jit(solution)/shard_map/ppermute | solution.py:190
  17.3 4.0 %collective-permute-start.7 = (bf16[256,256]{1,0:T(8,128)(2,1)S(1)}, bf16[256,256]{1,0:T(8,128)(2,1)S(1)}, u32[]{:S(2)}, u32[]{:S(2)}) collective-permute-start(bf16[256,256]{1,0:T(8,128)(2,1)S(1)} %constant_dynamic-update-slice_fusion.refs_2_), channel_id=1, source_target_pairs={{0,12},{4,0},{8,4},{12,8},{1,13},{5,1},{9,5},{13,9},{2,14},{6,2},{... | collective-permute-start | bytes 393224 | tf_op jit(solution)/shard_map/ppermute | solution.py:190
  17.9 8.1 %collective-permute-start.6 = (bf16[256,256]{1,0:T(8,128)(2,1)S(1)}, bf16[256,256]{1,0:T(8,128)(2,1)S(1)}, u32[]{:S(2)}, u32[]{:S(2)}) collective-permute-start(bf16[256,256]{1,0:T(8,128)(2,1)S(1)} %constant_dynamic-update-slice_fusion.refs_2_), channel_id=1, source_target_pairs={{0,8},{4,12},{8,0},{12,4},{1,9},{5,13},{9,1},{13,5},{2,10},{6,14},... | collective-permute-start | bytes 393224 | tf_op jit(solution)/shard_map/ppermute | solution.py:190
  18.9 7.1 %collective-permute-start.5 = (bf16[256,256]{1,0:T(8,128)(2,1)S(1)}, bf16[256,256]{1,0:T(8,128)(2,1)S(1)}, u32[]{:S(2)}, u32[]{:S(2)}) collective-permute-start(bf16[256,256]{1,0:T(8,128)(2,1)S(1)} %constant_dynamic-update-slice_fusion.refs_2_), channel_id=1, source_target_pairs={{0,4},{4,8},{8,12},{12,0},{1,5},{5,9},{9,13},{13,1},{2,6},{6,10},{... | collective-permute-start | bytes 393224 | tf_op jit(solution)/shard_map/ppermute | solution.py:190
  26.0 0.9 %copy-start = (s32[1,1,1,3,128,128]{5,4,3,2,1,0:T(8,128)S(1)}, s32[1,1,1,3,128,128]{5,4,3,2,1,0:T(8,128)}, u32[]{:S(2)}) copy-start(s32[1,1,1,3,128,128]{5,4,3,2,1,0:T(8,128)} %fibers.1) | copy-start | bytes 589828
  36.5 21.2 %collective-permute-start.8 = (s16[528,256]{1,0:T(8,128)(2,1)S(1)}, s16[528,256]{1,0:T(8,128)(2,1)S(1)}, u32[]{:S(2)}, u32[]{:S(2)}) collective-permute-start(s16[528,256]{1,0:T(8,128)(2,1)S(1)} %get-tuple-element.17), channel_id=1, source_target_pairs={{0,16},{16,0},{1,17},{17,1},{2,18},{18,2},{3,19},{19,3},{4,20},{20... | collective-permute-start | bytes 811016 | tf_op jit(solution)/shard_map/ppermute | solution.py:190
  50.2 5.4 %collective-permute-start.9 = (s16[272,256]{1,0:T(8,128)(2,1)S(1)}, s16[272,256]{1,0:T(8,128)(2,1)S(1)}, u32[]{:S(2)}, u32[]{:S(2)}) collective-permute-start(s16[272,256]{1,0:T(8,128)(2,1)S(1)} %get-tuple-element.18), channel_id=1, source_target_pairs={{0,4},{4,8},{8,12},{12,0},{1,5},{5,9},{9,13},{13,1},{2,6},{6,10},{... | collective-permute-start | bytes 417800 | tf_op jit(solution)/shard_map/ppermute | solution.py:190
  50.2 6.5 %collective-permute-start.10 = (s16[272,256]{1,0:T(8,128)(2,1)S(1)}, s16[272,256]{1,0:T(8,128)(2,1)S(1)}, u32[]{:S(2)}, u32[]{:S(2)}) collective-permute-start(s16[272,256]{1,0:T(8,128)(2,1)S(1)} %get-tuple-element.19), channel_id=1, source_target_pairs={{0,8},{4,12},{8,0},{12,4},{1,9},{5,13},{9,1},{13,5},{2,10},{6,14},... | collective-permute-start | bytes 417800 | tf_op jit(solution)/shard_map/ppermute | solution.py:190
  51.2 6.4 %collective-permute-start.11 = (s16[272,256]{1,0:T(8,128)(2,1)S(1)}, s16[272,256]{1,0:T(8,128)(2,1)S(1)}, u32[]{:S(2)}, u32[]{:S(2)}) collective-permute-start(s16[272,256]{1,0:T(8,128)(2,1)S(1)} %get-tuple-element.20), channel_id=1, source_target_pairs={{0,12},{4,0},{8,4},{12,8},{1,13},{5,1},{9,5},{13,9},{2,14},{6,2},{... | collective-permute-start | bytes 417800 | tf_op jit(solution)/shard_map/ppermute | solution.py:190
  58.1 8.1 %collective-permute-start.12 = (s16[176,256]{1,0:T(8,128)(2,1)S(1)}, s16[176,256]{1,0:T(8,128)(2,1)S(1)}, u32[]{:S(2)}, u32[]{:S(2)}) collective-permute-start(s16[176,256]{1,0:T(8,128)(2,1)S(1)} %get-tuple-element.23), channel_id=1, source_target_pairs={{0,1},{1,2},{2,3},{3,0},{4,5},{5,6},{6,7},{7,4},{8,9},{9,10},{10,1... | collective-permute-start | bytes 270344 | tf_op jit(solution)/shard_map/ppermute | solution.py:190
  58.1 10.0 %collective-permute-start.13 = (s16[176,256]{1,0:T(8,128)(2,1)S(1)}, s16[176,256]{1,0:T(8,128)(2,1)S(1)}, u32[]{:S(2)}, u32[]{:S(2)}) collective-permute-start(s16[176,256]{1,0:T(8,128)(2,1)S(1)} %get-tuple-element.24), channel_id=1, source_target_pairs={{0,2},{1,3},{2,0},{3,1},{4,6},{5,7},{6,4},{7,5},{8,10},{9,11},{10,... | collective-permute-start | bytes 270344 | tf_op jit(solution)/shard_map/ppermute | solution.py:190
  59.4 8.7 %collective-permute-start.14 = (s16[176,256]{1,0:T(8,128)(2,1)S(1)}, s16[176,256]{1,0:T(8,128)(2,1)S(1)}, u32[]{:S(2)}, u32[]{:S(2)}) collective-permute-start(s16[176,256]{1,0:T(8,128)(2,1)S(1)} %get-tuple-element.25), channel_id=1, source_target_pairs={{0,3},{1,0},{2,1},{3,2},{4,7},{5,4},{6,5},{7,6},{8,11},{9,8},{10,9... | collective-permute-start | bytes 270344 | tf_op jit(solution)/shard_map/ppermute | solution.py:190
  62.1 4.0 %collective-permute-start.15 = (s16[80,256]{1,0:T(8,128)(2,1)S(1)}, s16[80,256]{1,0:T(8,128)(2,1)S(1)}, u32[]{:S(2)}, u32[]{:S(2)}) collective-permute-start(s16[80,256]{1,0:T(8,128)(2,1)S(1)} %get-tuple-element.26), channel_id=1, source_target_pairs={{0,16},{16,0},{1,17},{17,1},{2,18},{18,2},{3,19},{19,3},{4,20},{20... | collective-permute-start | bytes 122888 | tf_op jit(solution)/shard_map/ppermute | solution.py:190

commit v3 on v2

--- a/solution.py
+++ b/solution.py
@@ -8,7 +8,7 @@
 from jax.sharding import PartitionSpec as P
 
 BLK = 128
-STEP = 64
+CHUNK = 32
 GROUP = 8
 PAD = 16
 TOP = 32000.0
@@ -37,102 +37,119 @@
     return parts
 
 
-def block_kernel(nx, ny, nz, filled, coords, entries, fibers, *refs):
+def add_block(slot, coords, weights, slabs, grads, held):
+    slab_a, slab_b, slab_c = slabs
+    grad_a, grad_b, grad_c = grads
+    f32, bf16 = jnp.float32, jnp.bfloat16
+    at_a, at_b, at_c = (pl.multiple_of(coords[0, 0, 0, i, slot] * BLK, BLK) for i in range(3))
+    rows_a = slab_a[pl.ds(at_a, BLK), :].astype(f32)
+    rows_b = slab_b[pl.ds(at_b, BLK), :]
+    rows_c = slab_c[pl.ds(at_c, BLK), :]
+    rank = rows_b.shape[1]
+    wide_b = rows_b.astype(f32)
+    weight = weights[slot]
+
+    def start(first):
+        mixed = []
+        for u in range(first, first + GROUP):
+            row = jnp.broadcast_to(rows_a[u : u + 1, :], (16, rank)).astype(bf16)
+            mixed.append((rows_b.reshape(BLK // 16, 16, rank) * row[None]).reshape(BLK, rank))
+        mixed = jnp.concatenate(mixed, 0)
+        return mixed, lax.dot_general(mixed, rows_c, (((1,), (1,)), ((), ())), preferred_element_type=f32)
+
+    sum_b = sum_c = jnp.zeros((BLK, rank), f32)
+    parts = []
+    later = start(0)
+    for first in range(0, BLK, GROUP):
+        mixed, rate = later
+        if first + GROUP < BLK:
+            later = start(first + GROUP)
+        error = []
+        for i in range(GROUP):
+            seen = held[slot, first + i].astype(f32)
+            one = (jnp.exp(rate[i * BLK : (i + 1) * BLK]) - seen).astype(bf16)
+            error.append(one * weight[:, first + i : first + i + 1])
+        error = jnp.concatenate(error, 0)
+        spread = jnp.dot(error, rows_c, preferred_element_type=f32)
+        for i in range(GROUP):
+            mine = spread[i * BLK : (i + 1) * BLK]
+            sum_b = sum_b + mine * rows_a[first + i : first + i + 1, :]
+            parts.append(jnp.sum(mine * wide_b, 0, keepdims=True))
+        sum_c = sum_c + lax.dot_general(error, mixed, (((0,), (0,)), ((), ())), preferred_element_type=f32)
+    grad_a[pl.ds(at_a, BLK), :] += jnp.concatenate(parts, 0)
+    grad_b[pl.ds(at_b, BLK), :] += sum_b
+    grad_c[pl.ds(at_c, BLK), :] += sum_c
+
+
+def block_kernel(nx, ny, nz, filled, coords, entries, weights, *refs):
     got_b, got_ac = refs[:nx], refs[nx : nx + ny]
     refs = refs[nx + ny :]
     own_b, own_ac = refs[:2]
     send_b, send_ac = refs[2 : 1 + nx], refs[1 + nx : nx + ny]
-    slab_a, slab_b, slab_c, grad_a, grad_b, grad_c = refs[nx + ny :]
+    slab_a, slab_b, slab_c, grad_a, grad_b, grad_c, held, arrivals = refs[nx + ny :]
     x, y, z = (lax.axis_index(name) for name in ("gx", "gy", "gz"))
-    rank = slab_a.shape[1]
     all_a, all_b, all_c = (s.shape[0] for s in (slab_a, slab_b, slab_c))
     per_a, per_b, per_c = all_a // (ny * nz), all_b // (nx * nz), all_c // (nx * ny)
-    slot, step = pl.program_id(0), pl.program_id(1)
-
-    @pl.when((slot == 0) & (step == 0))
-    def _():
-        grad_a[...] = jnp.zeros_like(grad_a)
-        grad_b[...] = jnp.zeros_like(grad_b)
-        grad_c[...] = jnp.zeros_like(grad_c)
-        for j in range(nz):
-            of_z = lax.rem(z + nz - j, nz)
-            for i in range(nx):
-                at = (lax.rem(x + nx - i, nx) * nz + of_z) * per_b
-                slab_b[pl.ds(pl.multiple_of(at, per_b), per_b), :] = got_b[i][j * per_b : (j + 1) * per_b, :]
-            for i in range(ny):
-                at = (lax.rem(y + ny - i, ny) * nz + of_z) * per_a
-                slab_a[pl.ds(pl.multiple_of(at, per_a), per_a), :] = got_ac[i][j * per_a : (j + 1) * per_a, :]
-        for j in range(nx):
-            of_x = lax.rem(x + nx - j, nx)
-            for i in range(ny):
-                at = (of_x * ny + lax.rem(y + ny - i, ny)) * per_c
-                first = nz * per_a + j * per_c
-                slab_c[pl.ds(pl.multiple_of(at, per_c), per_c), :] = got_ac[i][first : first + per_c, :]
-
-    @pl.when(slot < filled[0, 0, 0])
-    def _():
-        at_a = pl.multiple_of(coords[0, 0, 0, 0, slot] * BLK + step * STEP, STEP)
-        at_b = pl.multiple_of(coords[0, 0, 0, 1, slot] * BLK, BLK)
-        at_c = pl.multiple_of(coords[0, 0, 0, 2, slot] * BLK, BLK)
-        rows_a = slab_a[pl.ds(at_a, STEP), :].astype(jnp.float32)
-        rows_b = slab_b[pl.ds(at_b, BLK), :]
-        rows_c = slab_c[pl.ds(at_c, BLK), :]
-        wide_b = rows_b.astype(jnp.float32)
-        sum_b = jnp.zeros((BLK, rank), jnp.float32)
-        sum_c = jnp.zeros((BLK, rank), jnp.float32)
-        parts = []
-        weight = jnp.transpose(fibers[0, 0, 0, 0].astype(jnp.float32)).astype(jnp.bfloat16)
-        for first in range(0, STEP, GROUP):
-            mixed = []
-            for u in range(first, first + GROUP):
-                row = jnp.broadcast_to(rows_a[u : u + 1, :], (16, rank)).astype(jnp.bfloat16)
-                mixed.append((rows_b.reshape(BLK // 16, 16, rank) * row[None]).reshape(BLK, rank))
-            mixed = jnp.concatenate(mixed, 0)
-            rate = lax.dot_general(mixed, rows_c, (((1,), (1,)), ((), ())), preferred_element_type=jnp.float32)
-            seen = entries[0, 0, 0, 0, first : first + GROUP].reshape(GROUP * BLK, BLK).astype(jnp.float32)
-            error = (jnp.exp(rate) - seen).astype(jnp.bfloat16)
-            error = [
-                error[i * BLK : (i + 1) * BLK] * weight[:, first + i : first + i + 1] for i in range(GROUP)
-            ]
-            error = jnp.concatenate(error, 0)
-            spread = jnp.dot(error, rows_c, preferred_element_type=jnp.float32)
-            for i in range(GROUP):
-                mine = spread[i * BLK : (i + 1) * BLK]
-                sum_b = sum_b + mine * rows_a[first + i : first + i + 1, :]
-                parts.append(jnp.sum(mine * wide_b, 0, keepdims=True))
-            sum_c = sum_c + lax.dot_general(
-                error, mixed, (((0,), (0,)), ((), ())), preferred_element_type=jnp.float32
-            )
-        grad_a[pl.ds(at_a, STEP), :] += jnp.concatenate(parts, 0)
-        grad_b[pl.ds(at_b, BLK), :] += sum_b
-        grad_c[pl.ds(at_c, BLK), :] += sum_c
-
-    @pl.when((slot == pl.num_programs(0) - 1) & (step == pl.num_programs(1) - 1))
-    def _():
-        some_b, some_a = all_b // nx, all_a // ny
+    count = filled[0, 0, 0]
+
+    def copy(slot, chunk):
+        rows = pl.ds(chunk * CHUNK, CHUNK)
+        return pltpu.make_async_copy(
+            entries.at[0, 0, 0, slot, rows], held.at[slot, rows], arrivals.at[slot, chunk]
+        )
+
+    def fetch(slot):
+        @pl.when(slot < count)
+        def _():
+            for chunk in range(BLK // CHUNK):
+                copy(slot, chunk).start()
+
+    fetch(0)
+    grad_a[...] = jnp.zeros_like(grad_a)
+    grad_b[...] = jnp.zeros_like(grad_b)
+    grad_c[...] = jnp.zeros_like(grad_c)
+    for j in range(nz):
+        of_z = lax.rem(z + nz - j, nz)
         for i in range(nx):
-            to_x = lax.rem(x + i, nx)
-            part_b = grad_b[pl.ds(pl.multiple_of(to_x * some_b, some_b), some_b), :]
-            if i == 0:
-                own_b[...] = part_b
-            else:
-                pack((part_b,), send_b[i - 1])
+            at = (lax.rem(x + nx - i, nx) * nz + of_z) * per_b
+            slab_b[pl.ds(pl.multiple_of(at, per_b), per_b), :] = got_b[i][j * per_b : (j + 1) * per_b, :]
         for i in range(ny):
-            to_y = lax.rem(y + i, ny)
-            part_a = grad_a[pl.ds(pl.multiple_of(to_y * some_a, some_a), some_a), :]
-            part_c = jnp.concatenate(
-                [grad_c[pl.ds(pl.multiple_of((j * ny + to_y) * per_c, per_c), per_c), :] for j in range(nx)], 0
-            )
-            if i == 0:
-                own_ac[:some_a, :] = part_a
-                own_ac[some_a:, :] = part_c
-            else:
-                pack((part_a, part_c), send_ac[i - 1])
-
-
-def whole(array):
-    zeros = (0,) * len(array.shape)
-    return pl.BlockSpec(array.shape, lambda *_: zeros)
+            at = (lax.rem(y + ny - i, ny) * nz + of_z) * per_a
+            slab_a[pl.ds(pl.multiple_of(at, per_a), per_a), :] = got_ac[i][j * per_a : (j + 1) * per_a, :]
+    for j in range(nx):
+        of_x = lax.rem(x + nx - j, nx)
+        for i in range(ny):
+            at = (of_x * ny + lax.rem(y + ny - i, ny)) * per_c
+            first = nz * per_a + j * per_c
+            slab_c[pl.ds(pl.multiple_of(at, per_c), per_c), :] = got_ac[i][first : first + per_c, :]
+
+    @pl.loop(0, count)
+    def _(slot):
+        slabs, grads = (slab_a, slab_b, slab_c), (grad_a, grad_b, grad_c)
+        for chunk in range(BLK // CHUNK):
+            copy(slot, chunk).wait()
+        fetch(slot + 1)
+        add_block(slot, coords, weights, slabs, grads, held)
+
+    some_b, some_a = all_b // nx, all_a // ny
+    for i in range(nx):
+        to_x = lax.rem(x + i, nx)
+        part_b = grad_b[pl.ds(pl.multiple_of(to_x * some_b, some_b), some_b), :]
+        if i == 0:
+            own_b[...] = part_b
+        else:
+            pack((part_b,), send_b[i - 1])
+    for i in range(ny):
+        to_y = lax.rem(y + i, ny)
+        part_a = grad_a[pl.ds(pl.multiple_of(to_y * some_a, some_a), some_a), :]
+        part_c = jnp.concatenate(
+            [grad_c[pl.ds(pl.multiple_of((j * ny + to_y) * per_c, per_c), per_c), :] for j in range(nx)], 0
+        )
+        if i == 0:
+            own_ac[:some_a, :] = part_a
+            own_ac[some_a:, :] = part_c
+        else:
+            pack((part_a, part_c), send_ac[i - 1])
 
 
 def middle_kernel(nx, ny, nz, sizes, *refs):
@@ -206,36 +223,23 @@
     got_b = around(jnp.concatenate([p[:per_b] for p in along_z], 0), "gx", nx)
     got_ac = around(jnp.concatenate([p[per_b:] for p in along_z] + along_x, 0), "gy", ny)
 
-    def where(slot, step, filled, coords):
-        held = filled[0, 0, 0]
-        last = jnp.maximum(held - 1, 0)
-        return (0, 0, 0, jnp.minimum(slot, last), jnp.where(slot < held, step, BLK // STEP - 1), 0, 0)
-
+    weights = jnp.swapaxes(fiber_mask[0, 0, 0], 1, 2).astype(jnp.bfloat16)
     f32, i16 = jnp.float32, jnp.int16
     outs = [jax.ShapeDtypeStruct((some_b, rank), f32), jax.ShapeDtypeStruct((some_a + some_c, rank), f32)]
     outs += [jax.ShapeDtypeStruct((some_b + PAD, rank), i16)] * (nx - 1)
     outs += [jax.ShapeDtypeStruct((some_a + some_c + PAD, rank), i16)] * (ny - 1)
     results = pl.pallas_call(
         functools.partial(block_kernel, nx, ny, nz),
-        grid_spec=pltpu.PrefetchScalarGridSpec(
-            num_scalar_prefetch=2,
-            grid=(slots, BLK // STEP),
-            in_specs=[
-                pl.BlockSpec((1, 1, 1, 1, STEP, BLK, BLK), where),
-                pl.BlockSpec((1, 1, 1, 1, STEP, BLK), lambda *at: where(*at)[:-1]),
-                *map(whole, got_b),
-                *map(whole, got_ac),
-            ],
-            out_specs=[*map(whole, outs)],
-            scratch_shapes=[pltpu.VMEM((n, rank), jnp.bfloat16) for n in (all_a, all_b, all_c)]
-            + [pltpu.VMEM((n, rank), f32) for n in (all_a, all_b, all_c)],
-        ),
+        in_specs=[pl.BlockSpec(memory_space=pltpu.SMEM)] * 2
+        + [pl.BlockSpec(memory_space=pl.ANY)]
+        + [pl.BlockSpec(memory_space=pltpu.VMEM)] * (1 + nx + ny),
+        scratch_shapes=[pltpu.VMEM((n, rank), jnp.bfloat16) for n in (all_a, all_b, all_c)]
+        + [pltpu.VMEM((n, rank), f32) for n in (all_a, all_b, all_c)]
+        + [pltpu.VMEM((slots, BLK, BLK, BLK), jnp.bfloat16), pltpu.SemaphoreType.DMA((slots, BLK // CHUNK))],
         out_shape=outs,
-        compiler_params=pltpu.CompilerParams(
-            vmem_limit_bytes=40 * 2**20, dimension_semantics=("arbitrary", "arbitrary")
-        ),
+        compiler_params=pltpu.CompilerParams(vmem_limit_bytes=44 * 2**20),
         name="blocks",
-    )(block_counts, block_coords, tensor_blocks, fiber_mask, *got_b, *got_ac)
+    )(block_counts, block_coords, tensor_blocks, weights, *got_b, *got_ac)
 
     own_b, own_ac = results[:2]
     got_b = [shift(r, "gx", nx, i + 1) for i, r in enumerate(results[2 : 1 + nx])]

time: 69.1 us -> 66.3 us (0.959)
  waiting for transfers between devices: 20.7 us -> 18.4 us
    ppermute x16, waiting for transfers between devices: 20.7 us -> 18.4 us  [shift(): lax.ppermute(array, axis, [(i, (i + by) % size) for i in range(size)])]
    unnamed x8 -> x7, local copies, waits for them, and re-layouts: 3.1 us -> 3.22 us
  transfers between devices with their start and end apart: 16 -> 16, of which waited for: 9 -> 10; matrix products, arithmetic and copies ran while one was open for 4% -> 6% of each run, Pallas kernels for 0% -> 0%
where the time goes in v3:
time: 66.3 us; the launch traced here: 66.7 us
  starting transfers between devices  31.6 us (48%)
  waiting for transfers between devices  18.4 us (28%)
  Pallas kernels  10.4 us (16%)
  local copies, waits for them, and re-layouts  3.24 us (5%)
  other arithmetic  1.74 us (3%)
  between operations  1.34 us (2%)
    ppermute x16, starting transfers between devices, shift(): lax.ppermute(array, axis, [(i, (i + by) % size) for i in range(size)])  31.6 us
    ppermute x16, waiting for transfers between devices, shift(): lax.ppermute(array, axis, [(i, (i + by) % size) for i in range(size)])  18.4 us
    pallas_call x1, Pallas kernels, per_device(): pl.pallas_call(functools.partial(block_kernel, nx, ny, nz), in_specs=[pl....  9.27 us
    unnamed x7, local copies, waits for them, and re-layouts  3.22 us
  transfers between devices with their start and end apart: 16, of which 10 were waited for; matrix products, arithmetic and copies ran while one was open for 6% of the time, Pallas kernels for 0%

profile of v3, /device:TPU:0, one launch (start us, length us, event | category | flops | bytes accessed | tf_op | source)
XLA Modules:
  0.0 66.7 jit_solution(14903577743146739992)
XLA Ops:
  0.6 0.9 %pad_maximum_fusion.1 = bf16[160,256]{1,0:T(8,128)(2,1)S(1)} fusion(bf16[32,256]{1,0:T(8,128)(2,1)} %bitcast.11, bf16[128,256]{1,0:T(8,128)(2,1)} %bitcast.9), kind=kLoop, calls=%fused_computation.2 | loop fusion | flops 163840 | bytes 163840 | tf_op jit(solution)/shard_map/concatenate | solution.py:221
  1.5 5.0 %collective-permute-start.2 = (bf16[160,256]{1,0:T(8,128)(2,1)S(1)}, bf16[160,256]{1,0:T(8,128)(2,1)S(1)}, u32[]{:S(2)}, u32[]{:S(2)}) collective-permute-start(bf16[160,256]{1,0:T(8,128)(2,1)S(1)} %pad_maximum_fusion.1), channel_id=1, source_target_pairs={{0,3},{1,0},{2,1},{3,2},{4,7},{5,4},{6,5},{7,6},{8,11},{9,8},{10,9... | collective-permute-start | bytes 245768 | tf_op jit(solution)/shard_map/ppermute | solution.py:207
  6.5 1.0 %collective-permute-start = (bf16[160,256]{1,0:T(8,128)(2,1)S(1)}, bf16[160,256]{1,0:T(8,128)(2,1)S(1)}, u32[]{:S(2)}, u32[]{:S(2)}) collective-permute-start(bf16[160,256]{1,0:T(8,128)(2,1)S(1)} %pad_maximum_fusion.1), channel_id=1, source_target_pairs={{0,1},{1,2},{2,3},{3,0},{4,5},{5,6},{6,7},{7,4},{8,9},{9,10},{10,1... | collective-permute-start | bytes 245768 | tf_op jit(solution)/shard_map/ppermute | solution.py:207
  7.6 1.5 %collective-permute-start.4 = (bf16[64,256]{1,0:T(8,128)(2,1)}, bf16[64,256]{1,0:T(8,128)(2,1)S(1)}, u32[]{:S(2)}, u32[]{:S(2)}) collective-permute-start(bf16[64,256]{1,0:T(8,128)(2,1)} %bitcast.12), channel_id=1, source_target_pairs={{0,16},{16,0},{1,17},{17,1},{2,18},{18,2},{3,19},{19,3},{4,20},{20... | collective-permute-start | bytes 98312 | tf_op jit(solution)/shard_map/ppermute | solution.py:207
  11.1 1.1 %copy.10 = s32[1,1,1,3,128,128]{4,5,3,2,1,0:T(8,128)S(1)} copy(s32[1,1,1,3,128,128]{5,4,3,2,1,0:T(8,128)} %param.8) | data formatting | bytes 393216 | tf_op args[1]
  12.8 1.3 %collective-permute-done.1 = bf16[160,256]{1,0:T(8,128)(2,1)S(1)} collective-permute-done((bf16[160,256]{1,0:T(8,128)(2,1)S(1)}, bf16[160,256]{1,0:T(8,128)(2,1)S(1)}, u32[]{:S(2)}, u32[]{:S(2)}) %collective-permute-start.1) | collective-permute-done | bytes 81952 | tf_op jit(solution)/shard_map/ppermute | solution.py:207
  14.1 0.8 %constant_dynamic-update-slice_fusion.1 = bf16[256,256]{1,0:T(8,128)(2,1)S(1)} fusion(bf16[256,256]{1,0:T(8,128)(2,1)S(1)} %slice_dynamic-update-slice_fusion, bf16[1,64,256]{2,1,0:T(8,128)(2,1)} %param.13), kind=kLoop, calls=%fused_computation.7 | loop fusion | bytes 65536
  14.9 0.9 %pad_maximum_fusion.refs_0_ = bf16[512,256]{1,0:T(8,128)(2,1)S(1)} fusion(bf16[128,256]{1,0:T(8,128)(2,1)S(1)} %slice.26, bf16[128,256]{1,0:T(8,128)(2,1)S(1)} %slice.25, bf16[128,256]{1,0:T(8,128)(2,1)S(1)} %slice.24, bf16[128,256]{1,0:T(8,128)(2,1)} %bitcast.10), kind=kLoop, calls=%fused_computation | loop fusion | flops 1048576 | bytes 524288 | tf_op jit(solution)/shard_map/concatenate | solution.py:223
  15.7 1.6 %collective-permute-start.3 = (bf16[512,256]{1,0:T(8,128)(2,1)S(1)}, bf16[512,256]{1,0:T(8,128)(2,1)S(1)}, u32[]{:S(2)}, u32[]{:S(2)}) collective-permute-start(bf16[512,256]{1,0:T(8,128)(2,1)S(1)} %pad_maximum_fusion.refs_0_), channel_id=1, source_target_pairs={{0,16},{16,0},{1,17},{17,1},{2,18},{18,2},{3,19},{19,3},{4,20},{20... | collective-permute-start | bytes 786440 | tf_op jit(solution)/shard_map/ppermute | solution.py:207
  17.8 1.0 %collective-permute-start.6 = (bf16[256,256]{1,0:T(8,128)(2,1)S(1)}, bf16[256,256]{1,0:T(8,128)(2,1)S(1)}, u32[]{:S(2)}, u32[]{:S(2)}) collective-permute-start(bf16[256,256]{1,0:T(8,128)(2,1)S(1)} %constant_dynamic-update-slice_fusion.refs_2_), channel_id=1, source_target_pairs={{0,8},{4,12},{8,0},{12,4},{1,9},{5,13},{9,1},{13,5},{2,10},{6,14},... | collective-permute-start | bytes 393224 | tf_op jit(solution)/shard_map/ppermute | solution.py:207
  19.1 2.2 %collective-permute-done.7.refs_5_ = bf16[256,256]{1,0:T(8,128)(2,1)S(1)} collective-permute-done((bf16[256,256]{1,0:T(8,128)(2,1)S(1)}, bf16[256,256]{1,0:T(8,128)(2,1)S(1)}, u32[]{:S(2)}, u32[]{:S(2)}) %collective-permute-start.7) | collective-permute-done | bytes 131104 | tf_op jit(solution)/shard_map/ppermute | solution.py:207
  21.3 4.6 %collective-permute-done.6.refs_4_ = bf16[256,256]{1,0:T(8,128)(2,1)S(1)} collective-permute-done((bf16[256,256]{1,0:T(8,128)(2,1)S(1)}, bf16[256,256]{1,0:T(8,128)(2,1)S(1)}, u32[]{:S(2)}, u32[]{:S(2)}) %collective-permute-start.6) | collective-permute-done | bytes 131104 | tf_op jit(solution)/shard_map/ppermute | solution.py:207
  26.0 9.3 %blocks.1 = (f32[512,256]{1,0:T(8,128)S(1)}, f32[256,256]{1,0:T(8,128)S(1)}, s16[528,256]{1,0:T(8,128)(2,1)S(1)}, s16[272,256]{1,0:T(8,128)(2,1)S(1)}, s16[272,2...) custom-call(s32[1,1,1]{2,1,0:T(1,128)S(6)} %copy.17.filled, s32[1,1,1,3,3]{4,3,2,1,0:T(4,128)S(1)} %copy.11.coords, ...), custom_call_target="tpu_custom_call" | custom-call | tf_op jit(solution)/shard_map/blocks/pallas_call | solution.py:231
  35.3 6.7 %collective-permute-start.8 = (s16[528,256]{1,0:T(8,128)(2,1)S(1)}, s16[528,256]{1,0:T(8,128)(2,1)S(1)}, u32[]{:S(2)}, u32[]{:S(2)}) collective-permute-start(s16[528,256]{1,0:T(8,128)(2,1)S(1)} %get-tuple-element.17), channel_id=1, source_target_pairs={{0,16},{16,0},{1,17},{17,1},{2,18},{18,2},{3,19},{19,3},{4,20},{20... | collective-permute-start | bytes 811016 | tf_op jit(solution)/shard_map/ppermute | solution.py:207
  41.9 4.5 %collective-permute-start.9 = (s16[272,256]{1,0:T(8,128)(2,1)S(1)}, s16[272,256]{1,0:T(8,128)(2,1)S(1)}, u32[]{:S(2)}, u32[]{:S(2)}) collective-permute-start(s16[272,256]{1,0:T(8,128)(2,1)S(1)} %get-tuple-element.18), channel_id=1, source_target_pairs={{0,4},{4,8},{8,12},{12,0},{1,5},{5,9},{9,13},{13,1},{2,6},{6,10},{... | collective-permute-start | bytes 417800 | tf_op jit(solution)/shard_map/ppermute | solution.py:207
  46.5 2.3 %collective-permute-start.10 = (s16[272,256]{1,0:T(8,128)(2,1)S(1)}, s16[272,256]{1,0:T(8,128)(2,1)S(1)}, u32[]{:S(2)}, u32[]{:S(2)}) collective-permute-start(s16[272,256]{1,0:T(8,128)(2,1)S(1)} %get-tuple-element.19), channel_id=1, source_target_pairs={{0,8},{4,12},{8,0},{12,4},{1,9},{5,13},{9,1},{13,5},{2,10},{6,14},... | collective-permute-start | bytes 417800 | tf_op jit(solution)/shard_map/ppermute | solution.py:207
  48.7 1.4 %collective-permute-start.11 = (s16[272,256]{1,0:T(8,128)(2,1)S(1)}, s16[272,256]{1,0:T(8,128)(2,1)S(1)}, u32[]{:S(2)}, u32[]{:S(2)}) collective-permute-start(s16[272,256]{1,0:T(8,128)(2,1)S(1)} %get-tuple-element.20), channel_id=1, source_target_pairs={{0,12},{4,0},{8,4},{12,8},{1,13},{5,1},{9,5},{13,9},{2,14},{6,2},{... | collective-permute-start | bytes 417800 | tf_op jit(solution)/shard_map/ppermute | solution.py:207
  50.1 2.6 %collective-permute-done.10.refs_4_ = s16[272,256]{1,0:T(8,128)(2,1)S(1)} collective-permute-done((s16[272,256]{1,0:T(8,128)(2,1)S(1)}, s16[272,256]{1,0:T(8,128)(2,1)S(1)}, u32[]{:S(2)}, u32[]{:S(2)}) %collective-permute-start.10) | collective-permute-done | bytes 139296 | tf_op jit(solution)/shard_map/ppermute | solution.py:207
  52.8 2.4 %collective-permute-done.11.refs_5_ = s16[272,256]{1,0:T(8,128)(2,1)S(1)} collective-permute-done((s16[272,256]{1,0:T(8,128)(2,1)S(1)}, s16[272,256]{1,0:T(8,128)(2,1)S(1)}, u32[]{:S(2)}, u32[]{:S(2)}) %collective-permute-start.11) | collective-permute-done | bytes 139296 | tf_op jit(solution)/shard_map/ppermute | solution.py:207
  56.1 1.6 %collective-permute-start.13 = (s16[176,256]{1,0:T(8,128)(2,1)S(1)}, s16[176,256]{1,0:T(8,128)(2,1)S(1)}, u32[]{:S(2)}, u32[]{:S(2)}) collective-permute-start(s16[176,256]{1,0:T(8,128)(2,1)S(1)} %get-tuple-element.24), channel_id=1, source_target_pairs={{0,2},{1,3},{2,0},{3,1},{4,6},{5,7},{6,4},{7,5},{8,10},{9,11},{10,... | collective-permute-start | bytes 270344 | tf_op jit(solution)/shard_map/ppermute | solution.py:207
  57.7 2.8 %collective-permute-start.14 = (s16[176,256]{1,0:T(8,128)(2,1)S(1)}, s16[176,256]{1,0:T(8,128)(2,1)S(1)}, u32[]{:S(2)}, u32[]{:S(2)}) collective-permute-start(s16[176,256]{1,0:T(8,128)(2,1)S(1)} %get-tuple-element.25), channel_id=1, source_target_pairs={{0,3},{1,0},{2,1},{3,2},{4,7},{5,4},{6,5},{7,6},{8,11},{9,8},{10,9... | collective-permute-start | bytes 270344 | tf_op jit(solution)/shard_map/ppermute | solution.py:207
  60.6 0.8 %collective-permute-start.15 = (s16[80,256]{1,0:T(8,128)(2,1)S(1)}, s16[80,256]{1,0:T(8,128)(2,1)S(1)}, u32[]{:S(2)}, u32[]{:S(2)}) collective-permute-start(s16[80,256]{1,0:T(8,128)(2,1)S(1)} %get-tuple-element.26), channel_id=1, source_target_pairs={{0,16},{16,0},{1,17},{17,1},{2,18},{18,2},{3,19},{19,3},{4,20},{20... | collective-permute-start | bytes 122888 | tf_op jit(solution)/shard_map/ppermute | solution.py:207
  61.3 3.2 %collective-permute-done.15.refs_5_ = s16[80,256]{1,0:T(8,128)(2,1)S(1)} collective-permute-done((s16[80,256]{1,0:T(8,128)(2,1)S(1)}, s16[80,256]{1,0:T(8,128)(2,1)S(1)}, u32[]{:S(2)}, u32[]{:S(2)}) %collective-permute-start.15) | collective-permute-done | bytes 40992 | tf_op jit(solution)/shard_map/ppermute | solution.py:207
  64.6 1.1 %collective-permute-done.13.refs_3_ = s16[176,256]{1,0:T(8,128)(2,1)S(1)} collective-permute-done((s16[176,256]{1,0:T(8,128)(2,1)S(1)}, s16[176,256]{1,0:T(8,128)(2,1)S(1)}, u32[]{:S(2)}, u32[]{:S(2)}) %collective-permute-start.13) | collective-permute-done | bytes 90144 | tf_op jit(solution)/shard_map/ppermute | solution.py:207
  (25 shorter events, 4.8 us)
Async XLA Ops:
  1.5 12.6 %collective-permute-start.2 = (bf16[160,256]{1,0:T(8,128)(2,1)S(1)}, bf16[160,256]{1,0:T(8,128)(2,1)S(1)}, u32[]{:S(2)}, u32[]{:S(2)}) collective-permute-start(bf16[160,256]{1,0:T(8,128)(2,1)S(1)} %pad_maximum_fusion.1), channel_id=1, source_target_pairs={{0,3},{1,0},{2,1},{3,2},{4,7},{5,4},{6,5},{7,6},{8,11},{9,8},{10,9... | collective-permute-start | bytes 245768 | tf_op jit(solution)/shard_map/ppermute | solution.py:207
  6.5 7.5 %collective-permute-start.1 = (bf16[160,256]{1,0:T(8,128)(2,1)S(1)}, bf16[160,256]{1,0:T(8,128)(2,1)S(1)}, u32[]{:S(2)}, u32[]{:S(2)}) collective-permute-start(bf16[160,256]{1,0:T(8,128)(2,1)S(1)} %pad_maximum_fusion.1), channel_id=1, source_target_pairs={{0,2},{1,3},{2,0},{3,1},{4,6},{5,7},{6,4},{7,5},{8,10},{9,11},{10,... | collective-permute-start | bytes 245768 | tf_op jit(solution)/shard_map/ppermute | solution.py:207
  6.5 6.2 %collective-permute-start = (bf16[160,256]{1,0:T(8,128)(2,1)S(1)}, bf16[160,256]{1,0:T(8,128)(2,1)S(1)}, u32[]{:S(2)}, u32[]{:S(2)}) collective-permute-start(bf16[160,256]{1,0:T(8,128)(2,1)S(1)} %pad_maximum_fusion.1), channel_id=1, source_target_pairs={{0,1},{1,2},{2,3},{3,0},{4,5},{5,6},{6,7},{7,4},{8,9},{9,10},{10,1... | collective-permute-start | bytes 245768 | tf_op jit(solution)/shard_map/ppermute | solution.py:207
  7.6 9.8 %collective-permute-start.4 = (bf16[64,256]{1,0:T(8,128)(2,1)}, bf16[64,256]{1,0:T(8,128)(2,1)S(1)}, u32[]{:S(2)}, u32[]{:S(2)}) collective-permute-start(bf16[64,256]{1,0:T(8,128)(2,1)} %bitcast.12), channel_id=1, source_target_pairs={{0,16},{16,0},{1,17},{17,1},{2,18},{18,2},{3,19},{19,3},{4,20},{20... | collective-permute-start | bytes 98312 | tf_op jit(solution)/shard_map/ppermute | solution.py:207
  15.7 10.2 %collective-permute-start.3 = (bf16[512,256]{1,0:T(8,128)(2,1)S(1)}, bf16[512,256]{1,0:T(8,128)(2,1)S(1)}, u32[]{:S(2)}, u32[]{:S(2)}) collective-permute-start(bf16[512,256]{1,0:T(8,128)(2,1)S(1)} %pad_maximum_fusion.refs_0_), channel_id=1, source_target_pairs={{0,16},{16,0},{1,17},{17,1},{2,18},{18,2},{3,19},{19,3},{4,20},{20... | collective-permute-start | bytes 786440 | tf_op jit(solution)/shard_map/ppermute | solution.py:207
  17.3 4.0 %collective-permute-start.7 = (bf16[256,256]{1,0:T(8,128)(2,1)S(1)}, bf16[256,256]{1,0:T(8,128)(2,1)S(1)}, u32[]{:S(2)}, u32[]{:S(2)}) collective-permute-start(bf16[256,256]{1,0:T(8,128)(2,1)S(1)} %constant_dynamic-update-slice_fusion.refs_2_), channel_id=1, source_target_pairs={{0,12},{4,0},{8,4},{12,8},{1,13},{5,1},{9,5},{13,9},{2,14},{6,2},{... | collective-permute-start | bytes 393224 | tf_op jit(solution)/shard_map/ppermute | solution.py:207
  17.8 8.1 %collective-permute-start.6 = (bf16[256,256]{1,0:T(8,128)(2,1)S(1)}, bf16[256,256]{1,0:T(8,128)(2,1)S(1)}, u32[]{:S(2)}, u32[]{:S(2)}) collective-permute-start(bf16[256,256]{1,0:T(8,128)(2,1)S(1)} %constant_dynamic-update-slice_fusion.refs_2_), channel_id=1, source_target_pairs={{0,8},{4,12},{8,0},{12,4},{1,9},{5,13},{9,1},{13,5},{2,10},{6,14},... | collective-permute-start | bytes 393224 | tf_op jit(solution)/shard_map/ppermute | solution.py:207
  18.9 7.1 %collective-permute-start.5 = (bf16[256,256]{1,0:T(8,128)(2,1)S(1)}, bf16[256,256]{1,0:T(8,128)(2,1)S(1)}, u32[]{:S(2)}, u32[]{:S(2)}) collective-permute-start(bf16[256,256]{1,0:T(8,128)(2,1)S(1)} %constant_dynamic-update-slice_fusion.refs_2_), channel_id=1, source_target_pairs={{0,4},{4,8},{8,12},{12,0},{1,5},{5,9},{9,13},{13,1},{2,6},{6,10},{... | collective-permute-start | bytes 393224 | tf_op jit(solution)/shard_map/ppermute | solution.py:207
  35.3 19.9 %collective-permute-start.8 = (s16[528,256]{1,0:T(8,128)(2,1)S(1)}, s16[528,256]{1,0:T(8,128)(2,1)S(1)}, u32[]{:S(2)}, u32[]{:S(2)}) collective-permute-start(s16[528,256]{1,0:T(8,128)(2,1)S(1)} %get-tuple-element.17), channel_id=1, source_target_pairs={{0,16},{16,0},{1,17},{17,1},{2,18},{18,2},{3,19},{19,3},{4,20},{20... | collective-permute-start | bytes 811016 | tf_op jit(solution)/shard_map/ppermute | solution.py:207
  41.9 8.2 %collective-permute-start.9 = (s16[272,256]{1,0:T(8,128)(2,1)S(1)}, s16[272,256]{1,0:T(8,128)(2,1)S(1)}, u32[]{:S(2)}, u32[]{:S(2)}) collective-permute-start(s16[272,256]{1,0:T(8,128)(2,1)S(1)} %get-tuple-element.18), channel_id=1, source_target_pairs={{0,4},{4,8},{8,12},{12,0},{1,5},{5,9},{9,13},{13,1},{2,6},{6,10},{... | collective-permute-start | bytes 417800 | tf_op jit(solution)/shard_map/ppermute | solution.py:207
  46.5 6.3 %collective-permute-start.10 = (s16[272,256]{1,0:T(8,128)(2,1)S(1)}, s16[272,256]{1,0:T(8,128)(2,1)S(1)}, u32[]{:S(2)}, u32[]{:S(2)}) collective-permute-start(s16[272,256]{1,0:T(8,128)(2,1)S(1)} %get-tuple-element.19), channel_id=1, source_target_pairs={{0,8},{4,12},{8,0},{12,4},{1,9},{5,13},{9,1},{13,5},{2,10},{6,14},... | collective-permute-start | bytes 417800 | tf_op jit(solution)/shard_map/ppermute | solution.py:207
  48.7 6.4 %collective-permute-start.11 = (s16[272,256]{1,0:T(8,128)(2,1)S(1)}, s16[272,256]{1,0:T(8,128)(2,1)S(1)}, u32[]{:S(2)}, u32[]{:S(2)}) collective-permute-start(s16[272,256]{1,0:T(8,128)(2,1)S(1)} %get-tuple-element.20), channel_id=1, source_target_pairs={{0,12},{4,0},{8,4},{12,8},{1,13},{5,1},{9,5},{13,9},{2,14},{6,2},{... | collective-permute-start | bytes 417800 | tf_op jit(solution)/shard_map/ppermute | solution.py:207
  55.5 9.1 %collective-permute-start.12 = (s16[176,256]{1,0:T(8,128)(2,1)S(1)}, s16[176,256]{1,0:T(8,128)(2,1)S(1)}, u32[]{:S(2)}, u32[]{:S(2)}) collective-permute-start(s16[176,256]{1,0:T(8,128)(2,1)S(1)} %get-tuple-element.23), channel_id=1, source_target_pairs={{0,1},{1,2},{2,3},{3,0},{4,5},{5,6},{6,7},{7,4},{8,9},{9,10},{10,1... | collective-permute-start | bytes 270344 | tf_op jit(solution)/shard_map/ppermute | solution.py:207
  56.1 9.5 %collective-permute-start.13 = (s16[176,256]{1,0:T(8,128)(2,1)S(1)}, s16[176,256]{1,0:T(8,128)(2,1)S(1)}, u32[]{:S(2)}, u32[]{:S(2)}) collective-permute-start(s16[176,256]{1,0:T(8,128)(2,1)S(1)} %get-tuple-element.24), channel_id=1, source_target_pairs={{0,2},{1,3},{2,0},{3,1},{4,6},{5,7},{6,4},{7,5},{8,10},{9,11},{10,... | collective-permute-start | bytes 270344 | tf_op jit(solution)/shard_map/ppermute | solution.py:207
  57.7 8.2 %collective-permute-start.14 = (s16[176,256]{1,0:T(8,128)(2,1)S(1)}, s16[176,256]{1,0:T(8,128)(2,1)S(1)}, u32[]{:S(2)}, u32[]{:S(2)}) collective-permute-start(s16[176,256]{1,0:T(8,128)(2,1)S(1)} %get-tuple-element.25), channel_id=1, source_target_pairs={{0,3},{1,0},{2,1},{3,2},{4,7},{5,4},{6,5},{7,6},{8,11},{9,8},{10,9... | collective-permute-start | bytes 270344 | tf_op jit(solution)/shard_map/ppermute | solution.py:207
  60.6 4.0 %collective-permute-start.15 = (s16[80,256]{1,0:T(8,128)(2,1)S(1)}, s16[80,256]{1,0:T(8,128)(2,1)S(1)}, u32[]{:S(2)}, u32[]{:S(2)}) collective-permute-start(s16[80,256]{1,0:T(8,128)(2,1)S(1)} %get-tuple-element.26), channel_id=1, source_target_pairs={{0,16},{16,0},{1,17},{17,1},{2,18},{18,2},{3,19},{19,3},{4,20},{20... | collective-permute-start | bytes 122888 | tf_op jit(solution)/shard_map/ppermute | solution.py:207

commit v4 on v3

--- a/solution.py
+++ b/solution.py
@@ -37,17 +37,25 @@
     return parts
 
 
-def add_block(slot, coords, weights, slabs, grads, held):
+def take(items, *counts):
+    runs = []
+    for count in counts:
+        runs.append(items[:count])
+        items = items[count:]
+    return runs
+
+
+def add_block(slot, places, weights, slabs, grads, held):
     slab_a, slab_b, slab_c = slabs
     grad_a, grad_b, grad_c = grads
     f32, bf16 = jnp.float32, jnp.bfloat16
-    at_a, at_b, at_c = (pl.multiple_of(coords[0, 0, 0, i, slot] * BLK, BLK) for i in range(3))
+    at_a, at_b, at_c = (pl.multiple_of(places[i] * BLK, BLK) for i in range(3))
     rows_a = slab_a[pl.ds(at_a, BLK), :].astype(f32)
     rows_b = slab_b[pl.ds(at_b, BLK), :]
     rows_c = slab_c[pl.ds(at_c, BLK), :]
     rank = rows_b.shape[1]
     wide_b = rows_b.astype(f32)
-    weight = weights[slot]
+    weight = jnp.transpose(weights[slot].astype(f32)).astype(bf16)
 
     def start(first):
         mixed = []
@@ -81,16 +89,16 @@
     grad_c[pl.ds(at_c, BLK), :] += sum_c
 
 
-def block_kernel(nx, ny, nz, filled, coords, entries, weights, *refs):
-    got_b, got_ac = refs[:nx], refs[nx : nx + ny]
-    refs = refs[nx + ny :]
+def block_kernel(nx, ny, nz, table, entries, weights, *refs):
+    along_z, along_x, rest_b, got_ac = take(refs, nz, nx, nx - 1, ny)
+    refs = refs[nz + 2 * nx - 1 + ny :]
     own_b, own_ac = refs[:2]
     send_b, send_ac = refs[2 : 1 + nx], refs[1 + nx : nx + ny]
     slab_a, slab_b, slab_c, grad_a, grad_b, grad_c, held, arrivals = refs[nx + ny :]
     x, y, z = (lax.axis_index(name) for name in ("gx", "gy", "gz"))
     all_a, all_b, all_c = (s.shape[0] for s in (slab_a, slab_b, slab_c))
     per_a, per_b, per_c = all_a // (ny * nz), all_b // (nx * nz), all_c // (nx * ny)
-    count = filled[0, 0, 0]
+    count = table[0]
 
     def copy(slot, chunk):
         rows = pl.ds(chunk * CHUNK, CHUNK)
@@ -112,14 +120,20 @@
         of_z = lax.rem(z + nz - j, nz)
         for i in range(nx):
             at = (lax.rem(x + nx - i, nx) * nz + of_z) * per_b
-            slab_b[pl.ds(pl.multiple_of(at, per_b), per_b), :] = got_b[i][j * per_b : (j + 1) * per_b, :]
+            if i == 0:
+                rows = along_z[j][:per_b, :]
+            elif j == 0:
+                rows = along_x[i][per_c:, :]
+            else:
+                rows = rest_b[i - 1][(j - 1) * per_b : j * per_b, :]
+            slab_b[pl.ds(pl.multiple_of(at, per_b), per_b), :] = rows
         for i in range(ny):
-            at = (lax.rem(y + ny - i, ny) * nz + of_z) * per_a
+            at = (before(y, i, ny) * nz + of_z) * per_a
             slab_a[pl.ds(pl.multiple_of(at, per_a), per_a), :] = got_ac[i][j * per_a : (j + 1) * per_a, :]
     for j in range(nx):
         of_x = lax.rem(x + nx - j, nx)
         for i in range(ny):
-            at = (of_x * ny + lax.rem(y + ny - i, ny)) * per_c
+            at = (of_x * ny + before(y, i, ny)) * per_c
             first = nz * per_a + j * per_c
             slab_c[pl.ds(pl.multiple_of(at, per_c), per_c), :] = got_ac[i][first : first + per_c, :]
 
@@ -129,7 +143,8 @@
         for chunk in range(BLK // CHUNK):
             copy(slot, chunk).wait()
         fetch(slot + 1)
-        add_block(slot, coords, weights, slabs, grads, held)
+        places = [table[1 + 3 * slot + i] for i in range(3)]
+        add_block(slot, places, weights, slabs, grads, held)
 
     some_b, some_a = all_b // nx, all_a // ny
     for i in range(nx):
@@ -211,6 +226,22 @@
     return [array] + [shift(array, axis, size, by) for by in range(1, size)]
 
 
+def pairwise(array, axis, size):
+    near = 2 - size % 2
+    far = [array] + [shift(array, axis, size, by) for by in range(near, size, near)]
+    if near == 1:
+        return far
+    swapped = [lax.ppermute(item, axis, [(i, i ^ 1) for i in range(size)]) for item in far]
+    return [item for pair in zip(far, swapped) for item in pair]
+
+
+def before(me, place, size):
+    near = 2 - size % 2
+    if place % near:
+        me = me + 1 - 2 * lax.rem(me, 2)
+    return lax.rem(me + size - place // near * near, size)
+
+
 def per_device(nx, ny, nz, tensor_blocks, fiber_mask, block_coords, block_counts, factor_a, factor_b, factor_c):
     per_a, per_b, per_c = (f.shape[1] for f in (factor_a, factor_b, factor_c))
     rank = factor_a.shape[2]
@@ -219,27 +250,29 @@
     slots = tensor_blocks.shape[3]
 
     along_z = around(jnp.concatenate([factor_b[0], factor_a[0]], 0), "gz", nz)
-    along_x = around(factor_c[0], "gx", nx)
-    got_b = around(jnp.concatenate([p[:per_b] for p in along_z], 0), "gx", nx)
-    got_ac = around(jnp.concatenate([p[per_b:] for p in along_z] + along_x, 0), "gy", ny)
-
-    weights = jnp.swapaxes(fiber_mask[0, 0, 0], 1, 2).astype(jnp.bfloat16)
+    weights = fiber_mask[0, 0, 0].astype(jnp.bfloat16)
+    table = jnp.concatenate([block_counts.reshape(1), jnp.swapaxes(block_coords[0, 0, 0], 0, 1).reshape(3 * slots)])
+    rows_cb = jnp.concatenate([factor_c[0], factor_b[0]], 0)
+    rows_cb, weights, table = lax.optimization_barrier((rows_cb, weights, table))
+    along_x = around(rows_cb, "gx", nx)
+    some_ac = jnp.concatenate([p[per_b:] for p in along_z] + [p[:per_c] for p in along_x], 0)
+    got_ac = pairwise(some_ac, "gy", ny)
+    rest_b = around(jnp.concatenate([p[:per_b] for p in along_z[1:]], 0), "gx", nx)[1:]
     f32, i16 = jnp.float32, jnp.int16
     outs = [jax.ShapeDtypeStruct((some_b, rank), f32), jax.ShapeDtypeStruct((some_a + some_c, rank), f32)]
     outs += [jax.ShapeDtypeStruct((some_b + PAD, rank), i16)] * (nx - 1)
     outs += [jax.ShapeDtypeStruct((some_a + some_c + PAD, rank), i16)] * (ny - 1)
     results = pl.pallas_call(
         functools.partial(block_kernel, nx, ny, nz),
-        in_specs=[pl.BlockSpec(memory_space=pltpu.SMEM)] * 2
-        + [pl.BlockSpec(memory_space=pl.ANY)]
-        + [pl.BlockSpec(memory_space=pltpu.VMEM)] * (1 + nx + ny),
+        in_specs=[pl.BlockSpec(memory_space=pltpu.SMEM), pl.BlockSpec(memory_space=pl.ANY)]
+        + [pl.BlockSpec(memory_space=pltpu.VMEM)] * (nz + 2 * nx + ny),
         scratch_shapes=[pltpu.VMEM((n, rank), jnp.bfloat16) for n in (all_a, all_b, all_c)]
         + [pltpu.VMEM((n, rank), f32) for n in (all_a, all_b, all_c)]
         + [pltpu.VMEM((slots, BLK, BLK, BLK), jnp.bfloat16), pltpu.SemaphoreType.DMA((slots, BLK // CHUNK))],
         out_shape=outs,
         compiler_params=pltpu.CompilerParams(vmem_limit_bytes=44 * 2**20),
         name="blocks",
-    )(block_counts, block_coords, tensor_blocks, weights, *got_b, *got_ac)
+    )(table, tensor_blocks, weights, *along_z, *along_x, *rest_b, *got_ac)
 
     own_b, own_ac = results[:2]
     got_b = [shift(r, "gx", nx, i + 1) for i, r in enumerate(results[2 : 1 + nx])]

time: 66.3 us -> 63.4 us (0.956); the launches traced: 66.7 us -> 62.5 us
  starting transfers between devices: 31.6 us -> 24.9 us
  Pallas kernels: 10.4 us -> 15.9 us
  waiting for transfers between devices: 18.4 us -> 16 us
  local copies, waits for them, and re-layouts: 3.24 us -> 1.6 us
  other arithmetic: 1.74 us -> 2.75 us
    ppermute x16 -> x14, starting transfers between devices: 31.6 us -> 24.9 us  [shift(): lax.ppermute(array, axis, [(i, (i + by) % size) for i in range(size)])]
    pallas_call x1, Pallas kernels: 9.27 us -> 14.8 us  [per_device(): pl.pallas_call(functools.partial(block_kernel, nx, ny, nz), in_specs=[pl....]
    unnamed x7 -> x5, local copies, waits for them, and re-layouts: 3.22 us -> 0.73 us
    ppermute x16 -> x14, waiting for transfers between devices: 18.4 us -> 16 us  [shift(): lax.ppermute(array, axis, [(i, (i + by) % size) for i in range(size)])]
    convert_element_type x1, other arithmetic: 0.02 us -> 0.94 us  [per_device(): weights = fiber_mask[0, 0, 0].astype(jnp.bfloat16)]
    transpose x0 -> x1, local copies, waits for them, and re-layouts: none -> 0.77 us  [per_device(): jnp.swapaxes(block_coords[0, 0, 0], 0, 1).reshape(3 * slots)]
  transfers between devices with their start and end apart: 16 -> 16, of which waited for: 10 -> 8; matrix products, arithmetic and copies ran while one was open for 6% -> 6% of each run, Pallas kernels for 0% -> 0%
where the time goes in v4:
time: 63.4 us; the launch traced here: 62.5 us
  starting transfers between devices  24.9 us (39%)
  waiting for transfers between devices  16 us (25%)
  Pallas kernels  15.9 us (25%)
  other arithmetic  2.75 us (4%)
  local copies, waits for them, and re-layouts  1.6 us (3%)
  between operations  1.37 us (2%)
    ppermute x14, starting transfers between devices, shift(): lax.ppermute(array, axis, [(i, (i + by) % size) for i in range(size)])  24.9 us
    ppermute x14, waiting for transfers between devices, shift(): lax.ppermute(array, axis, [(i, (i + by) % size) for i in range(size)])  16 us
    pallas_call x1, Pallas kernels, per_device(): pl.pallas_call(functools.partial(block_kernel, nx, ny, nz), in_specs=[pl....  14.8 us
  transfers between devices with their start and end apart: 16, of which 8 were waited for; matrix products, arithmetic and copies ran while one was open for 6% of the time, Pallas kernels for 0%

profile of v4, /device:TPU:0, one launch (start us, length us, event | category | flops | bytes accessed | tf_op | source)
XLA Modules:
  0.0 62.5 jit_solution(16459948860222536619)
XLA Ops:
  0.6 0.9 %pad_maximum_fusion.2.refs_0_ = bf16[160,256]{1,0:T(8,128)(2,1)S(1)} fusion(bf16[32,256]{1,0:T(8,128)(2,1)} %bitcast.14, bf16[128,256]{1,0:T(8,128)(2,1)} %bitcast.12), kind=kLoop, calls=%fused_computation.3 | loop fusion | flops 163840 | bytes 163840 | tf_op jit(solution)/shard_map/concatenate | solution.py:252
  1.5 5.0 %collective-permute-start.2 = (bf16[160,256]{1,0:T(8,128)(2,1)S(1)}, bf16[160,256]{1,0:T(8,128)(2,1)S(1)}, u32[]{:S(2)}, u32[]{:S(2)}) collective-permute-start(bf16[160,256]{1,0:T(8,128)(2,1)S(1)} %pad_maximum_fusion.2.refs_0_), channel_id=1, source_target_pairs={{0,3},{1,0},{2,1},{3,2},{4,7},{5,4},{6,5},{7,6},{8,11},{9,8},{10,9... | collective-permute-start | bytes 245768 | tf_op jit(solution)/shard_map/ppermute | solution.py:222
  6.5 1.0 %collective-permute-start = (bf16[160,256]{1,0:T(8,128)(2,1)S(1)}, bf16[160,256]{1,0:T(8,128)(2,1)S(1)}, u32[]{:S(2)}, u32[]{:S(2)}) collective-permute-start(bf16[160,256]{1,0:T(8,128)(2,1)S(1)} %pad_maximum_fusion.2.refs_0_), channel_id=1, source_target_pairs={{0,1},{1,2},{2,3},{3,0},{4,5},{5,6},{6,7},{7,4},{8,9},{9,10},{10,1... | collective-permute-start | bytes 245768 | tf_op jit(solution)/shard_map/ppermute | solution.py:222
  8.2 0.8 %copy.12 = s32[1,1,1,3,3]{3,4,0,1,2:T(4,128)S(1)} copy(s32[1,1,1,3,3]{4,2,3,1,0:T(1,128)} %param.9) | data formatting | bytes 72 | tf_op jit(solution)/shard_map/transpose | solution.py:254
  9.1 0.9 %convert_bitcast_fusion.weights = bf16[3,128,128]{2,1,0:T(8,128)(2,1)S(1)} fusion(s32[1,1,1,3,128,128]{5,4,3,2,1,0:T(8,128)} %param.8), kind=kLoop, calls=%fused_computation.2 | loop fusion | flops 49152 | bytes 294912 | tf_op jit(solution)/shard_map/convert_element_type | solution.py:253
  10.0 0.9 %pad_maximum_fusion.1.refs_4_ = bf16[192,256]{1,0:T(8,128)(2,1)S(1)} fusion(bf16[128,256]{1,0:T(8,128)(2,1)} %bitcast.13, bf16[64,256]{1,0:T(8,128)(2,1)} %bitcast.15), kind=kLoop, calls=%fused_computation.1 | loop fusion | flops 196608 | bytes 196608 | tf_op jit(solution)/shard_map/concatenate | solution.py:255
  10.9 1.5 %collective-permute-start.3 = (bf16[192,256]{1,0:T(8,128)(2,1)S(1)}, bf16[192,256]{1,0:T(8,128)(2,1)S(1)}, u32[]{:S(2)}, u32[]{:S(2)}) collective-permute-start(bf16[192,256]{1,0:T(8,128)(2,1)S(1)} %pad_maximum_fusion.1.refs_4_), channel_id=1, source_target_pairs={{0,16},{16,0},{1,17},{17,1},{2,18},{18,2},{3,19},{19,3},{4,20},{20... | collective-permute-start | bytes 294920 | tf_op jit(solution)/shard_map/ppermute | solution.py:222
  13.2 0.9 %collective-permute-done.1.refs_2_ = bf16[160,256]{1,0:T(8,128)(2,1)S(1)} collective-permute-done((bf16[160,256]{1,0:T(8,128)(2,1)S(1)}, bf16[160,256]{1,0:T(8,128)(2,1)S(1)}, u32[]{:S(2)}, u32[]{:S(2)}) %collective-permute-start.1) | collective-permute-done | bytes 81952 | tf_op jit(solution)/shard_map/ppermute | solution.py:222
  14.1 1.4 %collective-permute-done.3.refs_5_ = bf16[192,256]{1,0:T(8,128)(2,1)S(1)} collective-permute-done((bf16[192,256]{1,0:T(8,128)(2,1)S(1)}, bf16[192,256]{1,0:T(8,128)(2,1)S(1)}, u32[]{:S(2)}, u32[]{:S(2)}) %collective-permute-start.3) | collective-permute-done | bytes 98336 | tf_op jit(solution)/shard_map/ppermute | solution.py:222
  15.6 1.5 %collective-permute-start.6 = (bf16[256,256]{1,0:T(8,128)(2,1)S(1)}, bf16[256,256]{1,0:T(8,128)(2,1)S(1)}, u32[]{:S(2)}, u32[]{:S(2)}) collective-permute-start(bf16[256,256]{1,0:T(8,128)(2,1)S(1)} %slice_dynamic-update-slice_fusion.refs_7_), channel_id=1, source_target_pairs={{0,8},{4,12},{8,0},{12,4},{1,9},{5,13},{9,1},{13,5},{2,10},{6,14},... | collective-permute-start | bytes 393224 | tf_op jit(solution)/shard_map/ppermute | solution.py:222
  17.1 1.6 %collective-permute-start.4 = (bf16[384,256]{1,0:T(8,128)(2,1)S(1)}, bf16[384,256]{1,0:T(8,128)(2,1)S(1)}, u32[]{:S(2)}, u32[]{:S(2)}) collective-permute-start(bf16[384,256]{1,0:T(8,128)(2,1)S(1)} %pad_maximum_fusion), channel_id=1, source_target_pairs={{0,16},{16,0},{1,17},{17,1},{2,18},{18,2},{3,19},{19,3},{4,20},{20... | collective-permute-start | bytes 589832 | tf_op jit(solution)/shard_map/ppermute | solution.py:222
  18.7 1.9 %collective-permute-done.6.refs_9_ = bf16[256,256]{1,0:T(8,128)(2,1)S(1)} collective-permute-done((bf16[256,256]{1,0:T(8,128)(2,1)S(1)}, bf16[256,256]{1,0:T(8,128)(2,1)S(1)}, u32[]{:S(2)}, u32[]{:S(2)}) %collective-permute-start.6) | collective-permute-done | bytes 131104 | tf_op jit(solution)/shard_map/ppermute | solution.py:222
  20.5 2.3 %collective-permute-done.4.refs_6_ = bf16[384,256]{1,0:T(8,128)(2,1)S(1)} collective-permute-done((bf16[384,256]{1,0:T(8,128)(2,1)S(1)}, bf16[384,256]{1,0:T(8,128)(2,1)S(1)}, u32[]{:S(2)}, u32[]{:S(2)}) %collective-permute-start.4) | collective-permute-done | bytes 196640 | tf_op jit(solution)/shard_map/ppermute | solution.py:222
  22.8 14.8 %blocks.1 = (f32[512,256]{1,0:T(8,128)S(1)}, f32[256,256]{1,0:T(8,128)S(1)}, s16[528,256]{1,0:T(8,128)(2,1)S(1)}, s16[272,256]{1,0:T(8,128)(2,1)S(1)}, s16[272,2...) custom-call(s32[10]{0:T(128)S(1)} %pad_add_fusion.table, bf16[1,1,1,3,128,128,128]{6,5,4,3,2,1,0:T(8,128)(2,1)} %entries.1, ...), custom_call_target="tpu_custom_call" | custom-call | tf_op jit(solution)/shard_map/blocks/pallas_call | solution.py:265
  37.7 6.2 %collective-permute-start.9 = (s16[272,256]{1,0:T(8,128)(2,1)S(1)}, s16[272,256]{1,0:T(8,128)(2,1)S(1)}, u32[]{:S(2)}, u32[]{:S(2)}) collective-permute-start(s16[272,256]{1,0:T(8,128)(2,1)S(1)} %get-tuple-element.24), channel_id=1, source_target_pairs={{0,4},{4,8},{8,12},{12,0},{1,5},{5,9},{9,13},{13,1},{2,6},{6,10},{... | collective-permute-start | bytes 417800 | tf_op jit(solution)/shard_map/ppermute | solution.py:222
  43.9 1.7 %collective-permute-start.10 = (s16[272,256]{1,0:T(8,128)(2,1)S(1)}, s16[272,256]{1,0:T(8,128)(2,1)S(1)}, u32[]{:S(2)}, u32[]{:S(2)}) collective-permute-start(s16[272,256]{1,0:T(8,128)(2,1)S(1)} %get-tuple-element.25), channel_id=1, source_target_pairs={{0,8},{4,12},{8,0},{12,4},{1,9},{5,13},{9,1},{13,5},{2,10},{6,14},... | collective-permute-start | bytes 417800 | tf_op jit(solution)/shard_map/ppermute | solution.py:222
  45.5 1.4 %collective-permute-start.11 = (s16[272,256]{1,0:T(8,128)(2,1)S(1)}, s16[272,256]{1,0:T(8,128)(2,1)S(1)}, u32[]{:S(2)}, u32[]{:S(2)}) collective-permute-start(s16[272,256]{1,0:T(8,128)(2,1)S(1)} %get-tuple-element.26), channel_id=1, source_target_pairs={{0,12},{4,0},{8,4},{12,8},{1,13},{5,1},{9,5},{13,9},{2,14},{6,2},{... | collective-permute-start | bytes 417800 | tf_op jit(solution)/shard_map/ppermute | solution.py:222
  47.0 2.7 %collective-permute-done.10.refs_4_ = s16[272,256]{1,0:T(8,128)(2,1)S(1)} collective-permute-done((s16[272,256]{1,0:T(8,128)(2,1)S(1)}, s16[272,256]{1,0:T(8,128)(2,1)S(1)}, u32[]{:S(2)}, u32[]{:S(2)}) %collective-permute-start.10) | collective-permute-done | bytes 139296 | tf_op jit(solution)/shard_map/ppermute | solution.py:222
  49.7 2.3 %collective-permute-done.11.refs_5_ = s16[272,256]{1,0:T(8,128)(2,1)S(1)} collective-permute-done((s16[272,256]{1,0:T(8,128)(2,1)S(1)}, s16[272,256]{1,0:T(8,128)(2,1)S(1)}, u32[]{:S(2)}, u32[]{:S(2)}) %collective-permute-start.11) | collective-permute-done | bytes 139296 | tf_op jit(solution)/shard_map/ppermute | solution.py:222
  52.4 2.9 %collective-permute-start.13 = (s16[176,256]{1,0:T(8,128)(2,1)S(1)}, s16[176,256]{1,0:T(8,128)(2,1)S(1)}, u32[]{:S(2)}, u32[]{:S(2)}) collective-permute-start(s16[176,256]{1,0:T(8,128)(2,1)S(1)} %get-tuple-element.30), channel_id=1, source_target_pairs={{0,2},{1,3},{2,0},{3,1},{4,6},{5,7},{6,4},{7,5},{8,10},{9,11},{10,... | collective-permute-start | bytes 270344 | tf_op jit(solution)/shard_map/ppermute | solution.py:222
  55.3 0.9 %collective-permute-start.14 = (s16[176,256]{1,0:T(8,128)(2,1)S(1)}, s16[176,256]{1,0:T(8,128)(2,1)S(1)}, u32[]{:S(2)}, u32[]{:S(2)}) collective-permute-start(s16[176,256]{1,0:T(8,128)(2,1)S(1)} %get-tuple-element.31), channel_id=1, source_target_pairs={{0,3},{1,0},{2,1},{3,2},{4,7},{5,4},{6,5},{7,6},{8,11},{9,8},{10,9... | collective-permute-start | bytes 270344 | tf_op jit(solution)/shard_map/ppermute | solution.py:222
  56.2 1.0 %collective-permute-start.15 = (s16[80,256]{1,0:T(8,128)(2,1)S(1)}, s16[80,256]{1,0:T(8,128)(2,1)S(1)}, u32[]{:S(2)}, u32[]{:S(2)}) collective-permute-start(s16[80,256]{1,0:T(8,128)(2,1)S(1)} %get-tuple-element.32), channel_id=1, source_target_pairs={{0,16},{16,0},{1,17},{17,1},{2,18},{18,2},{3,19},{19,3},{4,20},{20... | collective-permute-start | bytes 122888 | tf_op jit(solution)/shard_map/ppermute | solution.py:222
  57.3 3.2 %collective-permute-done.15.refs_5_ = s16[80,256]{1,0:T(8,128)(2,1)S(1)} collective-permute-done((s16[80,256]{1,0:T(8,128)(2,1)S(1)}, s16[80,256]{1,0:T(8,128)(2,1)S(1)}, u32[]{:S(2)}, u32[]{:S(2)}) %collective-permute-start.15) | collective-permute-done | bytes 40992 | tf_op jit(solution)/shard_map/ppermute | solution.py:222
  60.5 1.3 %collective-permute-done.13.refs_3_ = s16[176,256]{1,0:T(8,128)(2,1)S(1)} collective-permute-done((s16[176,256]{1,0:T(8,128)(2,1)S(1)}, s16[176,256]{1,0:T(8,128)(2,1)S(1)}, u32[]{:S(2)}, u32[]{:S(2)}) %collective-permute-start.13) | collective-permute-done | bytes 90144 | tf_op jit(solution)/shard_map/ppermute | solution.py:222
  (27 shorter events, 2.2 us)
Async XLA Ops:
  1.5 12.6 %collective-permute-start.2 = (bf16[160,256]{1,0:T(8,128)(2,1)S(1)}, bf16[160,256]{1,0:T(8,128)(2,1)S(1)}, u32[]{:S(2)}, u32[]{:S(2)}) collective-permute-start(bf16[160,256]{1,0:T(8,128)(2,1)S(1)} %pad_maximum_fusion.2.refs_0_), channel_id=1, source_target_pairs={{0,3},{1,0},{2,1},{3,2},{4,7},{5,4},{6,5},{7,6},{8,11},{9,8},{10,9... | collective-permute-start | bytes 245768 | tf_op jit(solution)/shard_map/ppermute | solution.py:222
  6.5 7.5 %collective-permute-start.1 = (bf16[160,256]{1,0:T(8,128)(2,1)S(1)}, bf16[160,256]{1,0:T(8,128)(2,1)S(1)}, u32[]{:S(2)}, u32[]{:S(2)}) collective-permute-start(bf16[160,256]{1,0:T(8,128)(2,1)S(1)} %pad_maximum_fusion.2.refs_0_), channel_id=1, source_target_pairs={{0,2},{1,3},{2,0},{3,1},{4,6},{5,7},{6,4},{7,5},{8,10},{9,11},{10,... | collective-permute-start | bytes 245768 | tf_op jit(solution)/shard_map/ppermute | solution.py:222
  6.5 6.6 %collective-permute-start = (bf16[160,256]{1,0:T(8,128)(2,1)S(1)}, bf16[160,256]{1,0:T(8,128)(2,1)S(1)}, u32[]{:S(2)}, u32[]{:S(2)}) collective-permute-start(bf16[160,256]{1,0:T(8,128)(2,1)S(1)} %pad_maximum_fusion.2.refs_0_), channel_id=1, source_target_pairs={{0,1},{1,2},{2,3},{3,0},{4,5},{5,6},{6,7},{7,4},{8,9},{9,10},{10,1... | collective-permute-start | bytes 245768 | tf_op jit(solution)/shard_map/ppermute | solution.py:222
  10.9 4.6 %collective-permute-start.3 = (bf16[192,256]{1,0:T(8,128)(2,1)S(1)}, bf16[192,256]{1,0:T(8,128)(2,1)S(1)}, u32[]{:S(2)}, u32[]{:S(2)}) collective-permute-start(bf16[192,256]{1,0:T(8,128)(2,1)S(1)} %pad_maximum_fusion.1.refs_4_), channel_id=1, source_target_pairs={{0,16},{16,0},{1,17},{17,1},{2,18},{18,2},{3,19},{19,3},{4,20},{20... | collective-permute-start | bytes 294920 | tf_op jit(solution)/shard_map/ppermute | solution.py:222
  15.6 5.0 %collective-permute-start.6 = (bf16[256,256]{1,0:T(8,128)(2,1)S(1)}, bf16[256,256]{1,0:T(8,128)(2,1)S(1)}, u32[]{:S(2)}, u32[]{:S(2)}) collective-permute-start(bf16[256,256]{1,0:T(8,128)(2,1)S(1)} %slice_dynamic-update-slice_fusion.refs_7_), channel_id=1, source_target_pairs={{0,8},{4,12},{8,0},{12,4},{1,9},{5,13},{9,1},{13,5},{2,10},{6,14},... | collective-permute-start | bytes 393224 | tf_op jit(solution)/shard_map/ppermute | solution.py:222
  17.1 5.7 %collective-permute-start.4 = (bf16[384,256]{1,0:T(8,128)(2,1)S(1)}, bf16[384,256]{1,0:T(8,128)(2,1)S(1)}, u32[]{:S(2)}, u32[]{:S(2)}) collective-permute-start(bf16[384,256]{1,0:T(8,128)(2,1)S(1)} %pad_maximum_fusion), channel_id=1, source_target_pairs={{0,16},{16,0},{1,17},{17,1},{2,18},{18,2},{3,19},{19,3},{4,20},{20... | collective-permute-start | bytes 589832 | tf_op jit(solution)/shard_map/ppermute | solution.py:222
  18.7 1.9 %collective-permute-start.5 = (bf16[256,256]{1,0:T(8,128)(2,1)S(1)}, bf16[256,256]{1,0:T(8,128)(2,1)S(1)}, u32[]{:S(2)}, u32[]{:S(2)}) collective-permute-start(bf16[256,256]{1,0:T(8,128)(2,1)S(1)} %slice_dynamic-update-slice_fusion.refs_7_), channel_id=1, source_target_pairs={{0,4},{4,0},{8,12},{12,8},{1,5},{5,1},{9,13},{13,9},{2,6},{6,2},{1... | collective-permute-start | bytes 393224 | tf_op jit(solution)/shard_map/ppermute | solution.py:234
  20.5 2.3 %collective-permute-start.7 = (bf16[256,256]{1,0:T(8,128)(2,1)S(1)}, bf16[256,256]{1,0:T(8,128)(2,1)S(1)}, u32[]{:S(2)}, u32[]{:S(2)}) collective-permute-start(bf16[256,256]{1,0:T(8,128)(2,1)S(1)} %collective-permute-done.6.refs_9_), channel_id=1, source_target_pairs={{0,4},{4,0},{8,12},{12,8},{1,5},{5,1},{9,13},{13,9},{2,6},{6,2},{1... | collective-permute-start | bytes 393224 | tf_op jit(solution)/shard_map/ppermute | solution.py:234
  37.6 14.4 %collective-permute-start.8 = (s16[528,256]{1,0:T(8,128)(2,1)S(1)}, s16[528,256]{1,0:T(8,128)(2,1)S(1)}, u32[]{:S(2)}, u32[]{:S(2)}) collective-permute-start(s16[528,256]{1,0:T(8,128)(2,1)S(1)} %get-tuple-element.23), channel_id=1, source_target_pairs={{0,16},{16,0},{1,17},{17,1},{2,18},{18,2},{3,19},{19,3},{4,20},{20... | collective-permute-start | bytes 811016 | tf_op jit(solution)/shard_map/ppermute | solution.py:222
  37.7 9.3 %collective-permute-start.9 = (s16[272,256]{1,0:T(8,128)(2,1)S(1)}, s16[272,256]{1,0:T(8,128)(2,1)S(1)}, u32[]{:S(2)}, u32[]{:S(2)}) collective-permute-start(s16[272,256]{1,0:T(8,128)(2,1)S(1)} %get-tuple-element.24), channel_id=1, source_target_pairs={{0,4},{4,8},{8,12},{12,0},{1,5},{5,9},{9,13},{13,1},{2,6},{6,10},{... | collective-permute-start | bytes 417800 | tf_op jit(solution)/shard_map/ppermute | solution.py:222
  43.9 5.8 %collective-permute-start.10 = (s16[272,256]{1,0:T(8,128)(2,1)S(1)}, s16[272,256]{1,0:T(8,128)(2,1)S(1)}, u32[]{:S(2)}, u32[]{:S(2)}) collective-permute-start(s16[272,256]{1,0:T(8,128)(2,1)S(1)} %get-tuple-element.25), channel_id=1, source_target_pairs={{0,8},{4,12},{8,0},{12,4},{1,9},{5,13},{9,1},{13,5},{2,10},{6,14},... | collective-permute-start | bytes 417800 | tf_op jit(solution)/shard_map/ppermute | solution.py:222
  45.5 6.4 %collective-permute-start.11 = (s16[272,256]{1,0:T(8,128)(2,1)S(1)}, s16[272,256]{1,0:T(8,128)(2,1)S(1)}, u32[]{:S(2)}, u32[]{:S(2)}) collective-permute-start(s16[272,256]{1,0:T(8,128)(2,1)S(1)} %get-tuple-element.26), channel_id=1, source_target_pairs={{0,12},{4,0},{8,4},{12,8},{1,13},{5,1},{9,5},{13,9},{2,14},{6,2},{... | collective-permute-start | bytes 417800 | tf_op jit(solution)/shard_map/ppermute | solution.py:222
  52.4 8.1 %collective-permute-start.12 = (s16[176,256]{1,0:T(8,128)(2,1)S(1)}, s16[176,256]{1,0:T(8,128)(2,1)S(1)}, u32[]{:S(2)}, u32[]{:S(2)}) collective-permute-start(s16[176,256]{1,0:T(8,128)(2,1)S(1)} %get-tuple-element.29), channel_id=1, source_target_pairs={{0,1},{1,2},{2,3},{3,0},{4,5},{5,6},{6,7},{7,4},{8,9},{9,10},{10,1... | collective-permute-start | bytes 270344 | tf_op jit(solution)/shard_map/ppermute | solution.py:222
  52.4 9.4 %collective-permute-start.13 = (s16[176,256]{1,0:T(8,128)(2,1)S(1)}, s16[176,256]{1,0:T(8,128)(2,1)S(1)}, u32[]{:S(2)}, u32[]{:S(2)}) collective-permute-start(s16[176,256]{1,0:T(8,128)(2,1)S(1)} %get-tuple-element.30), channel_id=1, source_target_pairs={{0,2},{1,3},{2,0},{3,1},{4,6},{5,7},{6,4},{7,5},{8,10},{9,11},{10,... | collective-permute-start | bytes 270344 | tf_op jit(solution)/shard_map/ppermute | solution.py:222
  55.3 6.5 %collective-permute-start.14 = (s16[176,256]{1,0:T(8,128)(2,1)S(1)}, s16[176,256]{1,0:T(8,128)(2,1)S(1)}, u32[]{:S(2)}, u32[]{:S(2)}) collective-permute-start(s16[176,256]{1,0:T(8,128)(2,1)S(1)} %get-tuple-element.31), channel_id=1, source_target_pairs={{0,3},{1,0},{2,1},{3,2},{4,7},{5,4},{6,5},{7,6},{8,11},{9,8},{10,9... | collective-permute-start | bytes 270344 | tf_op jit(solution)/shard_map/ppermute | solution.py:222
  56.2 4.2 %collective-permute-start.15 = (s16[80,256]{1,0:T(8,128)(2,1)S(1)}, s16[80,256]{1,0:T(8,128)(2,1)S(1)}, u32[]{:S(2)}, u32[]{:S(2)}) collective-permute-start(s16[80,256]{1,0:T(8,128)(2,1)S(1)} %get-tuple-element.32), channel_id=1, source_target_pairs={{0,16},{16,0},{1,17},{17,1},{2,18},{18,2},{3,19},{19,3},{4,20},{20... | collective-permute-start | bytes 122888 | tf_op jit(solution)/shard_map/ppermute | solution.py:222

commit v5 on v4

--- a/solution.py
+++ b/solution.py
@@ -252,9 +252,8 @@
     along_z = around(jnp.concatenate([factor_b[0], factor_a[0]], 0), "gz", nz)
     weights = fiber_mask[0, 0, 0].astype(jnp.bfloat16)
     table = jnp.concatenate([block_counts.reshape(1), jnp.swapaxes(block_coords[0, 0, 0], 0, 1).reshape(3 * slots)])
-    rows_cb = jnp.concatenate([factor_c[0], factor_b[0]], 0)
-    rows_cb, weights, table = lax.optimization_barrier((rows_cb, weights, table))
-    along_x = around(rows_cb, "gx", nx)
+    along_x = around(jnp.concatenate([factor_c[0], factor_b[0]], 0), "gx", nx)
+    *along_z, weights, table = lax.optimization_barrier((*along_z, weights, table))
     some_ac = jnp.concatenate([p[per_b:] for p in along_z] + [p[:per_c] for p in along_x], 0)
     got_ac = pairwise(some_ac, "gy", ny)
     rest_b = around(jnp.concatenate([p[:per_b] for p in along_z[1:]], 0), "gx", nx)[1:]

time: 63.4 us -> 62.7 us (0.989)
  the two profiles are of different devices: /device:TPU:0 before, /device:TPU:1 now
where the time goes in v5:
time: 62.7 us; the launch traced here: 62 us
  starting transfers between devices  31.7 us (51%)
  waiting for transfers between devices  14.4 us (23%)
  Pallas kernels  10.1 us (16%)
  other arithmetic  2.75 us (4%)
  local copies, waits for them, and re-layouts  1.65 us (3%)
  between operations  1.38 us (2%)
    ppermute x14, starting transfers between devices, shift(): lax.ppermute(array, axis, [(i, (i + by) % size) for i in range(size)])  28.7 us
    ppermute x14, waiting for transfers between devices, shift(): lax.ppermute(array, axis, [(i, (i + by) % size) for i in range(size)])  14.1 us
    pallas_call x1, Pallas kernels, per_device(): pl.pallas_call(functools.partial(block_kernel, nx, ny, nz), in_specs=[pl....  9.02 us
    ppermute x2, starting transfers between devices, pairwise(): lax.ppermute(item, axis, [(i, i ^ 1) for i in range(size)])  3.06 us
  transfers between devices with their start and end apart: 16, of which 8 were waited for; matrix products, arithmetic and copies ran while one was open for 6% of the time, Pallas kernels for 0%

profile of v5, /device:TPU:1, one launch (start us, length us, event | category | flops | bytes accessed | tf_op | source)
XLA Modules:
  0.0 62.0 jit_solution(13747076698584126663)
XLA Ops:
  0.6 0.9 %pad_maximum_fusion.2.refs_0_ = bf16[160,256]{1,0:T(8,128)(2,1)S(1)} fusion(bf16[32,256]{1,0:T(8,128)(2,1)} %bitcast.15, bf16[128,256]{1,0:T(8,128)(2,1)} %bitcast.12), kind=kLoop, calls=%fused_computation.3 | loop fusion | flops 163840 | bytes 163840 | tf_op jit(solution)/shard_map/concatenate | solution.py:252
  1.5 4.2 %collective-permute-start.2 = (bf16[160,256]{1,0:T(8,128)(2,1)S(1)}, bf16[160,256]{1,0:T(8,128)(2,1)S(1)}, u32[]{:S(2)}, u32[]{:S(2)}) collective-permute-start(bf16[160,256]{1,0:T(8,128)(2,1)S(1)} %pad_maximum_fusion.2.refs_0_), channel_id=1, source_target_pairs={{0,3},{1,0},{2,1},{3,2},{4,7},{5,4},{6,5},{7,6},{8,11},{9,8},{10,9... | collective-permute-start | bytes 245768 | tf_op jit(solution)/shard_map/ppermute | solution.py:222
  6.1 0.8 %pad_maximum_fusion.1.refs_4_ = bf16[192,256]{1,0:T(8,128)(2,1)S(1)} fusion(bf16[128,256]{1,0:T(8,128)(2,1)} %bitcast.13, bf16[64,256]{1,0:T(8,128)(2,1)} %bitcast.14), kind=kLoop, calls=%fused_computation.1 | loop fusion | flops 196608 | bytes 196608 | tf_op jit(solution)/shard_map/concatenate | solution.py:255
  6.9 1.3 %collective-permute-start.3 = (bf16[192,256]{1,0:T(8,128)(2,1)S(1)}, bf16[192,256]{1,0:T(8,128)(2,1)S(1)}, u32[]{:S(2)}, u32[]{:S(2)}) collective-permute-start(bf16[192,256]{1,0:T(8,128)(2,1)S(1)} %pad_maximum_fusion.1.refs_4_), channel_id=1, source_target_pairs={{0,16},{16,0},{1,17},{17,1},{2,18},{18,2},{3,19},{19,3},{4,20},{20... | collective-permute-start | bytes 294920 | tf_op jit(solution)/shard_map/ppermute | solution.py:222
  8.9 0.8 %copy.12 = s32[1,1,1,3,3]{3,4,0,1,2:T(4,128)S(1)} copy(s32[1,1,1,3,3]{4,2,3,1,0:T(1,128)} %param.9) | data formatting | bytes 72 | tf_op jit(solution)/shard_map/transpose | solution.py:254
  9.8 0.9 %convert_bitcast_fusion.weights = bf16[3,128,128]{2,1,0:T(8,128)(2,1)S(1)} fusion(s32[1,1,1,3,128,128]{5,4,3,2,1,0:T(8,128)} %param.8), kind=kLoop, calls=%fused_computation.2 | loop fusion | flops 49152 | bytes 294912 | tf_op jit(solution)/shard_map/convert_element_type | solution.py:253
  10.8 2.5 %collective-permute-done.1.refs_2_ = bf16[160,256]{1,0:T(8,128)(2,1)S(1)} collective-permute-done((bf16[160,256]{1,0:T(8,128)(2,1)S(1)}, bf16[160,256]{1,0:T(8,128)(2,1)S(1)}, u32[]{:S(2)}, u32[]{:S(2)}) %collective-permute-start.1) | collective-permute-done | bytes 81952 | tf_op jit(solution)/shard_map/ppermute | solution.py:222
  13.3 0.8 %constant_dynamic-update-slice_fusion = bf16[256,256]{1,0:T(8,128)(2,1)S(1)} fusion(bf16[256,256]{1,0:T(8,128)(2,1)S(1)} %slice_dynamic-update-slice_fusion.1, bf16[1,64,256]{2,1,0:T(8,128)(2,1)} %param.13), kind=kLoop, calls=%fused_computation.9 | loop fusion | bytes 65536
  14.2 1.3 %collective-permute-start.6 = (bf16[256,256]{1,0:T(8,128)(2,1)S(1)}, bf16[256,256]{1,0:T(8,128)(2,1)S(1)}, u32[]{:S(2)}, u32[]{:S(2)}) collective-permute-start(bf16[256,256]{1,0:T(8,128)(2,1)S(1)} %slice_dynamic-update-slice_fusion.refs_7_), channel_id=1, source_target_pairs={{0,8},{4,12},{8,0},{12,4},{1,9},{5,13},{9,1},{13,5},{2,10},{6,14},... | collective-permute-start | bytes 393224 | tf_op jit(solution)/shard_map/ppermute | solution.py:222
  15.5 1.3 %collective-permute-start.4 = (bf16[384,256]{1,0:T(8,128)(2,1)S(1)}, bf16[384,256]{1,0:T(8,128)(2,1)S(1)}, u32[]{:S(2)}, u32[]{:S(2)}) collective-permute-start(bf16[384,256]{1,0:T(8,128)(2,1)S(1)} %pad_maximum_fusion), channel_id=1, source_target_pairs={{0,16},{16,0},{1,17},{17,1},{2,18},{18,2},{3,19},{19,3},{4,20},{20... | collective-permute-start | bytes 589832 | tf_op jit(solution)/shard_map/ppermute | solution.py:222
  16.8 1.4 %collective-permute-start.5 = (bf16[256,256]{1,0:T(8,128)(2,1)S(1)}, bf16[256,256]{1,0:T(8,128)(2,1)S(1)}, u32[]{:S(2)}, u32[]{:S(2)}) collective-permute-start(bf16[256,256]{1,0:T(8,128)(2,1)S(1)} %slice_dynamic-update-slice_fusion.refs_7_), channel_id=1, source_target_pairs={{0,4},{4,0},{8,12},{12,8},{1,5},{5,1},{9,13},{13,9},{2,6},{6,2},{1... | collective-permute-start | bytes 393224 | tf_op jit(solution)/shard_map/ppermute | solution.py:234
  18.4 1.7 %collective-permute-start.7 = (bf16[256,256]{1,0:T(8,128)(2,1)S(1)}, bf16[256,256]{1,0:T(8,128)(2,1)S(1)}, u32[]{:S(2)}, u32[]{:S(2)}) collective-permute-start(bf16[256,256]{1,0:T(8,128)(2,1)S(1)} %collective-permute-done.6.refs_9_), channel_id=1, source_target_pairs={{0,4},{4,0},{8,12},{12,8},{1,5},{5,1},{9,13},{13,9},{2,6},{6,2},{1... | collective-permute-start | bytes 393224 | tf_op jit(solution)/shard_map/ppermute | solution.py:234
  20.1 0.7 %collective-permute-done.4.refs_6_ = bf16[384,256]{1,0:T(8,128)(2,1)S(1)} collective-permute-done((bf16[384,256]{1,0:T(8,128)(2,1)S(1)}, bf16[384,256]{1,0:T(8,128)(2,1)S(1)}, u32[]{:S(2)}, u32[]{:S(2)}) %collective-permute-start.4) | collective-permute-done | bytes 196640 | tf_op jit(solution)/shard_map/ppermute | solution.py:222
  21.1 9.0 %blocks.1 = (f32[512,256]{1,0:T(8,128)S(1)}, f32[256,256]{1,0:T(8,128)S(1)}, s16[528,256]{1,0:T(8,128)(2,1)S(1)}, s16[272,256]{1,0:T(8,128)(2,1)S(1)}, s16[272,2...) custom-call(s32[10]{0:T(128)S(1)} %pad_add_fusion.table, bf16[1,1,1,3,128,128,128]{6,5,4,3,2,1,0:T(8,128)(2,1)} %entries.1, ...), custom_call_target="tpu_custom_call" | custom-call | tf_op jit(solution)/shard_map/blocks/pallas_call | solution.py:264
  30.2 7.1 %collective-permute-start.8 = (s16[528,256]{1,0:T(8,128)(2,1)S(1)}, s16[528,256]{1,0:T(8,128)(2,1)S(1)}, u32[]{:S(2)}, u32[]{:S(2)}) collective-permute-start(s16[528,256]{1,0:T(8,128)(2,1)S(1)} %get-tuple-element.29), channel_id=1, source_target_pairs={{0,16},{16,0},{1,17},{17,1},{2,18},{18,2},{3,19},{19,3},{4,20},{20... | collective-permute-start | bytes 811016 | tf_op jit(solution)/shard_map/ppermute | solution.py:222
  37.2 7.6 %collective-permute-start.10 = (s16[272,256]{1,0:T(8,128)(2,1)S(1)}, s16[272,256]{1,0:T(8,128)(2,1)S(1)}, u32[]{:S(2)}, u32[]{:S(2)}) collective-permute-start(s16[272,256]{1,0:T(8,128)(2,1)S(1)} %get-tuple-element.31), channel_id=1, source_target_pairs={{0,8},{4,12},{8,0},{12,4},{1,9},{5,13},{9,1},{13,5},{2,10},{6,14},... | collective-permute-start | bytes 417800 | tf_op jit(solution)/shard_map/ppermute | solution.py:222
  45.0 6.2 %collective-permute-done.10.refs_4_ = s16[272,256]{1,0:T(8,128)(2,1)S(1)} collective-permute-done((s16[272,256]{1,0:T(8,128)(2,1)S(1)}, s16[272,256]{1,0:T(8,128)(2,1)S(1)}, u32[]{:S(2)}, u32[]{:S(2)}) %collective-permute-start.10) | collective-permute-done | bytes 139296 | tf_op jit(solution)/shard_map/ppermute | solution.py:222
  51.2 0.6 collective-permute-done.11.refs_5_
  52.2 1.4 %collective-permute-start.13 = (s16[176,256]{1,0:T(8,128)(2,1)S(1)}, s16[176,256]{1,0:T(8,128)(2,1)S(1)}, u32[]{:S(2)}, u32[]{:S(2)}) collective-permute-start(s16[176,256]{1,0:T(8,128)(2,1)S(1)} %get-tuple-element.36), channel_id=1, source_target_pairs={{0,2},{1,3},{2,0},{3,1},{4,6},{5,7},{6,4},{7,5},{8,10},{9,11},{10,... | collective-permute-start | bytes 270344 | tf_op jit(solution)/shard_map/ppermute | solution.py:222
  53.6 2.3 %collective-permute-start.14 = (s16[176,256]{1,0:T(8,128)(2,1)S(1)}, s16[176,256]{1,0:T(8,128)(2,1)S(1)}, u32[]{:S(2)}, u32[]{:S(2)}) collective-permute-start(s16[176,256]{1,0:T(8,128)(2,1)S(1)} %get-tuple-element.37), channel_id=1, source_target_pairs={{0,3},{1,0},{2,1},{3,2},{4,7},{5,4},{6,5},{7,6},{8,11},{9,8},{10,9... | collective-permute-start | bytes 270344 | tf_op jit(solution)/shard_map/ppermute | solution.py:222
  55.9 1.6 %collective-permute-start.15 = (s16[80,256]{1,0:T(8,128)(2,1)S(1)}, s16[80,256]{1,0:T(8,128)(2,1)S(1)}, u32[]{:S(2)}, u32[]{:S(2)}) collective-permute-start(s16[80,256]{1,0:T(8,128)(2,1)S(1)} %get-tuple-element.38), channel_id=1, source_target_pairs={{0,16},{16,0},{1,17},{17,1},{2,18},{18,2},{3,19},{19,3},{4,20},{20... | collective-permute-start | bytes 122888 | tf_op jit(solution)/shard_map/ppermute | solution.py:222
  57.5 2.0 %collective-permute-done.15.refs_5_ = s16[80,256]{1,0:T(8,128)(2,1)S(1)} collective-permute-done((s16[80,256]{1,0:T(8,128)(2,1)S(1)}, s16[80,256]{1,0:T(8,128)(2,1)S(1)}, u32[]{:S(2)}, u32[]{:S(2)}) %collective-permute-start.15) | collective-permute-done | bytes 40992 | tf_op jit(solution)/shard_map/ppermute | solution.py:222
  59.5 1.7 %collective-permute-done.13.refs_3_ = s16[176,256]{1,0:T(8,128)(2,1)S(1)} collective-permute-done((s16[176,256]{1,0:T(8,128)(2,1)S(1)}, s16[176,256]{1,0:T(8,128)(2,1)S(1)}, u32[]{:S(2)}, u32[]{:S(2)}) %collective-permute-start.13) | collective-permute-done | bytes 90144 | tf_op jit(solution)/shard_map/ppermute | solution.py:222
  61.3 0.7 %last.1 = (f32[1,32,256]{2,1,0:T(8,128)}, f32[1,128,256]{2,1,0:T(8,128)}, f32[1,64,256]{2,1,0:T(8,128)}) custom-call(f32[160,256]{1,0:T(8,128)S(1)} %get-tuple-element.33.refs_0_, f32[64,256]{1,0:T(8,128)S(1)} %get-tuple-element.34.refs_1_, s16[176,256]{1,0:T(8,128)(2,1)S(1)} %collective-permute-done.12.refs_2_, ...), custom_call_target="tpu_custom_call" | custom-call | tf_op jit(solution)/shard_map/last/pallas_call | solution.py:293
  (27 shorter events, 1.8 us)
Async XLA Ops:
  1.5 9.3 %collective-permute-start.2 = (bf16[160,256]{1,0:T(8,128)(2,1)S(1)}, bf16[160,256]{1,0:T(8,128)(2,1)S(1)}, u32[]{:S(2)}, u32[]{:S(2)}) collective-permute-start(bf16[160,256]{1,0:T(8,128)(2,1)S(1)} %pad_maximum_fusion.2.refs_0_), channel_id=1, source_target_pairs={{0,3},{1,0},{2,1},{3,2},{4,7},{5,4},{6,5},{7,6},{8,11},{9,8},{10,9... | collective-permute-start | bytes 245768 | tf_op jit(solution)/shard_map/ppermute | solution.py:222
  5.6 7.7 %collective-permute-start.1 = (bf16[160,256]{1,0:T(8,128)(2,1)S(1)}, bf16[160,256]{1,0:T(8,128)(2,1)S(1)}, u32[]{:S(2)}, u32[]{:S(2)}) collective-permute-start(bf16[160,256]{1,0:T(8,128)(2,1)S(1)} %pad_maximum_fusion.2.refs_0_), channel_id=1, source_target_pairs={{0,2},{1,3},{2,0},{3,1},{4,6},{5,7},{6,4},{7,5},{8,10},{9,11},{10,... | collective-permute-start | bytes 245768 | tf_op jit(solution)/shard_map/ppermute | solution.py:222
  5.6 7.7 %collective-permute-start = (bf16[160,256]{1,0:T(8,128)(2,1)S(1)}, bf16[160,256]{1,0:T(8,128)(2,1)S(1)}, u32[]{:S(2)}, u32[]{:S(2)}) collective-permute-start(bf16[160,256]{1,0:T(8,128)(2,1)S(1)} %pad_maximum_fusion.2.refs_0_), channel_id=1, source_target_pairs={{0,1},{1,2},{2,3},{3,0},{4,5},{5,6},{6,7},{7,4},{8,9},{9,10},{10,1... | collective-permute-start | bytes 245768 | tf_op jit(solution)/shard_map/ppermute | solution.py:222
  6.9 7.2 %collective-permute-start.3 = (bf16[192,256]{1,0:T(8,128)(2,1)S(1)}, bf16[192,256]{1,0:T(8,128)(2,1)S(1)}, u32[]{:S(2)}, u32[]{:S(2)}) collective-permute-start(bf16[192,256]{1,0:T(8,128)(2,1)S(1)} %pad_maximum_fusion.1.refs_4_), channel_id=1, source_target_pairs={{0,16},{16,0},{1,17},{17,1},{2,18},{18,2},{3,19},{19,3},{4,20},{20... | collective-permute-start | bytes 294920 | tf_op jit(solution)/shard_map/ppermute | solution.py:222
  14.2 4.3 %collective-permute-start.6 = (bf16[256,256]{1,0:T(8,128)(2,1)S(1)}, bf16[256,256]{1,0:T(8,128)(2,1)S(1)}, u32[]{:S(2)}, u32[]{:S(2)}) collective-permute-start(bf16[256,256]{1,0:T(8,128)(2,1)S(1)} %slice_dynamic-update-slice_fusion.refs_7_), channel_id=1, source_target_pairs={{0,8},{4,12},{8,0},{12,4},{1,9},{5,13},{9,1},{13,5},{2,10},{6,14},... | collective-permute-start | bytes 393224 | tf_op jit(solution)/shard_map/ppermute | solution.py:222
  15.5 5.4 %collective-permute-start.4 = (bf16[384,256]{1,0:T(8,128)(2,1)S(1)}, bf16[384,256]{1,0:T(8,128)(2,1)S(1)}, u32[]{:S(2)}, u32[]{:S(2)}) collective-permute-start(bf16[384,256]{1,0:T(8,128)(2,1)S(1)} %pad_maximum_fusion), channel_id=1, source_target_pairs={{0,16},{16,0},{1,17},{17,1},{2,18},{18,2},{3,19},{19,3},{4,20},{20... | collective-permute-start | bytes 589832 | tf_op jit(solution)/shard_map/ppermute | solution.py:222
  16.8 3.4 %collective-permute-start.5 = (bf16[256,256]{1,0:T(8,128)(2,1)S(1)}, bf16[256,256]{1,0:T(8,128)(2,1)S(1)}, u32[]{:S(2)}, u32[]{:S(2)}) collective-permute-start(bf16[256,256]{1,0:T(8,128)(2,1)S(1)} %slice_dynamic-update-slice_fusion.refs_7_), channel_id=1, source_target_pairs={{0,4},{4,0},{8,12},{12,8},{1,5},{5,1},{9,13},{13,9},{2,6},{6,2},{1... | collective-permute-start | bytes 393224 | tf_op jit(solution)/shard_map/ppermute | solution.py:234
  18.4 2.7 %collective-permute-start.7 = (bf16[256,256]{1,0:T(8,128)(2,1)S(1)}, bf16[256,256]{1,0:T(8,128)(2,1)S(1)}, u32[]{:S(2)}, u32[]{:S(2)}) collective-permute-start(bf16[256,256]{1,0:T(8,128)(2,1)S(1)} %collective-permute-done.6.refs_9_), channel_id=1, source_target_pairs={{0,4},{4,0},{8,12},{12,8},{1,5},{5,1},{9,13},{13,9},{2,6},{6,2},{1... | collective-permute-start | bytes 393224 | tf_op jit(solution)/shard_map/ppermute | solution.py:234
  30.2 21.6 %collective-permute-start.8 = (s16[528,256]{1,0:T(8,128)(2,1)S(1)}, s16[528,256]{1,0:T(8,128)(2,1)S(1)}, u32[]{:S(2)}, u32[]{:S(2)}) collective-permute-start(s16[528,256]{1,0:T(8,128)(2,1)S(1)} %get-tuple-element.29), channel_id=1, source_target_pairs={{0,16},{16,0},{1,17},{17,1},{2,18},{18,2},{3,19},{19,3},{4,20},{20... | collective-permute-start | bytes 811016 | tf_op jit(solution)/shard_map/ppermute | solution.py:222
  37.2 7.8 %collective-permute-start.9 = (s16[272,256]{1,0:T(8,128)(2,1)S(1)}, s16[272,256]{1,0:T(8,128)(2,1)S(1)}, u32[]{:S(2)}, u32[]{:S(2)}) collective-permute-start(s16[272,256]{1,0:T(8,128)(2,1)S(1)} %get-tuple-element.30), channel_id=1, source_target_pairs={{0,4},{4,8},{8,12},{12,0},{1,5},{5,9},{9,13},{13,1},{2,6},{6,10},{... | collective-permute-start | bytes 417800 | tf_op jit(solution)/shard_map/ppermute | solution.py:222
  37.2 14.0 %collective-permute-start.10 = (s16[272,256]{1,0:T(8,128)(2,1)S(1)}, s16[272,256]{1,0:T(8,128)(2,1)S(1)}, u32[]{:S(2)}, u32[]{:S(2)}) collective-permute-start(s16[272,256]{1,0:T(8,128)(2,1)S(1)} %get-tuple-element.31), channel_id=1, source_target_pairs={{0,8},{4,12},{8,0},{12,4},{1,9},{5,13},{9,1},{13,5},{2,10},{6,14},... | collective-permute-start | bytes 417800 | tf_op jit(solution)/shard_map/ppermute | solution.py:222
  44.9 6.9 %collective-permute-start.11 = (s16[272,256]{1,0:T(8,128)(2,1)S(1)}, s16[272,256]{1,0:T(8,128)(2,1)S(1)}, u32[]{:S(2)}, u32[]{:S(2)}) collective-permute-start(s16[272,256]{1,0:T(8,128)(2,1)S(1)} %get-tuple-element.32), channel_id=1, source_target_pairs={{0,12},{4,0},{8,4},{12,8},{1,13},{5,1},{9,5},{13,9},{2,14},{6,2},{... | collective-permute-start | bytes 417800 | tf_op jit(solution)/shard_map/ppermute | solution.py:222
  52.2 7.4 %collective-permute-start.12 = (s16[176,256]{1,0:T(8,128)(2,1)S(1)}, s16[176,256]{1,0:T(8,128)(2,1)S(1)}, u32[]{:S(2)}, u32[]{:S(2)}) collective-permute-start(s16[176,256]{1,0:T(8,128)(2,1)S(1)} %get-tuple-element.35), channel_id=1, source_target_pairs={{0,1},{1,2},{2,3},{3,0},{4,5},{5,6},{6,7},{7,4},{8,9},{9,10},{10,1... | collective-permute-start | bytes 270344 | tf_op jit(solution)/shard_map/ppermute | solution.py:222
  52.2 9.0 %collective-permute-start.13 = (s16[176,256]{1,0:T(8,128)(2,1)S(1)}, s16[176,256]{1,0:T(8,128)(2,1)S(1)}, u32[]{:S(2)}, u32[]{:S(2)}) collective-permute-start(s16[176,256]{1,0:T(8,128)(2,1)S(1)} %get-tuple-element.36), channel_id=1, source_target_pairs={{0,2},{1,3},{2,0},{3,1},{4,6},{5,7},{6,4},{7,5},{8,10},{9,11},{10,... | collective-permute-start | bytes 270344 | tf_op jit(solution)/shard_map/ppermute | solution.py:222
  53.6 7.7 %collective-permute-start.14 = (s16[176,256]{1,0:T(8,128)(2,1)S(1)}, s16[176,256]{1,0:T(8,128)(2,1)S(1)}, u32[]{:S(2)}, u32[]{:S(2)}) collective-permute-start(s16[176,256]{1,0:T(8,128)(2,1)S(1)} %get-tuple-element.37), channel_id=1, source_target_pairs={{0,3},{1,0},{2,1},{3,2},{4,7},{5,4},{6,5},{7,6},{8,11},{9,8},{10,9... | collective-permute-start | bytes 270344 | tf_op jit(solution)/shard_map/ppermute | solution.py:222
  55.9 3.6 %collective-permute-start.15 = (s16[80,256]{1,0:T(8,128)(2,1)S(1)}, s16[80,256]{1,0:T(8,128)(2,1)S(1)}, u32[]{:S(2)}, u32[]{:S(2)}) collective-permute-start(s16[80,256]{1,0:T(8,128)(2,1)S(1)} %get-tuple-element.38), channel_id=1, source_target_pairs={{0,16},{16,0},{1,17},{17,1},{2,18},{18,2},{3,19},{19,3},{4,20},{20... | collective-permute-start | bytes 122888 | tf_op jit(solution)/shard_map/ppermute | solution.py:222

commit v6 on v5

--- a/solution.py
+++ b/solution.py
@@ -45,7 +45,7 @@
     return runs
 
 
-def add_block(slot, places, weights, slabs, grads, held):
+def add_block(places, weight, slabs, grads, held):
     slab_a, slab_b, slab_c = slabs
     grad_a, grad_b, grad_c = grads
     f32, bf16 = jnp.float32, jnp.bfloat16
@@ -55,7 +55,7 @@
     rows_c = slab_c[pl.ds(at_c, BLK), :]
     rank = rows_b.shape[1]
     wide_b = rows_b.astype(f32)
-    weight = jnp.transpose(weights[slot].astype(f32)).astype(bf16)
+    weight = jnp.transpose(weight.astype(f32)).astype(bf16)
 
     def start(first):
         mixed = []
@@ -74,7 +74,7 @@
             later = start(first + GROUP)
         error = []
         for i in range(GROUP):
-            seen = held[slot, first + i].astype(f32)
+            seen = held[first + i].astype(f32)
             one = (jnp.exp(rate[i * BLK : (i + 1) * BLK]) - seen).astype(bf16)
             error.append(one * weight[:, first + i : first + i + 1])
         error = jnp.concatenate(error, 0)
@@ -89,7 +89,7 @@
     grad_c[pl.ds(at_c, BLK), :] += sum_c
 
 
-def block_kernel(nx, ny, nz, table, entries, weights, *refs):
+def block_kernel(nx, ny, nz, table, entries, weights, early, *refs):
     along_z, along_x, rest_b, got_ac = take(refs, nz, nx, nx - 1, ny)
     refs = refs[nz + 2 * nx - 1 + ny :]
     own_b, own_ac = refs[:2]
@@ -103,7 +103,7 @@
     def copy(slot, chunk):
         rows = pl.ds(chunk * CHUNK, CHUNK)
         return pltpu.make_async_copy(
-            entries.at[0, 0, 0, slot, rows], held.at[slot, rows], arrivals.at[slot, chunk]
+            entries.at[0, 0, 0, slot, rows], held.at[slot - 1, rows], arrivals.at[slot - 1, chunk]
         )
 
     def fetch(slot):
@@ -112,7 +112,7 @@
             for chunk in range(BLK // CHUNK):
                 copy(slot, chunk).start()
 
-    fetch(0)
+    fetch(1)
     grad_a[...] = jnp.zeros_like(grad_a)
     grad_b[...] = jnp.zeros_like(grad_b)
     grad_c[...] = jnp.zeros_like(grad_c)
@@ -137,14 +137,21 @@
             first = nz * per_a + j * per_c
             slab_c[pl.ds(pl.multiple_of(at, per_c), per_c), :] = got_ac[i][first : first + per_c, :]
 
-    @pl.loop(0, count)
+    def add(slot, ready):
+        places = [table[1 + 3 * slot + i] for i in range(3)]
+        slabs, grads = (slab_a, slab_b, slab_c), (grad_a, grad_b, grad_c)
+        add_block(places, weights[slot], slabs, grads, ready)
+
+    @pl.when(count > 0)
+    def _():
+        add(0, early)
+
+    @pl.loop(1, count)
     def _(slot):
-        slabs, grads = (slab_a, slab_b, slab_c), (grad_a, grad_b, grad_c)
         for chunk in range(BLK // CHUNK):
             copy(slot, chunk).wait()
         fetch(slot + 1)
-        places = [table[1 + 3 * slot + i] for i in range(3)]
-        add_block(slot, places, weights, slabs, grads, held)
+        add(slot, held.at[slot - 1])
 
     some_b, some_a = all_b // nx, all_a // ny
     for i in range(nx):
@@ -257,6 +264,8 @@
     some_ac = jnp.concatenate([p[per_b:] for p in along_z] + [p[:per_c] for p in along_x], 0)
     got_ac = pairwise(some_ac, "gy", ny)
     rest_b = around(jnp.concatenate([p[:per_b] for p in along_z[1:]], 0), "gx", nx)[1:]
+    early = jnp.maximum(tensor_blocks[0, 0, 0, 0], 0)
+
     f32, i16 = jnp.float32, jnp.int16
     outs = [jax.ShapeDtypeStruct((some_b, rank), f32), jax.ShapeDtypeStruct((some_a + some_c, rank), f32)]
     outs += [jax.ShapeDtypeStruct((some_b + PAD, rank), i16)] * (nx - 1)
@@ -264,14 +273,14 @@
     results = pl.pallas_call(
         functools.partial(block_kernel, nx, ny, nz),
         in_specs=[pl.BlockSpec(memory_space=pltpu.SMEM), pl.BlockSpec(memory_space=pl.ANY)]
-        + [pl.BlockSpec(memory_space=pltpu.VMEM)] * (nz + 2 * nx + ny),
+        + [pl.BlockSpec(memory_space=pltpu.VMEM)] * (1 + nz + 2 * nx + ny),
         scratch_shapes=[pltpu.VMEM((n, rank), jnp.bfloat16) for n in (all_a, all_b, all_c)]
         + [pltpu.VMEM((n, rank), f32) for n in (all_a, all_b, all_c)]
-        + [pltpu.VMEM((slots, BLK, BLK, BLK), jnp.bfloat16), pltpu.SemaphoreType.DMA((slots, BLK // CHUNK))],
+        + [pltpu.VMEM((slots - 1, BLK, BLK, BLK), jnp.bfloat16), pltpu.SemaphoreType.DMA((slots - 1, BLK // CHUNK))],
         out_shape=outs,
         compiler_params=pltpu.CompilerParams(vmem_limit_bytes=44 * 2**20),
         name="blocks",
-    )(table, tensor_blocks, weights, *along_z, *along_x, *rest_b, *got_ac)
+    )(table, tensor_blocks, weights, early, *along_z, *along_x, *rest_b, *got_ac)
 
     own_b, own_ac = results[:2]
     got_b = [shift(r, "gx", nx, i + 1) for i, r in enumerate(results[2 : 1 + nx])]

time: 62.7 us -> 62 us (0.989)
  the two profiles are of different devices: /device:TPU:1 before, /device:TPU:0 now
where the time goes in v6:
time: 62 us; the launch traced here: 61.8 us
  starting transfers between devices  36.9 us (60%)
  waiting for transfers between devices  14.4 us (23%)
  other arithmetic  5.21 us (8%)
  Pallas kernels  2.38 us (4%)
  local copies, waits for them, and re-layouts  1.65 us (3%)
  between operations  1.38 us (2%)
    ppermute x14, starting transfers between devices, shift(): lax.ppermute(array, axis, [(i, (i + by) % size) for i in range(size)])  36.9 us
    ppermute x14, waiting for transfers between devices, shift(): lax.ppermute(array, axis, [(i, (i + by) % size) for i in range(size)])  14.3 us
    max x1, other arithmetic, per_device(): early = jnp.maximum(tensor_blocks[0, 0, 0, 0], 0)  2.46 us
    pallas_call x1, Pallas kernels, per_device(): pl.pallas_call(functools.partial(block_kernel, nx, ny, nz), in_specs=[pl....  1.27 us
  transfers between devices with their start and end apart: 16, of which 7 were waited for; matrix products, arithmetic and copies ran while one was open for 10% of the time, Pallas kernels for 0%

profile of v6, /device:TPU:0, one launch (start us, length us, event | category | flops | bytes accessed | tf_op | source)
XLA Modules:
  0.0 61.8 jit_solution(6859896178292784137)
XLA Ops:
  0.6 0.9 %pad_maximum_fusion.2.refs_0_ = bf16[160,256]{1,0:T(8,128)(2,1)S(1)} fusion(bf16[32,256]{1,0:T(8,128)(2,1)} %bitcast.17, bf16[128,256]{1,0:T(8,128)(2,1)} %bitcast.14), kind=kLoop, calls=%fused_computation.4 | loop fusion | flops 163840 | bytes 163840 | tf_op jit(solution)/shard_map/concatenate | solution.py:259
  1.5 5.0 %collective-permute-start.2 = (bf16[160,256]{1,0:T(8,128)(2,1)S(1)}, bf16[160,256]{1,0:T(8,128)(2,1)S(1)}, u32[]{:S(2)}, u32[]{:S(2)}) collective-permute-start(bf16[160,256]{1,0:T(8,128)(2,1)S(1)} %pad_maximum_fusion.2.refs_0_), channel_id=1, source_target_pairs={{0,3},{1,0},{2,1},{3,2},{4,7},{5,4},{6,5},{7,6},{8,11},{9,8},{10,9... | collective-permute-start | bytes 245768 | tf_op jit(solution)/shard_map/ppermute | solution.py:229
  6.5 1.0 %collective-permute-start = (bf16[160,256]{1,0:T(8,128)(2,1)S(1)}, bf16[160,256]{1,0:T(8,128)(2,1)S(1)}, u32[]{:S(2)}, u32[]{:S(2)}) collective-permute-start(bf16[160,256]{1,0:T(8,128)(2,1)S(1)} %pad_maximum_fusion.2.refs_0_), channel_id=1, source_target_pairs={{0,1},{1,2},{2,3},{3,0},{4,5},{5,6},{6,7},{7,4},{8,9},{9,10},{10,1... | collective-permute-start | bytes 245768 | tf_op jit(solution)/shard_map/ppermute | solution.py:229
  7.6 0.8 %pad_maximum_fusion.1.refs_4_ = bf16[192,256]{1,0:T(8,128)(2,1)S(1)} fusion(bf16[128,256]{1,0:T(8,128)(2,1)} %bitcast.15, bf16[64,256]{1,0:T(8,128)(2,1)} %bitcast.16), kind=kLoop, calls=%fused_computation.2 | loop fusion | flops 196608 | bytes 196608 | tf_op jit(solution)/shard_map/concatenate | solution.py:262
  8.4 1.6 %collective-permute-start.3 = (bf16[192,256]{1,0:T(8,128)(2,1)S(1)}, bf16[192,256]{1,0:T(8,128)(2,1)S(1)}, u32[]{:S(2)}, u32[]{:S(2)}) collective-permute-start(bf16[192,256]{1,0:T(8,128)(2,1)S(1)} %pad_maximum_fusion.1.refs_4_), channel_id=1, source_target_pairs={{0,16},{16,0},{1,17},{17,1},{2,18},{18,2},{3,19},{19,3},{4,20},{20... | collective-permute-start | bytes 294920 | tf_op jit(solution)/shard_map/ppermute | solution.py:229
  10.6 0.8 %copy.12 = s32[1,1,1,3,3]{3,4,0,1,2:T(4,128)S(1)} copy(s32[1,1,1,3,3]{4,2,3,1,0:T(1,128)} %param.9) | data formatting | bytes 72 | tf_op jit(solution)/shard_map/transpose | solution.py:261
  11.5 0.9 %convert_bitcast_fusion.weights = bf16[3,128,128]{2,1,0:T(8,128)(2,1)S(1)} fusion(s32[1,1,1,3,128,128]{5,4,3,2,1,0:T(8,128)} %param.8), kind=kLoop, calls=%fused_computation.3 | loop fusion | flops 49152 | bytes 294912 | tf_op jit(solution)/shard_map/convert_element_type | solution.py:260
  12.5 1.5 %collective-permute-done.1.refs_2_ = bf16[160,256]{1,0:T(8,128)(2,1)S(1)} collective-permute-done((bf16[160,256]{1,0:T(8,128)(2,1)S(1)}, bf16[160,256]{1,0:T(8,128)(2,1)S(1)}, u32[]{:S(2)}, u32[]{:S(2)}) %collective-permute-start.1) | collective-permute-done | bytes 81952 | tf_op jit(solution)/shard_map/ppermute | solution.py:229
  14.1 0.8 %constant_dynamic-update-slice_fusion = bf16[256,256]{1,0:T(8,128)(2,1)S(1)} fusion(bf16[256,256]{1,0:T(8,128)(2,1)S(1)} %slice_dynamic-update-slice_fusion.1, bf16[1,64,256]{2,1,0:T(8,128)(2,1)} %param.13), kind=kLoop, calls=%fused_computation.10 | loop fusion | bytes 65536
  14.9 1.6 %collective-permute-start.6 = (bf16[256,256]{1,0:T(8,128)(2,1)S(1)}, bf16[256,256]{1,0:T(8,128)(2,1)S(1)}, u32[]{:S(2)}, u32[]{:S(2)}) collective-permute-start(bf16[256,256]{1,0:T(8,128)(2,1)S(1)} %slice_dynamic-update-slice_fusion.refs_7_), channel_id=1, source_target_pairs={{0,8},{4,12},{8,0},{12,4},{1,9},{5,13},{9,1},{13,5},{2,10},{6,14},... | collective-permute-start | bytes 393224 | tf_op jit(solution)/shard_map/ppermute | solution.py:229
  16.5 1.6 %collective-permute-start.4 = (bf16[384,256]{1,0:T(8,128)(2,1)S(1)}, bf16[384,256]{1,0:T(8,128)(2,1)S(1)}, u32[]{:S(2)}, u32[]{:S(2)}) collective-permute-start(bf16[384,256]{1,0:T(8,128)(2,1)S(1)} %pad_maximum_fusion), channel_id=1, source_target_pairs={{0,16},{16,0},{1,17},{17,1},{2,18},{18,2},{3,19},{19,3},{4,20},{20... | collective-permute-start | bytes 589832 | tf_op jit(solution)/shard_map/ppermute | solution.py:229
  18.1 2.0 %collective-permute-done.6.refs_9_ = bf16[256,256]{1,0:T(8,128)(2,1)S(1)} collective-permute-done((bf16[256,256]{1,0:T(8,128)(2,1)S(1)}, bf16[256,256]{1,0:T(8,128)(2,1)S(1)}, u32[]{:S(2)}, u32[]{:S(2)}) %collective-permute-start.6) | collective-permute-done | bytes 131104 | tf_op jit(solution)/shard_map/ppermute | solution.py:229
  20.0 2.5 %maximum_bitcast_fusion.early = bf16[128,128,128]{2,1,0:T(8,128)(2,1)S(1)} fusion(bf16[1,1,1,3,128,128,128]{6,5,4,3,2,1,0:T(8,128)(2,1)} %entries.1), kind=kLoop, calls=%fused_computation | loop fusion | flops 2097152 | bytes 8388608 | tf_op jit(solution)/shard_map/max | solution.py:267
  22.8 1.3 %blocks.1 = (f32[512,256]{1,0:T(8,128)S(1)}, f32[256,256]{1,0:T(8,128)S(1)}, s16[528,256]{1,0:T(8,128)(2,1)S(1)}, s16[272,256]{1,0:T(8,128)(2,1)S(1)}, s16[272,2...) custom-call(s32[10]{0:T(128)S(1)} %pad_add_fusion.table, bf16[1,1,1,3,128,128,128]{6,5,4,3,2,1,0:T(8,128)(2,1)} %entries.1, ...), custom_call_target="tpu_custom_call" | custom-call | tf_op jit(solution)/shard_map/blocks/pallas_call | solution.py:273
  24.1 13.2 %collective-permute-start.8 = (s16[528,256]{1,0:T(8,128)(2,1)S(1)}, s16[528,256]{1,0:T(8,128)(2,1)S(1)}, u32[]{:S(2)}, u32[]{:S(2)}) collective-permute-start(s16[528,256]{1,0:T(8,128)(2,1)S(1)} %get-tuple-element.29), channel_id=1, source_target_pairs={{0,16},{16,0},{1,17},{17,1},{2,18},{18,2},{3,19},{19,3},{4,20},{20... | collective-permute-start | bytes 811016 | tf_op jit(solution)/shard_map/ppermute | solution.py:229
  37.3 7.1 %collective-permute-start.10 = (s16[272,256]{1,0:T(8,128)(2,1)S(1)}, s16[272,256]{1,0:T(8,128)(2,1)S(1)}, u32[]{:S(2)}, u32[]{:S(2)}) collective-permute-start(s16[272,256]{1,0:T(8,128)(2,1)S(1)} %get-tuple-element.31), channel_id=1, source_target_pairs={{0,8},{4,12},{8,0},{12,4},{1,9},{5,13},{9,1},{13,5},{2,10},{6,14},... | collective-permute-start | bytes 417800 | tf_op jit(solution)/shard_map/ppermute | solution.py:229
  44.4 1.4 %collective-permute-start.11 = (s16[272,256]{1,0:T(8,128)(2,1)S(1)}, s16[272,256]{1,0:T(8,128)(2,1)S(1)}, u32[]{:S(2)}, u32[]{:S(2)}) collective-permute-start(s16[272,256]{1,0:T(8,128)(2,1)S(1)} %get-tuple-element.32), channel_id=1, source_target_pairs={{0,12},{4,0},{8,4},{12,8},{1,13},{5,1},{9,5},{13,9},{2,14},{6,2},{... | collective-permute-start | bytes 417800 | tf_op jit(solution)/shard_map/ppermute | solution.py:229
  45.8 2.6 %collective-permute-done.10.refs_4_ = s16[272,256]{1,0:T(8,128)(2,1)S(1)} collective-permute-done((s16[272,256]{1,0:T(8,128)(2,1)S(1)}, s16[272,256]{1,0:T(8,128)(2,1)S(1)}, u32[]{:S(2)}, u32[]{:S(2)}) %collective-permute-start.10) | collective-permute-done | bytes 139296 | tf_op jit(solution)/shard_map/ppermute | solution.py:229
  48.4 2.4 %collective-permute-done.11.refs_5_ = s16[272,256]{1,0:T(8,128)(2,1)S(1)} collective-permute-done((s16[272,256]{1,0:T(8,128)(2,1)S(1)}, s16[272,256]{1,0:T(8,128)(2,1)S(1)}, u32[]{:S(2)}, u32[]{:S(2)}) %collective-permute-start.11) | collective-permute-done | bytes 139296 | tf_op jit(solution)/shard_map/ppermute | solution.py:229
  51.2 2.6 %collective-permute-start.13 = (s16[176,256]{1,0:T(8,128)(2,1)S(1)}, s16[176,256]{1,0:T(8,128)(2,1)S(1)}, u32[]{:S(2)}, u32[]{:S(2)}) collective-permute-start(s16[176,256]{1,0:T(8,128)(2,1)S(1)} %get-tuple-element.36), channel_id=1, source_target_pairs={{0,2},{1,3},{2,0},{3,1},{4,6},{5,7},{6,4},{7,5},{8,10},{9,11},{10,... | collective-permute-start | bytes 270344 | tf_op jit(solution)/shard_map/ppermute | solution.py:229
  53.8 1.7 %collective-permute-start.14 = (s16[176,256]{1,0:T(8,128)(2,1)S(1)}, s16[176,256]{1,0:T(8,128)(2,1)S(1)}, u32[]{:S(2)}, u32[]{:S(2)}) collective-permute-start(s16[176,256]{1,0:T(8,128)(2,1)S(1)} %get-tuple-element.37), channel_id=1, source_target_pairs={{0,3},{1,0},{2,1},{3,2},{4,7},{5,4},{6,5},{7,6},{8,11},{9,8},{10,9... | collective-permute-start | bytes 270344 | tf_op jit(solution)/shard_map/ppermute | solution.py:229
  55.5 4.0 %collective-permute-done.15.refs_5_ = s16[80,256]{1,0:T(8,128)(2,1)S(1)} collective-permute-done((s16[80,256]{1,0:T(8,128)(2,1)S(1)}, s16[80,256]{1,0:T(8,128)(2,1)S(1)}, u32[]{:S(2)}, u32[]{:S(2)}) %collective-permute-start.15) | collective-permute-done | bytes 40992 | tf_op jit(solution)/shard_map/ppermute | solution.py:229
  59.5 1.6 %collective-permute-done.13.refs_3_ = s16[176,256]{1,0:T(8,128)(2,1)S(1)} collective-permute-done((s16[176,256]{1,0:T(8,128)(2,1)S(1)}, s16[176,256]{1,0:T(8,128)(2,1)S(1)}, u32[]{:S(2)}, u32[]{:S(2)}) %collective-permute-start.13) | collective-permute-done | bytes 90144 | tf_op jit(solution)/shard_map/ppermute | solution.py:229
  61.1 0.8 %last.1 = (f32[1,32,256]{2,1,0:T(8,128)}, f32[1,128,256]{2,1,0:T(8,128)}, f32[1,64,256]{2,1,0:T(8,128)}) custom-call(f32[160,256]{1,0:T(8,128)S(1)} %get-tuple-element.33.refs_0_, f32[64,256]{1,0:T(8,128)S(1)} %get-tuple-element.34.refs_1_, s16[176,256]{1,0:T(8,128)(2,1)S(1)} %collective-permute-done.12.refs_2_, ...), custom_call_target="tpu_custom_call" | custom-call | tf_op jit(solution)/shard_map/last/pallas_call | solution.py:302
  (28 shorter events, 0.9 us)
Async XLA Ops:
  1.5 11.0 %collective-permute-start.2 = (bf16[160,256]{1,0:T(8,128)(2,1)S(1)}, bf16[160,256]{1,0:T(8,128)(2,1)S(1)}, u32[]{:S(2)}, u32[]{:S(2)}) collective-permute-start(bf16[160,256]{1,0:T(8,128)(2,1)S(1)} %pad_maximum_fusion.2.refs_0_), channel_id=1, source_target_pairs={{0,3},{1,0},{2,1},{3,2},{4,7},{5,4},{6,5},{7,6},{8,11},{9,8},{10,9... | collective-permute-start | bytes 245768 | tf_op jit(solution)/shard_map/ppermute | solution.py:229
  6.5 7.5 %collective-permute-start.1 = (bf16[160,256]{1,0:T(8,128)(2,1)S(1)}, bf16[160,256]{1,0:T(8,128)(2,1)S(1)}, u32[]{:S(2)}, u32[]{:S(2)}) collective-permute-start(bf16[160,256]{1,0:T(8,128)(2,1)S(1)} %pad_maximum_fusion.2.refs_0_), channel_id=1, source_target_pairs={{0,2},{1,3},{2,0},{3,1},{4,6},{5,7},{6,4},{7,5},{8,10},{9,11},{10,... | collective-permute-start | bytes 245768 | tf_op jit(solution)/shard_map/ppermute | solution.py:229
  6.5 7.5 %collective-permute-start = (bf16[160,256]{1,0:T(8,128)(2,1)S(1)}, bf16[160,256]{1,0:T(8,128)(2,1)S(1)}, u32[]{:S(2)}, u32[]{:S(2)}) collective-permute-start(bf16[160,256]{1,0:T(8,128)(2,1)S(1)} %pad_maximum_fusion.2.refs_0_), channel_id=1, source_target_pairs={{0,1},{1,2},{2,3},{3,0},{4,5},{5,6},{6,7},{7,4},{8,9},{9,10},{10,1... | collective-permute-start | bytes 245768 | tf_op jit(solution)/shard_map/ppermute | solution.py:229
  8.4 6.5 %collective-permute-start.3 = (bf16[192,256]{1,0:T(8,128)(2,1)S(1)}, bf16[192,256]{1,0:T(8,128)(2,1)S(1)}, u32[]{:S(2)}, u32[]{:S(2)}) collective-permute-start(bf16[192,256]{1,0:T(8,128)(2,1)S(1)} %pad_maximum_fusion.1.refs_4_), channel_id=1, source_target_pairs={{0,16},{16,0},{1,17},{17,1},{2,18},{18,2},{3,19},{19,3},{4,20},{20... | collective-permute-start | bytes 294920 | tf_op jit(solution)/shard_map/ppermute | solution.py:229
  14.9 5.2 %collective-permute-start.6 = (bf16[256,256]{1,0:T(8,128)(2,1)S(1)}, bf16[256,256]{1,0:T(8,128)(2,1)S(1)}, u32[]{:S(2)}, u32[]{:S(2)}) collective-permute-start(bf16[256,256]{1,0:T(8,128)(2,1)S(1)} %slice_dynamic-update-slice_fusion.refs_7_), channel_id=1, source_target_pairs={{0,8},{4,12},{8,0},{12,4},{1,9},{5,13},{9,1},{13,5},{2,10},{6,14},... | collective-permute-start | bytes 393224 | tf_op jit(solution)/shard_map/ppermute | solution.py:229
  16.5 6.3 %collective-permute-start.4 = (bf16[384,256]{1,0:T(8,128)(2,1)S(1)}, bf16[384,256]{1,0:T(8,128)(2,1)S(1)}, u32[]{:S(2)}, u32[]{:S(2)}) collective-permute-start(bf16[384,256]{1,0:T(8,128)(2,1)S(1)} %pad_maximum_fusion), channel_id=1, source_target_pairs={{0,16},{16,0},{1,17},{17,1},{2,18},{18,2},{3,19},{19,3},{4,20},{20... | collective-permute-start | bytes 589832 | tf_op jit(solution)/shard_map/ppermute | solution.py:229
  18.1 4.4 %collective-permute-start.5 = (bf16[256,256]{1,0:T(8,128)(2,1)S(1)}, bf16[256,256]{1,0:T(8,128)(2,1)S(1)}, u32[]{:S(2)}, u32[]{:S(2)}) collective-permute-start(bf16[256,256]{1,0:T(8,128)(2,1)S(1)} %slice_dynamic-update-slice_fusion.refs_7_), channel_id=1, source_target_pairs={{0,4},{4,0},{8,12},{12,8},{1,5},{5,1},{9,13},{13,9},{2,6},{6,2},{1... | collective-permute-start | bytes 393224 | tf_op jit(solution)/shard_map/ppermute | solution.py:241
  20.0 2.7 %collective-permute-start.7 = (bf16[256,256]{1,0:T(8,128)(2,1)S(1)}, bf16[256,256]{1,0:T(8,128)(2,1)S(1)}, u32[]{:S(2)}, u32[]{:S(2)}) collective-permute-start(bf16[256,256]{1,0:T(8,128)(2,1)S(1)} %collective-permute-done.6.refs_9_), channel_id=1, source_target_pairs={{0,4},{4,0},{8,12},{12,8},{1,5},{5,1},{9,13},{13,9},{2,6},{6,2},{1... | collective-permute-start | bytes 393224 | tf_op jit(solution)/shard_map/ppermute | solution.py:241
  24.1 26.7 %collective-permute-start.8 = (s16[528,256]{1,0:T(8,128)(2,1)S(1)}, s16[528,256]{1,0:T(8,128)(2,1)S(1)}, u32[]{:S(2)}, u32[]{:S(2)}) collective-permute-start(s16[528,256]{1,0:T(8,128)(2,1)S(1)} %get-tuple-element.29), channel_id=1, source_target_pairs={{0,16},{16,0},{1,17},{17,1},{2,18},{18,2},{3,19},{19,3},{4,20},{20... | collective-permute-start | bytes 811016 | tf_op jit(solution)/shard_map/ppermute | solution.py:229
  37.3 8.5 %collective-permute-start.9 = (s16[272,256]{1,0:T(8,128)(2,1)S(1)}, s16[272,256]{1,0:T(8,128)(2,1)S(1)}, u32[]{:S(2)}, u32[]{:S(2)}) collective-permute-start(s16[272,256]{1,0:T(8,128)(2,1)S(1)} %get-tuple-element.30), channel_id=1, source_target_pairs={{0,4},{4,8},{8,12},{12,0},{1,5},{5,9},{9,13},{13,1},{2,6},{6,10},{... | collective-permute-start | bytes 417800 | tf_op jit(solution)/shard_map/ppermute | solution.py:229
  37.3 11.1 %collective-permute-start.10 = (s16[272,256]{1,0:T(8,128)(2,1)S(1)}, s16[272,256]{1,0:T(8,128)(2,1)S(1)}, u32[]{:S(2)}, u32[]{:S(2)}) collective-permute-start(s16[272,256]{1,0:T(8,128)(2,1)S(1)} %get-tuple-element.31), channel_id=1, source_target_pairs={{0,8},{4,12},{8,0},{12,4},{1,9},{5,13},{9,1},{13,5},{2,10},{6,14},... | collective-permute-start | bytes 417800 | tf_op jit(solution)/shard_map/ppermute | solution.py:229
  44.4 6.4 %collective-permute-start.11 = (s16[272,256]{1,0:T(8,128)(2,1)S(1)}, s16[272,256]{1,0:T(8,128)(2,1)S(1)}, u32[]{:S(2)}, u32[]{:S(2)}) collective-permute-start(s16[272,256]{1,0:T(8,128)(2,1)S(1)} %get-tuple-element.32), channel_id=1, source_target_pairs={{0,12},{4,0},{8,4},{12,8},{1,13},{5,1},{9,5},{13,9},{2,14},{6,2},{... | collective-permute-start | bytes 417800 | tf_op jit(solution)/shard_map/ppermute | solution.py:229
  51.2 8.4 %collective-permute-start.12 = (s16[176,256]{1,0:T(8,128)(2,1)S(1)}, s16[176,256]{1,0:T(8,128)(2,1)S(1)}, u32[]{:S(2)}, u32[]{:S(2)}) collective-permute-start(s16[176,256]{1,0:T(8,128)(2,1)S(1)} %get-tuple-element.35), channel_id=1, source_target_pairs={{0,1},{1,2},{2,3},{3,0},{4,5},{5,6},{6,7},{7,4},{8,9},{9,10},{10,1... | collective-permute-start | bytes 270344 | tf_op jit(solution)/shard_map/ppermute | solution.py:229
  51.2 9.9 %collective-permute-start.13 = (s16[176,256]{1,0:T(8,128)(2,1)S(1)}, s16[176,256]{1,0:T(8,128)(2,1)S(1)}, u32[]{:S(2)}, u32[]{:S(2)}) collective-permute-start(s16[176,256]{1,0:T(8,128)(2,1)S(1)} %get-tuple-element.36), channel_id=1, source_target_pairs={{0,2},{1,3},{2,0},{3,1},{4,6},{5,7},{6,4},{7,5},{8,10},{9,11},{10,... | collective-permute-start | bytes 270344 | tf_op jit(solution)/shard_map/ppermute | solution.py:229
  53.8 7.3 %collective-permute-start.14 = (s16[176,256]{1,0:T(8,128)(2,1)S(1)}, s16[176,256]{1,0:T(8,128)(2,1)S(1)}, u32[]{:S(2)}, u32[]{:S(2)}) collective-permute-start(s16[176,256]{1,0:T(8,128)(2,1)S(1)} %get-tuple-element.37), channel_id=1, source_target_pairs={{0,3},{1,0},{2,1},{3,2},{4,7},{5,4},{6,5},{7,6},{8,11},{9,8},{10,9... | collective-permute-start | bytes 270344 | tf_op jit(solution)/shard_map/ppermute | solution.py:229
  55.5 4.0 %collective-permute-start.15 = (s16[80,256]{1,0:T(8,128)(2,1)S(1)}, s16[80,256]{1,0:T(8,128)(2,1)S(1)}, u32[]{:S(2)}, u32[]{:S(2)}) collective-permute-start(s16[80,256]{1,0:T(8,128)(2,1)S(1)} %get-tuple-element.38), channel_id=1, source_target_pairs={{0,16},{16,0},{1,17},{17,1},{2,18},{18,2},{3,19},{19,3},{4,20},{20... | collective-permute-start | bytes 122888 | tf_op jit(solution)/shard_map/ppermute | solution.py:229

commit v7 on v6

--- a/solution.py
+++ b/solution.py
@@ -233,13 +233,14 @@
     return [array] + [shift(array, axis, size, by) for by in range(1, size)]
 
 
-def pairwise(array, axis, size):
+def pairwise(array, axis, size, meanwhile):
     near = 2 - size % 2
     far = [array] + [shift(array, axis, size, by) for by in range(near, size, near)]
     if near == 1:
-        return far
-    swapped = [lax.ppermute(item, axis, [(i, i ^ 1) for i in range(size)]) for item in far]
-    return [item for pair in zip(far, swapped) for item in pair]
+        return far, meanwhile
+    own, meanwhile = lax.optimization_barrier((array, meanwhile))
+    swapped = [lax.ppermute(item, axis, [(i, i ^ 1) for i in range(size)]) for item in [own] + far[1:]]
+    return [item for pair in zip(far, swapped) for item in pair], meanwhile
 
 
 def before(me, place, size):
@@ -262,9 +263,9 @@
     along_x = around(jnp.concatenate([factor_c[0], factor_b[0]], 0), "gx", nx)
     *along_z, weights, table = lax.optimization_barrier((*along_z, weights, table))
     some_ac = jnp.concatenate([p[per_b:] for p in along_z] + [p[:per_c] for p in along_x], 0)
-    got_ac = pairwise(some_ac, "gy", ny)
+    early = jnp.maximum(tensor_blocks[0, 0, 0, 0], 0)
+    got_ac, early = pairwise(some_ac, "gy", ny, early)
     rest_b = around(jnp.concatenate([p[:per_b] for p in along_z[1:]], 0), "gx", nx)[1:]
-    early = jnp.maximum(tensor_blocks[0, 0, 0, 0], 0)
 
     f32, i16 = jnp.float32, jnp.int16
     outs = [jax.ShapeDtypeStruct((some_b, rank), f32), jax.ShapeDtypeStruct((some_a + some_c, rank), f32)]

time: 62 us -> 61.4 us (level)
  waiting for transfers between devices: 14.4 us -> 13.4 us
    ppermute x14, waiting for transfers between devices: 14.3 us -> 12 us  [shift(): lax.ppermute(array, axis, [(i, (i + by) % size) for i in range(size)])]
    ppermute x2, waiting for transfers between devices: 0.01 us -> 1.34 us  [pairwise(): lax.ppermute(item, axis, [(i, i ^ 1) for i in range(size)])]
  transfers between devices with their start and end apart: 16 -> 16, of which waited for: 7 -> 8; matrix products, arithmetic and copies ran while one was open for 10% -> 10% of each run, Pallas kernels for 0% -> 0%
where the time goes in v7:
time: 61.4 us; the launch traced here: 61.1 us
  starting transfers between devices  37.1 us (60%)
  waiting for transfers between devices  13.4 us (22%)
  other arithmetic  5.2 us (8%)
  Pallas kernels  2.38 us (4%)
  local copies, waits for them, and re-layouts  1.65 us (3%)
  between operations  1.39 us (2%)
    ppermute x14, starting transfers between devices, shift(): lax.ppermute(array, axis, [(i, (i + by) % size) for i in range(size)])  37.1 us
    ppermute x14, waiting for transfers between devices, shift(): lax.ppermute(array, axis, [(i, (i + by) % size) for i in range(size)])  12 us
    max x1, other arithmetic, per_device(): early = jnp.maximum(tensor_blocks[0, 0, 0, 0], 0)  2.46 us
    ppermute x2, waiting for transfers between devices, pairwise(): lax.ppermute(item, axis, [(i, i ^ 1) for i in range(size)])  1.34 us
    pallas_call x1, Pallas kernels, per_device(): pl.pallas_call(functools.partial(block_kernel, nx, ny, nz), in_specs=[pl....  1.27 us
  transfers between devices with their start and end apart: 16, of which 8 were waited for; matrix products, arithmetic and copies ran while one was open for 10% of the time, Pallas kernels for 0%

profile of v7, /device:TPU:0, one launch (start us, length us, event | category | flops | bytes accessed | tf_op | source)
XLA Modules:
  0.0 61.1 jit_solution(13318701699902353179)
XLA Ops:
  0.6 0.9 %pad_maximum_fusion.2.refs_0_ = bf16[160,256]{1,0:T(8,128)(2,1)S(1)} fusion(bf16[32,256]{1,0:T(8,128)(2,1)} %bitcast.17, bf16[128,256]{1,0:T(8,128)(2,1)} %bitcast.14), kind=kLoop, calls=%fused_computation.4 | loop fusion | flops 163840 | bytes 163840 | tf_op jit(solution)/shard_map/concatenate | solution.py:260
  1.5 5.0 %collective-permute-start.2 = (bf16[160,256]{1,0:T(8,128)(2,1)S(1)}, bf16[160,256]{1,0:T(8,128)(2,1)S(1)}, u32[]{:S(2)}, u32[]{:S(2)}) collective-permute-start(bf16[160,256]{1,0:T(8,128)(2,1)S(1)} %pad_maximum_fusion.2.refs_0_), channel_id=1, source_target_pairs={{0,3},{1,0},{2,1},{3,2},{4,7},{5,4},{6,5},{7,6},{8,11},{9,8},{10,9... | collective-permute-start | bytes 245768 | tf_op jit(solution)/shard_map/ppermute | solution.py:229
  6.5 1.0 %collective-permute-start = (bf16[160,256]{1,0:T(8,128)(2,1)S(1)}, bf16[160,256]{1,0:T(8,128)(2,1)S(1)}, u32[]{:S(2)}, u32[]{:S(2)}) collective-permute-start(bf16[160,256]{1,0:T(8,128)(2,1)S(1)} %pad_maximum_fusion.2.refs_0_), channel_id=1, source_target_pairs={{0,1},{1,2},{2,3},{3,0},{4,5},{5,6},{6,7},{7,4},{8,9},{9,10},{10,1... | collective-permute-start | bytes 245768 | tf_op jit(solution)/shard_map/ppermute | solution.py:229
  7.6 0.8 %pad_maximum_fusion.1.refs_4_ = bf16[192,256]{1,0:T(8,128)(2,1)S(1)} fusion(bf16[128,256]{1,0:T(8,128)(2,1)} %bitcast.15, bf16[64,256]{1,0:T(8,128)(2,1)} %bitcast.16), kind=kLoop, calls=%fused_computation.2 | loop fusion | flops 196608 | bytes 196608 | tf_op jit(solution)/shard_map/concatenate | solution.py:263
  8.4 1.6 %collective-permute-start.3 = (bf16[192,256]{1,0:T(8,128)(2,1)S(1)}, bf16[192,256]{1,0:T(8,128)(2,1)S(1)}, u32[]{:S(2)}, u32[]{:S(2)}) collective-permute-start(bf16[192,256]{1,0:T(8,128)(2,1)S(1)} %pad_maximum_fusion.1.refs_4_), channel_id=1, source_target_pairs={{0,16},{16,0},{1,17},{17,1},{2,18},{18,2},{3,19},{19,3},{4,20},{20... | collective-permute-start | bytes 294920 | tf_op jit(solution)/shard_map/ppermute | solution.py:229
  10.6 0.8 %copy.12 = s32[1,1,1,3,3]{3,4,0,1,2:T(4,128)S(1)} copy(s32[1,1,1,3,3]{4,2,3,1,0:T(1,128)} %param.9) | data formatting | bytes 72 | tf_op jit(solution)/shard_map/transpose | solution.py:262
  11.5 0.9 %convert_bitcast_fusion.weights = bf16[3,128,128]{2,1,0:T(8,128)(2,1)S(1)} fusion(s32[1,1,1,3,128,128]{5,4,3,2,1,0:T(8,128)} %param.8), kind=kLoop, calls=%fused_computation.3 | loop fusion | flops 49152 | bytes 294912 | tf_op jit(solution)/shard_map/convert_element_type | solution.py:261
  12.5 1.5 %collective-permute-done.1.refs_2_ = bf16[160,256]{1,0:T(8,128)(2,1)S(1)} collective-permute-done((bf16[160,256]{1,0:T(8,128)(2,1)S(1)}, bf16[160,256]{1,0:T(8,128)(2,1)S(1)}, u32[]{:S(2)}, u32[]{:S(2)}) %collective-permute-start.1) | collective-permute-done | bytes 81952 | tf_op jit(solution)/shard_map/ppermute | solution.py:229
  14.9 1.6 %collective-permute-start.4 = (bf16[384,256]{1,0:T(8,128)(2,1)S(1)}, bf16[384,256]{1,0:T(8,128)(2,1)S(1)}, u32[]{:S(2)}, u32[]{:S(2)}) collective-permute-start(bf16[384,256]{1,0:T(8,128)(2,1)S(1)} %pad_maximum_fusion), channel_id=1, source_target_pairs={{0,16},{16,0},{1,17},{17,1},{2,18},{18,2},{3,19},{19,3},{4,20},{20... | collective-permute-start | bytes 589832 | tf_op jit(solution)/shard_map/ppermute | solution.py:229
  16.5 1.5 %collective-permute-start.6 = (bf16[256,256]{1,0:T(8,128)(2,1)S(1)}, bf16[256,256]{1,0:T(8,128)(2,1)S(1)}, u32[]{:S(2)}, u32[]{:S(2)}) collective-permute-start(bf16[256,256]{1,0:T(8,128)(2,1)S(1)} %slice_dynamic-update-slice_fusion.refs_7_), channel_id=1, source_target_pairs={{0,8},{4,12},{8,0},{12,4},{1,9},{5,13},{9,1},{13,5},{2,10},{6,14},... | collective-permute-start | bytes 393224 | tf_op jit(solution)/shard_map/ppermute | solution.py:229
  18.0 2.5 %maximum_bitcast_fusion.early = bf16[128,128,128]{2,1,0:T(8,128)(2,1)S(1)} fusion(bf16[1,1,1,3,128,128,128]{6,5,4,3,2,1,0:T(8,128)(2,1)} %entries.1), kind=kLoop, calls=%fused_computation | loop fusion | flops 2097152 | bytes 8388608 | tf_op jit(solution)/shard_map/max | solution.py:266
  20.6 0.9 %collective-permute-done.6.refs_9_ = bf16[256,256]{1,0:T(8,128)(2,1)S(1)} collective-permute-done((bf16[256,256]{1,0:T(8,128)(2,1)S(1)}, bf16[256,256]{1,0:T(8,128)(2,1)S(1)}, u32[]{:S(2)}, u32[]{:S(2)}) %collective-permute-start.6) | collective-permute-done | bytes 131104 | tf_op jit(solution)/shard_map/ppermute | solution.py:229
  21.9 0.9 %collective-permute-done.7.refs_10_ = bf16[256,256]{1,0:T(8,128)(2,1)S(1)} collective-permute-done((bf16[256,256]{1,0:T(8,128)(2,1)S(1)}, bf16[256,256]{1,0:T(8,128)(2,1)S(1)}, u32[]{:S(2)}, u32[]{:S(2)}) %collective-permute-start.7) | collective-permute-done | bytes 131104 | tf_op jit(solution)/shard_map/ppermute | solution.py:242
  22.8 1.3 %blocks.1 = (f32[512,256]{1,0:T(8,128)S(1)}, f32[256,256]{1,0:T(8,128)S(1)}, s16[528,256]{1,0:T(8,128)(2,1)S(1)}, s16[272,256]{1,0:T(8,128)(2,1)S(1)}, s16[272,2...) custom-call(s32[10]{0:T(128)S(1)} %pad_add_fusion.table, bf16[1,1,1,3,128,128,128]{6,5,4,3,2,1,0:T(8,128)(2,1)} %entries.1, ...), custom_call_target="tpu_custom_call" | custom-call | tf_op jit(solution)/shard_map/blocks/pallas_call | solution.py:274
  24.7 17.3 %collective-permute-start.9 = (s16[272,256]{1,0:T(8,128)(2,1)S(1)}, s16[272,256]{1,0:T(8,128)(2,1)S(1)}, u32[]{:S(2)}, u32[]{:S(2)}) collective-permute-start(s16[272,256]{1,0:T(8,128)(2,1)S(1)} %get-tuple-element.34), channel_id=1, source_target_pairs={{0,4},{4,8},{8,12},{12,0},{1,5},{5,9},{9,13},{13,1},{2,6},{6,10},{... | collective-permute-start | bytes 417800 | tf_op jit(solution)/shard_map/ppermute | solution.py:229
  42.0 1.3 %collective-permute-start.10 = (s16[272,256]{1,0:T(8,128)(2,1)S(1)}, s16[272,256]{1,0:T(8,128)(2,1)S(1)}, u32[]{:S(2)}, u32[]{:S(2)}) collective-permute-start(s16[272,256]{1,0:T(8,128)(2,1)S(1)} %get-tuple-element.35), channel_id=1, source_target_pairs={{0,8},{4,12},{8,0},{12,4},{1,9},{5,13},{9,1},{13,5},{2,10},{6,14},... | collective-permute-start | bytes 417800 | tf_op jit(solution)/shard_map/ppermute | solution.py:229
  43.2 1.4 %collective-permute-start.11 = (s16[272,256]{1,0:T(8,128)(2,1)S(1)}, s16[272,256]{1,0:T(8,128)(2,1)S(1)}, u32[]{:S(2)}, u32[]{:S(2)}) collective-permute-start(s16[272,256]{1,0:T(8,128)(2,1)S(1)} %get-tuple-element.36), channel_id=1, source_target_pairs={{0,12},{4,0},{8,4},{12,8},{1,13},{5,1},{9,5},{13,9},{2,14},{6,2},{... | collective-permute-start | bytes 417800 | tf_op jit(solution)/shard_map/ppermute | solution.py:229
  44.6 3.5 %collective-permute-done.10.refs_4_ = s16[272,256]{1,0:T(8,128)(2,1)S(1)} collective-permute-done((s16[272,256]{1,0:T(8,128)(2,1)S(1)}, s16[272,256]{1,0:T(8,128)(2,1)S(1)}, u32[]{:S(2)}, u32[]{:S(2)}) %collective-permute-start.10) | collective-permute-done | bytes 139296 | tf_op jit(solution)/shard_map/ppermute | solution.py:229
  48.2 1.5 %collective-permute-done.11.refs_5_ = s16[272,256]{1,0:T(8,128)(2,1)S(1)} collective-permute-done((s16[272,256]{1,0:T(8,128)(2,1)S(1)}, s16[272,256]{1,0:T(8,128)(2,1)S(1)}, u32[]{:S(2)}, u32[]{:S(2)}) %collective-permute-start.11) | collective-permute-done | bytes 139296 | tf_op jit(solution)/shard_map/ppermute | solution.py:229
  50.3 1.5 %collective-permute-start.13 = (s16[176,256]{1,0:T(8,128)(2,1)S(1)}, s16[176,256]{1,0:T(8,128)(2,1)S(1)}, u32[]{:S(2)}, u32[]{:S(2)}) collective-permute-start(s16[176,256]{1,0:T(8,128)(2,1)S(1)} %get-tuple-element.40), channel_id=1, source_target_pairs={{0,2},{1,3},{2,0},{3,1},{4,6},{5,7},{6,4},{7,5},{8,10},{9,11},{10,... | collective-permute-start | bytes 270344 | tf_op jit(solution)/shard_map/ppermute | solution.py:229
  51.8 2.1 %collective-permute-start.14 = (s16[176,256]{1,0:T(8,128)(2,1)S(1)}, s16[176,256]{1,0:T(8,128)(2,1)S(1)}, u32[]{:S(2)}, u32[]{:S(2)}) collective-permute-start(s16[176,256]{1,0:T(8,128)(2,1)S(1)} %get-tuple-element.41), channel_id=1, source_target_pairs={{0,3},{1,0},{2,1},{3,2},{4,7},{5,4},{6,5},{7,6},{8,11},{9,8},{10,9... | collective-permute-start | bytes 270344 | tf_op jit(solution)/shard_map/ppermute | solution.py:229
  53.9 2.0 %collective-permute-start.15 = (s16[80,256]{1,0:T(8,128)(2,1)S(1)}, s16[80,256]{1,0:T(8,128)(2,1)S(1)}, u32[]{:S(2)}, u32[]{:S(2)}) collective-permute-start(s16[80,256]{1,0:T(8,128)(2,1)S(1)} %get-tuple-element.42), channel_id=1, source_target_pairs={{0,16},{16,0},{1,17},{17,1},{2,18},{18,2},{3,19},{19,3},{4,20},{20... | collective-permute-start | bytes 122888 | tf_op jit(solution)/shard_map/ppermute | solution.py:229
  55.8 2.0 %collective-permute-done.15.refs_5_ = s16[80,256]{1,0:T(8,128)(2,1)S(1)} collective-permute-done((s16[80,256]{1,0:T(8,128)(2,1)S(1)}, s16[80,256]{1,0:T(8,128)(2,1)S(1)}, u32[]{:S(2)}, u32[]{:S(2)}) %collective-permute-start.15) | collective-permute-done | bytes 40992 | tf_op jit(solution)/shard_map/ppermute | solution.py:229
  57.9 2.5 %collective-permute-done.13.refs_3_ = s16[176,256]{1,0:T(8,128)(2,1)S(1)} collective-permute-done((s16[176,256]{1,0:T(8,128)(2,1)S(1)}, s16[176,256]{1,0:T(8,128)(2,1)S(1)}, u32[]{:S(2)}, u32[]{:S(2)}) %collective-permute-start.13) | collective-permute-done | bytes 90144 | tf_op jit(solution)/shard_map/ppermute | solution.py:229
  (28 shorter events, 3.4 us)
Async XLA Ops:
  1.5 11.0 %collective-permute-start.2 = (bf16[160,256]{1,0:T(8,128)(2,1)S(1)}, bf16[160,256]{1,0:T(8,128)(2,1)S(1)}, u32[]{:S(2)}, u32[]{:S(2)}) collective-permute-start(bf16[160,256]{1,0:T(8,128)(2,1)S(1)} %pad_maximum_fusion.2.refs_0_), channel_id=1, source_target_pairs={{0,3},{1,0},{2,1},{3,2},{4,7},{5,4},{6,5},{7,6},{8,11},{9,8},{10,9... | collective-permute-start | bytes 245768 | tf_op jit(solution)/shard_map/ppermute | solution.py:229
  6.5 7.5 %collective-permute-start.1 = (bf16[160,256]{1,0:T(8,128)(2,1)S(1)}, bf16[160,256]{1,0:T(8,128)(2,1)S(1)}, u32[]{:S(2)}, u32[]{:S(2)}) collective-permute-start(bf16[160,256]{1,0:T(8,128)(2,1)S(1)} %pad_maximum_fusion.2.refs_0_), channel_id=1, source_target_pairs={{0,2},{1,3},{2,0},{3,1},{4,6},{5,7},{6,4},{7,5},{8,10},{9,11},{10,... | collective-permute-start | bytes 245768 | tf_op jit(solution)/shard_map/ppermute | solution.py:229
  6.5 7.5 %collective-permute-start = (bf16[160,256]{1,0:T(8,128)(2,1)S(1)}, bf16[160,256]{1,0:T(8,128)(2,1)S(1)}, u32[]{:S(2)}, u32[]{:S(2)}) collective-permute-start(bf16[160,256]{1,0:T(8,128)(2,1)S(1)} %pad_maximum_fusion.2.refs_0_), channel_id=1, source_target_pairs={{0,1},{1,2},{2,3},{3,0},{4,5},{5,6},{6,7},{7,4},{8,9},{9,10},{10,1... | collective-permute-start | bytes 245768 | tf_op jit(solution)/shard_map/ppermute | solution.py:229
  8.4 8.1 %collective-permute-start.3 = (bf16[192,256]{1,0:T(8,128)(2,1)S(1)}, bf16[192,256]{1,0:T(8,128)(2,1)S(1)}, u32[]{:S(2)}, u32[]{:S(2)}) collective-permute-start(bf16[192,256]{1,0:T(8,128)(2,1)S(1)} %pad_maximum_fusion.1.refs_4_), channel_id=1, source_target_pairs={{0,16},{16,0},{1,17},{17,1},{2,18},{18,2},{3,19},{19,3},{4,20},{20... | collective-permute-start | bytes 294920 | tf_op jit(solution)/shard_map/ppermute | solution.py:229
  14.9 7.0 %collective-permute-start.4 = (bf16[384,256]{1,0:T(8,128)(2,1)S(1)}, bf16[384,256]{1,0:T(8,128)(2,1)S(1)}, u32[]{:S(2)}, u32[]{:S(2)}) collective-permute-start(bf16[384,256]{1,0:T(8,128)(2,1)S(1)} %pad_maximum_fusion), channel_id=1, source_target_pairs={{0,16},{16,0},{1,17},{17,1},{2,18},{18,2},{3,19},{19,3},{4,20},{20... | collective-permute-start | bytes 589832 | tf_op jit(solution)/shard_map/ppermute | solution.py:229
  16.5 5.0 %collective-permute-start.6 = (bf16[256,256]{1,0:T(8,128)(2,1)S(1)}, bf16[256,256]{1,0:T(8,128)(2,1)S(1)}, u32[]{:S(2)}, u32[]{:S(2)}) collective-permute-start(bf16[256,256]{1,0:T(8,128)(2,1)S(1)} %slice_dynamic-update-slice_fusion.refs_7_), channel_id=1, source_target_pairs={{0,8},{4,12},{8,0},{12,4},{1,9},{5,13},{9,1},{13,5},{2,10},{6,14},... | collective-permute-start | bytes 393224 | tf_op jit(solution)/shard_map/ppermute | solution.py:229
  20.5 1.4 %collective-permute-start.5 = (bf16[256,256]{1,0:T(8,128)(2,1)S(1)}, bf16[256,256]{1,0:T(8,128)(2,1)S(1)}, u32[]{:S(2)}, u32[]{:S(2)}) collective-permute-start(bf16[256,256]{1,0:T(8,128)(2,1)S(1)} %slice_dynamic-update-slice_fusion.refs_7_), channel_id=1, source_target_pairs={{0,4},{4,0},{8,12},{12,8},{1,5},{5,1},{9,13},{13,9},{2,6},{6,2},{1... | collective-permute-start | bytes 393224 | tf_op jit(solution)/shard_map/ppermute | solution.py:242
  21.5 1.3 %collective-permute-start.7 = (bf16[256,256]{1,0:T(8,128)(2,1)S(1)}, bf16[256,256]{1,0:T(8,128)(2,1)S(1)}, u32[]{:S(2)}, u32[]{:S(2)}) collective-permute-start(bf16[256,256]{1,0:T(8,128)(2,1)S(1)} %collective-permute-done.6.refs_9_), channel_id=1, source_target_pairs={{0,4},{4,0},{8,12},{12,8},{1,5},{5,1},{9,13},{13,9},{2,6},{6,2},{1... | collective-permute-start | bytes 393224 | tf_op jit(solution)/shard_map/ppermute | solution.py:242
  24.1 25.5 %collective-permute-start.8 = (s16[528,256]{1,0:T(8,128)(2,1)S(1)}, s16[528,256]{1,0:T(8,128)(2,1)S(1)}, u32[]{:S(2)}, u32[]{:S(2)}) collective-permute-start(s16[528,256]{1,0:T(8,128)(2,1)S(1)} %get-tuple-element.33), channel_id=1, source_target_pairs={{0,16},{16,0},{1,17},{17,1},{2,18},{18,2},{3,19},{19,3},{4,20},{20... | collective-permute-start | bytes 811016 | tf_op jit(solution)/shard_map/ppermute | solution.py:229
  24.7 19.9 %collective-permute-start.9 = (s16[272,256]{1,0:T(8,128)(2,1)S(1)}, s16[272,256]{1,0:T(8,128)(2,1)S(1)}, u32[]{:S(2)}, u32[]{:S(2)}) collective-permute-start(s16[272,256]{1,0:T(8,128)(2,1)S(1)} %get-tuple-element.34), channel_id=1, source_target_pairs={{0,4},{4,8},{8,12},{12,0},{1,5},{5,9},{9,13},{13,1},{2,6},{6,10},{... | collective-permute-start | bytes 417800 | tf_op jit(solution)/shard_map/ppermute | solution.py:229
  42.0 6.2 %collective-permute-start.10 = (s16[272,256]{1,0:T(8,128)(2,1)S(1)}, s16[272,256]{1,0:T(8,128)(2,1)S(1)}, u32[]{:S(2)}, u32[]{:S(2)}) collective-permute-start(s16[272,256]{1,0:T(8,128)(2,1)S(1)} %get-tuple-element.35), channel_id=1, source_target_pairs={{0,8},{4,12},{8,0},{12,4},{1,9},{5,13},{9,1},{13,5},{2,10},{6,14},... | collective-permute-start | bytes 417800 | tf_op jit(solution)/shard_map/ppermute | solution.py:229
  43.2 6.4 %collective-permute-start.11 = (s16[272,256]{1,0:T(8,128)(2,1)S(1)}, s16[272,256]{1,0:T(8,128)(2,1)S(1)}, u32[]{:S(2)}, u32[]{:S(2)}) collective-permute-start(s16[272,256]{1,0:T(8,128)(2,1)S(1)} %get-tuple-element.36), channel_id=1, source_target_pairs={{0,12},{4,0},{8,4},{12,8},{1,13},{5,1},{9,5},{13,9},{2,14},{6,2},{... | collective-permute-start | bytes 417800 | tf_op jit(solution)/shard_map/ppermute | solution.py:229
  50.0 7.9 %collective-permute-start.12 = (s16[176,256]{1,0:T(8,128)(2,1)S(1)}, s16[176,256]{1,0:T(8,128)(2,1)S(1)}, u32[]{:S(2)}, u32[]{:S(2)}) collective-permute-start(s16[176,256]{1,0:T(8,128)(2,1)S(1)} %get-tuple-element.39), channel_id=1, source_target_pairs={{0,1},{1,2},{2,3},{3,0},{4,5},{5,6},{6,7},{7,4},{8,9},{9,10},{10,1... | collective-permute-start | bytes 270344 | tf_op jit(solution)/shard_map/ppermute | solution.py:229
  50.3 10.1 %collective-permute-start.13 = (s16[176,256]{1,0:T(8,128)(2,1)S(1)}, s16[176,256]{1,0:T(8,128)(2,1)S(1)}, u32[]{:S(2)}, u32[]{:S(2)}) collective-permute-start(s16[176,256]{1,0:T(8,128)(2,1)S(1)} %get-tuple-element.40), channel_id=1, source_target_pairs={{0,2},{1,3},{2,0},{3,1},{4,6},{5,7},{6,4},{7,5},{8,10},{9,11},{10,... | collective-permute-start | bytes 270344 | tf_op jit(solution)/shard_map/ppermute | solution.py:229
  51.8 8.6 %collective-permute-start.14 = (s16[176,256]{1,0:T(8,128)(2,1)S(1)}, s16[176,256]{1,0:T(8,128)(2,1)S(1)}, u32[]{:S(2)}, u32[]{:S(2)}) collective-permute-start(s16[176,256]{1,0:T(8,128)(2,1)S(1)} %get-tuple-element.41), channel_id=1, source_target_pairs={{0,3},{1,0},{2,1},{3,2},{4,7},{5,4},{6,5},{7,6},{8,11},{9,8},{10,9... | collective-permute-start | bytes 270344 | tf_op jit(solution)/shard_map/ppermute | solution.py:229
  53.9 4.0 %collective-permute-start.15 = (s16[80,256]{1,0:T(8,128)(2,1)S(1)}, s16[80,256]{1,0:T(8,128)(2,1)S(1)}, u32[]{:S(2)}, u32[]{:S(2)}) collective-permute-start(s16[80,256]{1,0:T(8,128)(2,1)S(1)} %get-tuple-element.42), channel_id=1, source_target_pairs={{0,16},{16,0},{1,17},{17,1},{2,18},{18,2},{3,19},{19,3},{4,20},{20... | collective-permute-start | bytes 122888 | tf_op jit(solution)/shard_map/ppermute | solution.py:229
